TPU v7x, 128 devices: a whole 4x4x4 slice. The times are simulated.
128 devices in a mesh: sym: 8 (over y_hi, x), tile: 8 (over z, y_lo), occ: 2 (over core).
Axes of the slice: x: 4, y: 4 (y_hi: 2, y_lo: 2; y = y_hi * 2 + y_lo), z: 4, core: 2. Of those that a mesh axis runs over, the one named last changes fastest.
Arguments:
- irrep_dims: int32 [8], replicated, may hold values from 1 to 384, 1600 in all
- chol_vectors: bfloat16 [16, 3072, 384], P(('sym', 'occ'), 'tile'), may hold values from -0.375 to 0.375
- amplitudes: bfloat16 [8, 16, 3072, 384], P('sym', 'occ', 'tile'), may hold values from -6 to 6
Outputs:
- sigma_ladder: float32 [8, 16, 3072, 384], P('sym', 'occ', 'tile')
Inputs may be any that keep to these rules, and one draw needn't show every extreme that they name: irrep_dims[h] is the number of virtual orbitals of irrep h; the entries sum to 1600 and the largest is exactly 384.
All inputs are finite; a program needn't handle non-finite values.
Results may differ from a plain program's by a relative error of at most 0.0029.
Values may be sent and summed in bfloat16 or wider, within the bound.
A program may use at most 128 MiB of HBM per device.

v0:
```python
import jax
import jax.numpy as jnp
from jax import lax
from jax.experimental import pallas as pl
from jax.experimental.pallas import tpu as pltpu
from jax.sharding import PartitionSpec as P

V = 384
NI = 8
PIECES = 2
PV = V // PIECES
HALF = NI * V // 2
CROSSF, OWN, PASS_Z, FWD_Y, PASS_Y, PAR = range(6)
PARTS = 2
SEQUENCE = (1, 1, 1, 1, 1, 1, 2, 2, 2, 2, 2, 2)
UNITS = (
    ((0, 0), (0, 0), (0, 0), (0, 0), (0, 0), (0, 0), (0, 0), (0, 0), (0, 0), (0, 0), (0, 0), (0, 0), (0, 0), (0, 0), (0, 0), (0, 0)),
    ((0, 1), (0, 1), (0, 1), (0, 1), (0, 1), (0, 1), (0, 1), (0, 1), (0, 1), (0, 1), (0, 1), (0, 1), (0, 1), (0, 1), (0, 1), (0, 1)),
    ((0, 3), (0, 3), (0, 3), (0, 3), (0, 3), (0, 3), (0, 3), (0, 3), (0, 3), (0, 3), (0, 3), (0, 3), (0, 3), (0, 3), (0, 3), (0, 3)),
    ((1, 0), (1, 0), (1, 0), (1, 0), (0, 2), (0, 2), (1, 0), (1, 0), (1, 0), (1, 0), (1, 0), (1, 0), (1, 0), (1, 0), (1, 0), (1, 0)),
    ((0, 2), (0, 2), (0, 2), (0, 2), (1, 1), (1, 0), (0, 2), (0, 2), (0, 2), (0, 2), (0, 2), (0, 2), (0, 2), (0, 2), (0, 2), (0, 2)),
    ((1, 1), (1, 1), (1, 1), (1, 1), (1, 3), (1, 1), (1, 1), (1, 1), (1, 3), (1, 3), (1, 1), (1, 1), (1, 1), (1, 1), (1, 1), (1, 1)),
    ((0, 0), (0, 0), (0, 0), (0, 0), (0, 0), (0, 0), (0, 0), (0, 0), (0, 0), (0, 0), (0, 0), (0, 0), (0, 0), (0, 0), (0, 0), (0, 0)),
    ((1, 0), (1, 0), (1, 0), (1, 0), (0, 1), (1, 0), (1, 0), (1, 0), (1, 0), (1, 0), (1, 0), (1, 0), (1, 0), (1, 0), (1, 0), (1, 0)),
    ((0, 1), (0, 1), (0, 1), (0, 1), (1, 1), (0, 1), (1, 1), (1, 1), (0, 1), (0, 1), (0, 1), (0, 1), (0, 1), (0, 1), (0, 1), (0, 1)),
    ((1, 1), (1, 1), (0, 3), (0, 3), (0, 3), (1, 1), (0, 1), (0, 1), (0, 3), (0, 3), (1, 1), (1, 1), (1, 1), (1, 1), (1, 1), (1, 1)),
    ((0, 3), (0, 3), (0, 2), (0, 2), (1, 3), (0, 3), (0, 3), (0, 3), (1, 3), (1, 3), (0, 3), (0, 3), (0, 3), (0, 3), (0, 3), (0, 3)),
    ((0, 2), (0, 2), (1, 1), (1, 1), (0, 2), (0, 2), (0, 2), (0, 2), (0, 2), (0, 2), (0, 2), (0, 2), (0, 2), (0, 2), (0, 2), (0, 2)),
)
EVENTS = (
    (
        (2, ((CROSSF, 0), (CROSSF, 1), (OWN, 0, 1, 0), (OWN, 0, 3, 0), (PASS_Z, 0, 0), (PASS_Z, 0, 1), (OWN, 0, 1, 1), (OWN, 0, 3, 1),)),
        (3, ((OWN, 1, 0, 0), (OWN, 1, 0, 1), (PASS_Z, 1, 0), (PASS_Z, 3, 0),)),
        (4, ((OWN, 0, 2, 0), (OWN, 0, 2, 1),)),
        (5, ((FWD_Y, 0, 0), (FWD_Y, 0, 1),)),
        (6, ((OWN, 1, 1, 0),)),
        (7, ((PASS_Z, 1, 1), (PASS_Z, 3, 1),)),
        (8, ((OWN, 1, 1, 1), (PASS_Y, 0, 1),)),
        (9, ((OWN, 1, 3, 0), (FWD_Y, 1, 0), (FWD_Y, 3, 0),)),
        (11, ((OWN, 1, 2, 0), (OWN, 1, 2, 1), (PASS_Z, 2, 0), (PASS_Z, 2, 1),)),
        (12, ((PASS_Y, 1, 0),)),
        (13, ((FWD_Y, 1, 1), (FWD_Y, 3, 1),)),
        (15, ((FWD_Y, 2, 0), (FWD_Y, 2, 1),)),
        (16, ((PASS_Y, 3, 1),)),
        (18, ((OWN, 1, 3, 1),)),
        (19, ((PASS_Y, 2, 0),)),
    ),
    (
        (2, ((CROSSF, 0), (CROSSF, 1), (OWN, 0, 1, 0), (OWN, 0, 3, 0), (PASS_Z, 0, 0), (PASS_Z, 0, 1), (OWN, 0, 1, 1), (OWN, 0, 3, 1),)),
        (3, ((OWN, 1, 0, 0), (OWN, 1, 0, 1), (PASS_Z, 1, 0), (PASS_Z, 3, 0),)),
        (4, ((OWN, 0, 2, 0), (OWN, 0, 2, 1),)),
        (5, ((FWD_Y, 0, 0), (FWD_Y, 0, 1),)),
        (6, ((OWN, 1, 1, 0),)),
        (7, ((PASS_Z, 1, 1), (PASS_Z, 3, 1),)),
        (8, ((OWN, 1, 1, 1), (PASS_Y, 0, 0),)),
        (9, ((OWN, 1, 3, 0), (FWD_Y, 1, 0), (FWD_Y, 3, 0),)),
        (11, ((OWN, 1, 3, 1), (OWN, 1, 2, 1), (PASS_Z, 2, 0), (PASS_Z, 2, 1),)),
        (12, ((PASS_Y, 3, 0),)),
        (13, ((OWN, 1, 2, 0), (FWD_Y, 1, 1), (FWD_Y, 3, 1),)),
        (15, ((FWD_Y, 2, 0), (FWD_Y, 2, 1),)),
        (16, ((PASS_Y, 1, 1),)),
        (18, ((PASS_Y, 2, 1),)),
    ),
    (
        (2, ((CROSSF, 0), (CROSSF, 1), (OWN, 0, 1, 0), (OWN, 0, 3, 0), (PASS_Z, 0, 0), (PASS_Z, 0, 1), (OWN, 0, 1, 1), (OWN, 0, 3, 1),)),
        (3, ((OWN, 1, 0, 0), (OWN, 1, 0, 1), (PASS_Z, 1, 0), (PASS_Z, 3, 0),)),
        (4, ((OWN, 0, 2, 0), (OWN, 0, 2, 1),)),
        (5, ((PAR, 0, 0, 0), (PAR, 0, 0, 1),)),
        (6, ((OWN, 1, 1, 0),)),
        (7, ((OWN, 1, 3, 0), (PASS_Z, 1, 1), (PASS_Z, 3, 1),)),
        (8, ((OWN, 1, 1, 1), (PASS_Y, 0, 0),)),
        (9, ((OWN, 1, 3, 1), (PAR, 0, 1, 0), (PAR, 0, 3, 0),)),
        (11, ((OWN, 1, 2, 0), (OWN, 1, 2, 1), (PASS_Z, 2, 0), (PASS_Z, 2, 1), (PAR, 1, 0, 0), (PAR, 1, 0, 1),)),
        (13, ((PASS_Y, 3, 0), (PAR, 0, 1, 1), (PAR, 0, 3, 1),)),
        (15, ((PAR, 0, 2, 0), (PAR, 0, 2, 1), (PAR, 1, 3, 0),)),
        (16, ((PAR, 1, 1, 0),)),
        (18, ((PASS_Y, 1, 1),)),
        (20, ((PASS_Y, 2, 1),)),
        (21, ((PAR, 1, 3, 1),)),
        (22, ((PAR, 1, 1, 1),)),
        (23, ((PAR, 1, 2, 0), (PAR, 1, 2, 1),)),
    ),
    (
        (2, ((CROSSF, 0), (CROSSF, 1), (OWN, 0, 1, 0), (OWN, 0, 3, 0), (PASS_Z, 0, 0), (PASS_Z, 0, 1), (OWN, 0, 1, 1), (OWN, 0, 3, 1),)),
        (3, ((OWN, 1, 0, 0), (OWN, 1, 0, 1), (PASS_Z, 1, 0), (PASS_Z, 3, 0),)),
        (4, ((OWN, 0, 2, 0), (OWN, 0, 2, 1),)),
        (5, ((PAR, 0, 0, 0), (PAR, 0, 0, 1),)),
        (6, ((OWN, 1, 1, 0),)),
        (7, ((OWN, 1, 3, 0), (PASS_Z, 1, 1), (PASS_Z, 3, 1),)),
        (8, ((OWN, 1, 1, 1), (PASS_Y, 0, 1),)),
        (9, ((OWN, 1, 3, 1), (PAR, 0, 1, 0), (PAR, 0, 3, 0),)),
        (11, ((OWN, 1, 2, 0), (OWN, 1, 2, 1), (PASS_Z, 2, 0), (PASS_Z, 2, 1), (PAR, 1, 0, 0), (PAR, 1, 0, 1),)),
        (13, ((PASS_Y, 1, 0), (PAR, 0, 1, 1), (PAR, 0, 3, 1),)),
        (15, ((PAR, 0, 2, 0), (PAR, 0, 2, 1), (PAR, 1, 1, 0),)),
        (16, ((PAR, 1, 3, 0),)),
        (18, ((PASS_Y, 3, 1),)),
        (20, ((PASS_Y, 2, 0),)),
        (21, ((PAR, 1, 1, 1),)),
        (22, ((PAR, 1, 3, 1),)),
        (23, ((PAR, 1, 2, 1),)),
        (24, ((PAR, 1, 2, 0),)),
    ),
    (
        (2, ((CROSSF, 0), (OWN, 0, 1, 0), (OWN, 0, 3, 0), (PASS_Z, 0, 0), (PASS_Z, 0, 1), (PAR, 0, 0, 0), (OWN, 0, 1, 1), (PAR, 1, 0, 0), (OWN, 0, 3, 1), (CROSSF, 1),)),
        (3, ((PASS_Z, 1, 0), (PASS_Z, 3, 0),)),
        (4, ((OWN, 0, 2, 0), (PAR, 0, 0, 1), (PAR, 1, 0, 1),)),
        (5, ((OWN, 0, 2, 1), (FWD_Y, 0, 0), (FWD_Y, 0, 1),)),
        (6, ((OWN, 1, 0, 0), (OWN, 1, 1, 0), (PAR, 0, 1, 0),)),
        (7, ((OWN, 1, 3, 0), (PASS_Z, 1, 1), (PASS_Z, 3, 1),)),
        (8, ((OWN, 1, 1, 1), (PAR, 0, 3, 0), (PAR, 1, 1, 0), (OWN, 1, 3, 1), (FWD_Y, 1, 0), (FWD_Y, 3, 0),)),
        (9, ((PAR, 0, 1, 1), (PAR, 1, 3, 0),)),
        (10, ((OWN, 1, 2, 0), (OWN, 1, 2, 1), (PASS_Z, 2, 0), (PASS_Z, 2, 1),)),
        (11, ((PAR, 1, 1, 1),)),
        (12, ((FWD_Y, 1, 1), (FWD_Y, 3, 1), (PAR, 0, 3, 1),)),
        (14, ((OWN, 1, 0, 1), (FWD_Y, 2, 0), (PAR, 1, 3, 1),)),
        (15, ((FWD_Y, 2, 1),)),
        (16, ((PAR, 0, 2, 0), (PAR, 1, 2, 0),)),
        (18, ((PAR, 0, 2, 1), (PAR, 1, 2, 1),)),
    ),
    (
        (2, ((CROSSF, 0), (OWN, 0, 1, 0), (OWN, 0, 3, 0), (PASS_Z, 0, 0), (PASS_Z, 0, 1), (PAR, 1, 0, 0), (OWN, 0, 1, 1), (PAR, 0, 0, 0), (OWN, 0, 3, 1), (CROSSF, 1),)),
        (3, ((PASS_Z, 1, 0), (PASS_Z, 3, 0),)),
        (4, ((OWN, 0, 2, 0), (PAR, 0, 0, 1), (PAR, 1, 0, 1),)),
        (5, ((OWN, 0, 2, 1), (FWD_Y, 0, 0), (FWD_Y, 0, 1),)),
        (6, ((OWN, 1, 0, 0), (OWN, 1, 0, 1), (OWN, 1, 1, 0),)),
        (7, ((OWN, 1, 3, 0), (PASS_Z, 1, 1), (PASS_Z, 3, 1),)),
        (8, ((OWN, 1, 1, 1), (PAR, 0, 1, 0), (PAR, 1, 1, 0),)),
        (9, ((OWN, 1, 3, 1), (FWD_Y, 1, 0), (FWD_Y, 3, 0),)),
        (10, ((PAR, 0, 3, 0), (PAR, 1, 3, 0),)),
        (11, ((OWN, 1, 2, 0), (OWN, 1, 2, 1), (PASS_Z, 2, 0), (PASS_Z, 2, 1),)),
        (12, ((PAR, 0, 1, 1), (PAR, 1, 1, 1),)),
        (13, ((FWD_Y, 1, 1), (FWD_Y, 3, 1),)),
        (14, ((PAR, 0, 3, 1), (PAR, 1, 3, 1),)),
        (15, ((FWD_Y, 2, 0), (FWD_Y, 2, 1),)),
        (16, ((PAR, 0, 2, 0), (PAR, 1, 2, 0),)),
        (19, ((PAR, 0, 2, 1), (PAR, 1, 2, 1),)),
    ),
    (
        (2, ((CROSSF, 0), (CROSSF, 1), (OWN, 0, 1, 0), (OWN, 0, 3, 0), (PASS_Z, 0, 0), (PASS_Z, 0, 1), (OWN, 0, 1, 1), (OWN, 0, 3, 1),)),
        (3, ((OWN, 1, 0, 0), (OWN, 1, 0, 1), (PASS_Z, 1, 0), (PASS_Z, 3, 0),)),
        (4, ((OWN, 0, 2, 0), (OWN, 0, 2, 1),)),
        (5, ((FWD_Y, 0, 0), (FWD_Y, 0, 1),)),
        (6, ((OWN, 1, 1, 0), (OWN, 1, 3, 0),)),
        (7, ((PASS_Z, 1, 1), (PASS_Z, 3, 1),)),
        (8, ((OWN, 1, 1, 1), (PAR, 0, 0, 0), (PAR, 1, 0, 0),)),
        (9, ((OWN, 1, 3, 1), (FWD_Y, 1, 0), (FWD_Y, 3, 0),)),
        (10, ((PAR, 0, 0, 1), (PAR, 1, 0, 1),)),
        (11, ((OWN, 1, 2, 0), (OWN, 1, 2, 1), (PASS_Z, 2, 0), (PASS_Z, 2, 1),)),
        (12, ((PAR, 0, 1, 0), (PAR, 1, 1, 0),)),
        (13, ((FWD_Y, 1, 1), (FWD_Y, 3, 1),)),
        (14, ((PAR, 1, 3, 0),)),
        (15, ((FWD_Y, 2, 0), (FWD_Y, 2, 1), (PAR, 0, 3, 0),)),
        (16, ((PAR, 1, 1, 1), (PAR, 0, 1, 1),)),
        (18, ((PAR, 0, 3, 1), (PAR, 1, 3, 1),)),
        (20, ((PAR, 0, 2, 0), (PAR, 1, 2, 0),)),
        (22, ((PAR, 0, 2, 1), (PAR, 1, 2, 1),)),
    ),
    (
        (2, ((CROSSF, 0), (CROSSF, 1), (OWN, 0, 1, 0), (OWN, 0, 3, 0), (PASS_Z, 0, 0), (PASS_Z, 0, 1), (OWN, 0, 1, 1), (OWN, 0, 3, 1),)),
        (3, ((OWN, 1, 0, 0), (PASS_Z, 1, 0), (PASS_Z, 3, 0),)),
        (4, ((OWN, 0, 2, 0), (OWN, 0, 2, 1),)),
        (5, ((OWN, 1, 0, 1), (FWD_Y, 0, 0), (FWD_Y, 0, 1),)),
        (6, ((OWN, 1, 1, 0), (OWN, 1, 3, 0),)),
        (7, ((PASS_Z, 1, 1), (PASS_Z, 3, 1),)),
        (8, ((OWN, 1, 1, 1), (PAR, 0, 0, 0), (PAR, 1, 0, 0),)),
        (9, ((OWN, 1, 3, 1), (FWD_Y, 1, 0), (FWD_Y, 3, 0),)),
        (10, ((PAR, 0, 0, 1), (PAR, 1, 0, 1),)),
        (11, ((OWN, 1, 2, 0), (OWN, 1, 2, 1), (PASS_Z, 2, 0), (PASS_Z, 2, 1),)),
        (12, ((PAR, 0, 1, 0), (PAR, 1, 1, 0),)),
        (13, ((FWD_Y, 1, 1), (FWD_Y, 3, 1),)),
        (14, ((PAR, 1, 3, 0),)),
        (15, ((FWD_Y, 2, 0), (FWD_Y, 2, 1), (PAR, 0, 3, 0),)),
        (16, ((PAR, 1, 1, 1), (PAR, 0, 1, 1),)),
        (18, ((PAR, 0, 3, 1), (PAR, 1, 3, 1),)),
        (20, ((PAR, 0, 2, 0), (PAR, 1, 2, 0),)),
        (22, ((PAR, 0, 2, 1), (PAR, 1, 2, 1),)),
    ),
    (
        (2, ((CROSSF, 0), (CROSSF, 1), (OWN, 0, 1, 0), (OWN, 0, 3, 0), (FWD_Y, 0, 0), (PAR, 0, 0, 0), (OWN, 0, 1, 1), (PAR, 0, 0, 1), (OWN, 0, 3, 1), (FWD_Y, 0, 1),)),
        (3, ((OWN, 1, 0, 0), (OWN, 1, 0, 1),)),
        (4, ((OWN, 0, 2, 0), (OWN, 0, 2, 1), (FWD_Y, 1, 0), (PAR, 0, 1, 0),)),
        (5, ((PASS_Y, 0, 0), (PASS_Y, 0, 1),)),
        (6, ((OWN, 1, 3, 0), (FWD_Y, 3, 0), (PAR, 0, 3, 0),)),
        (7, ((PASS_Y, 1, 0),)),
        (8, ((FWD_Y, 1, 1), (PAR, 0, 1, 1), (PAR, 1, 0, 0),)),
        (9, ((OWN, 1, 1, 0), (OWN, 1, 3, 1), (PAR, 1, 0, 1),)),
        (10, ((FWD_Y, 3, 1), (PASS_Y, 3, 0), (PAR, 0, 3, 1),)),
        (11, ((OWN, 1, 2, 0), (OWN, 1, 2, 1), (PAR, 1, 1, 0),)),
        (12, ((FWD_Y, 2, 0), (PASS_Y, 1, 1), (PAR, 0, 2, 0),)),
        (14, ((FWD_Y, 2, 1), (PASS_Y, 3, 1), (PAR, 0, 2, 1),)),
        (15, ((PAR, 1, 3, 0),)),
        (16, ((PASS_Y, 2, 0),)),
        (17, ((PAR, 1, 1, 1),)),
        (18, ((OWN, 1, 1, 1), (PAR, 1, 3, 1),)),
        (19, ((PASS_Y, 2, 1),)),
        (20, ((PAR, 1, 2, 0),)),
        (22, ((PAR, 1, 2, 1),)),
    ),
    (
        (2, ((CROSSF, 0), (CROSSF, 1), (OWN, 0, 1, 0), (OWN, 0, 3, 0), (FWD_Y, 0, 0), (PAR, 0, 0, 0), (OWN, 0, 1, 1), (PAR, 0, 0, 1), (OWN, 0, 3, 1), (FWD_Y, 0, 1),)),
        (3, ((OWN, 1, 0, 0), (OWN, 1, 0, 1),)),
        (4, ((OWN, 0, 2, 0), (OWN, 0, 2, 1), (FWD_Y, 1, 0), (PAR, 0, 1, 0),)),
        (5, ((PASS_Y, 0, 0), (PASS_Y, 0, 1),)),
        (6, ((OWN, 1, 3, 0), (FWD_Y, 3, 0), (PAR, 0, 3, 0),)),
        (7, ((PASS_Y, 1, 0),)),
        (8, ((FWD_Y, 1, 1), (PAR, 0, 1, 1), (PAR, 1, 0, 0),)),
        (9, ((OWN, 1, 1, 0), (OWN, 1, 3, 1), (PAR, 1, 0, 1),)),
        (10, ((FWD_Y, 3, 1), (PASS_Y, 3, 0), (PAR, 0, 3, 1),)),
        (11, ((OWN, 1, 1, 1), (OWN, 1, 2, 0), (PAR, 1, 1, 0),)),
        (12, ((FWD_Y, 2, 0), (PASS_Y, 1, 1), (PAR, 0, 2, 0),)),
        (13, ((OWN, 1, 2, 1),)),
        (14, ((FWD_Y, 2, 1), (PASS_Y, 3, 1), (PAR, 0, 2, 1),)),
        (15, ((PAR, 1, 3, 0),)),
        (16, ((PASS_Y, 2, 0),)),
        (17, ((PAR, 1, 1, 1),)),
        (18, ((PAR, 1, 3, 1),)),
        (19, ((PASS_Y, 2, 1),)),
        (20, ((PAR, 1, 2, 0),)),
        (22, ((PAR, 1, 2, 1),)),
    ),
    (
        (2, ((CROSSF, 0), (CROSSF, 1), (OWN, 0, 1, 0), (OWN, 0, 3, 0), (FWD_Y, 0, 0), (PAR, 0, 0, 0), (OWN, 0, 1, 1), (FWD_Y, 0, 1), (OWN, 0, 3, 1), (PAR, 0, 0, 1),)),
        (3, ((OWN, 1, 0, 0), (OWN, 1, 0, 1),)),
        (4, ((OWN, 0, 2, 0), (OWN, 0, 2, 1), (FWD_Y, 1, 0), (PAR, 0, 1, 0),)),
        (5, ((PASS_Y, 0, 0), (PASS_Y, 0, 1),)),
        (6, ((OWN, 1, 1, 0), (OWN, 1, 3, 0), (FWD_Y, 3, 0), (PAR, 0, 3, 0),)),
        (7, ((PASS_Y, 1, 0),)),
        (8, ((OWN, 1, 1, 1), (FWD_Y, 1, 1), (PAR, 0, 1, 1), (PAR, 1, 0, 0),)),
        (9, ((OWN, 1, 3, 1), (PAR, 1, 0, 1),)),
        (10, ((FWD_Y, 3, 1), (PASS_Y, 3, 0), (PAR, 0, 3, 1),)),
        (11, ((OWN, 1, 2, 0), (OWN, 1, 2, 1), (PAR, 1, 1, 0),)),
        (12, ((FWD_Y, 2, 0), (PASS_Y, 1, 1), (PAR, 0, 2, 0),)),
        (13, ((PASS_Y, 3, 1),)),
        (14, ((FWD_Y, 2, 1), (PAR, 0, 2, 1),)),
        (15, ((PAR, 1, 3, 0),)),
        (16, ((PASS_Y, 2, 0),)),
        (17, ((PAR, 1, 1, 1),)),
        (18, ((PAR, 1, 3, 1),)),
        (19, ((PASS_Y, 2, 1),)),
        (20, ((PAR, 1, 2, 0),)),
        (22, ((PAR, 1, 2, 1),)),
    ),
    (
        (2, ((CROSSF, 0), (CROSSF, 1), (OWN, 0, 1, 0), (OWN, 0, 3, 0), (FWD_Y, 0, 0), (PAR, 0, 0, 0), (OWN, 0, 1, 1), (FWD_Y, 0, 1), (OWN, 0, 3, 1), (PAR, 0, 0, 1),)),
        (3, ((OWN, 1, 0, 0), (OWN, 1, 0, 1),)),
        (4, ((OWN, 0, 2, 0), (OWN, 0, 2, 1), (FWD_Y, 1, 0), (PAR, 0, 1, 0),)),
        (5, ((PASS_Y, 0, 0), (PASS_Y, 0, 1),)),
        (6, ((OWN, 1, 1, 0), (OWN, 1, 3, 0), (FWD_Y, 3, 0), (PAR, 0, 3, 0),)),
        (7, ((PASS_Y, 1, 0),)),
        (8, ((OWN, 1, 1, 1), (FWD_Y, 1, 1), (PAR, 0, 1, 1), (PAR, 1, 0, 0),)),
        (9, ((OWN, 1, 3, 1), (PAR, 1, 0, 1),)),
        (10, ((FWD_Y, 3, 1), (PASS_Y, 3, 0), (PAR, 0, 3, 1),)),
        (11, ((OWN, 1, 2, 0), (OWN, 1, 2, 1), (PAR, 1, 1, 0),)),
        (12, ((FWD_Y, 2, 0), (PASS_Y, 1, 1), (PAR, 0, 2, 0),)),
        (13, ((PASS_Y, 3, 1),)),
        (14, ((FWD_Y, 2, 1), (PAR, 0, 2, 1),)),
        (15, ((PAR, 1, 3, 0),)),
        (16, ((PASS_Y, 2, 0),)),
        (17, ((PAR, 1, 1, 1),)),
        (18, ((PAR, 1, 3, 1),)),
        (19, ((PASS_Y, 2, 1),)),
        (20, ((PAR, 1, 2, 0),)),
        (22, ((PAR, 1, 2, 1),)),
    ),
    (
        (2, ((CROSSF, 0), (CROSSF, 1), (OWN, 0, 1, 0), (OWN, 0, 3, 0), (FWD_Y, 0, 0), (OWN, 0, 1, 1), (OWN, 0, 3, 1), (FWD_Y, 0, 1),)),
        (3, ((OWN, 1, 0, 0), (OWN, 1, 0, 1),)),
        (4, ((OWN, 0, 2, 0), (OWN, 0, 2, 1), (FWD_Y, 1, 0),)),
        (5, ((PAR, 0, 0, 0), (PAR, 1, 0, 0),)),
        (6, ((OWN, 1, 1, 0), (OWN, 1, 3, 0), (FWD_Y, 3, 0),)),
        (7, ((PAR, 0, 0, 1), (PAR, 1, 0, 1),)),
        (8, ((OWN, 1, 1, 1), (FWD_Y, 1, 1),)),
        (9, ((OWN, 1, 3, 1), (PAR, 0, 1, 0), (PAR, 1, 1, 0),)),
        (10, ((FWD_Y, 3, 1),)),
        (11, ((PAR, 0, 3, 0), (PAR, 1, 3, 0),)),
        (12, ((OWN, 1, 2, 0), (FWD_Y, 2, 0),)),
        (13, ((PAR, 0, 1, 1), (PAR, 1, 1, 1),)),
        (14, ((FWD_Y, 2, 1),)),
        (15, ((PAR, 0, 3, 1), (PAR, 1, 3, 1),)),
        (17, ((PAR, 0, 2, 0), (PAR, 1, 2, 0),)),
        (19, ((PAR, 0, 2, 1), (PAR, 1, 2, 1),)),
        (21, ((OWN, 1, 2, 1),)),
    ),
    (
        (2, ((CROSSF, 0), (CROSSF, 1), (OWN, 0, 1, 0), (OWN, 0, 3, 0), (FWD_Y, 0, 0), (OWN, 0, 1, 1), (OWN, 0, 3, 1), (FWD_Y, 0, 1),)),
        (3, ((OWN, 1, 0, 0), (OWN, 1, 0, 1),)),
        (4, ((OWN, 0, 2, 0), (OWN, 0, 2, 1), (FWD_Y, 1, 0),)),
        (5, ((PAR, 0, 0, 0), (PAR, 1, 0, 0),)),
        (6, ((OWN, 1, 1, 0), (OWN, 1, 3, 0), (FWD_Y, 3, 0),)),
        (7, ((PAR, 0, 0, 1), (PAR, 1, 0, 1),)),
        (8, ((OWN, 1, 1, 1), (FWD_Y, 1, 1),)),
        (9, ((OWN, 1, 3, 1), (PAR, 0, 1, 0), (PAR, 1, 1, 0),)),
        (10, ((FWD_Y, 3, 1),)),
        (11, ((PAR, 0, 3, 0), (PAR, 1, 3, 0),)),
        (12, ((OWN, 1, 2, 0), (FWD_Y, 2, 0),)),
        (13, ((PAR, 0, 1, 1), (PAR, 1, 1, 1),)),
        (14, ((OWN, 1, 2, 1), (FWD_Y, 2, 1),)),
        (15, ((PAR, 0, 3, 1), (PAR, 1, 3, 1),)),
        (17, ((PAR, 0, 2, 0), (PAR, 1, 2, 0),)),
        (19, ((PAR, 0, 2, 1), (PAR, 1, 2, 1),)),
    ),
    (
        (2, ((CROSSF, 0), (CROSSF, 1), (OWN, 0, 1, 0), (OWN, 0, 3, 0), (FWD_Y, 0, 0), (OWN, 0, 1, 1), (OWN, 0, 3, 1), (FWD_Y, 0, 1),)),
        (3, ((OWN, 1, 0, 0), (OWN, 1, 0, 1),)),
        (4, ((OWN, 0, 2, 0), (OWN, 0, 2, 1), (FWD_Y, 1, 0),)),
        (5, ((PAR, 0, 0, 0), (PAR, 1, 0, 0),)),
        (6, ((OWN, 1, 1, 0), (OWN, 1, 3, 0), (FWD_Y, 3, 0),)),
        (7, ((PAR, 0, 0, 1), (PAR, 1, 0, 1),)),
        (8, ((OWN, 1, 1, 1), (FWD_Y, 1, 1),)),
        (9, ((OWN, 1, 3, 1), (PAR, 0, 1, 0), (PAR, 1, 1, 0),)),
        (10, ((FWD_Y, 3, 1),)),
        (11, ((OWN, 1, 2, 0), (OWN, 1, 2, 1), (PAR, 0, 3, 0), (PAR, 1, 3, 0),)),
        (12, ((FWD_Y, 2, 0),)),
        (13, ((PAR, 0, 1, 1), (PAR, 1, 1, 1),)),
        (14, ((FWD_Y, 2, 1),)),
        (15, ((PAR, 0, 3, 1), (PAR, 1, 3, 1),)),
        (17, ((PAR, 0, 2, 0), (PAR, 1, 2, 0),)),
        (19, ((PAR, 0, 2, 1), (PAR, 1, 2, 1),)),
    ),
    (
        (2, ((CROSSF, 0), (CROSSF, 1), (OWN, 0, 1, 0), (OWN, 0, 3, 0), (FWD_Y, 0, 0), (OWN, 0, 1, 1), (OWN, 0, 3, 1), (FWD_Y, 0, 1),)),
        (3, ((OWN, 1, 0, 0), (OWN, 1, 0, 1),)),
        (4, ((OWN, 0, 2, 0), (OWN, 0, 2, 1), (FWD_Y, 1, 0),)),
        (5, ((PAR, 0, 0, 0), (PAR, 1, 0, 0),)),
        (6, ((OWN, 1, 1, 0), (OWN, 1, 3, 0), (FWD_Y, 3, 0),)),
        (7, ((PAR, 0, 0, 1), (PAR, 1, 0, 1),)),
        (8, ((OWN, 1, 1, 1), (FWD_Y, 1, 1),)),
        (9, ((OWN, 1, 3, 1), (PAR, 0, 1, 0), (PAR, 1, 1, 0),)),
        (10, ((FWD_Y, 3, 1),)),
        (11, ((OWN, 1, 2, 0), (OWN, 1, 2, 1), (PAR, 0, 3, 0), (PAR, 1, 3, 0),)),
        (12, ((FWD_Y, 2, 0),)),
        (13, ((PAR, 0, 1, 1), (PAR, 1, 1, 1),)),
        (14, ((FWD_Y, 2, 1),)),
        (15, ((PAR, 0, 3, 1), (PAR, 1, 3, 1),)),
        (17, ((PAR, 0, 2, 0), (PAR, 1, 2, 0),)),
        (19, ((PAR, 0, 2, 1), (PAR, 1, 2, 1),)),
    ),
)

STAGES = len(SEQUENCE)
POINTS = PARTS * STAGES + 1
PAR_AT, T1_AT, T2_AT, T3_AT, TC_AT, SLOTS = 32, 64, 72, 80, 88, 90
WAYS = ("x+", "x-", "y+", "y-", "z+", "z-", "core", "ya", "yb", "za", "zb")
WAIT = 15
CLASSES = [(x, y) for x in range(4) for y in range(4)]


def sign_of(j, k):
    return "+" if (k + (0, 1, 1, 0)[j]) % 2 == 0 else "-"


def name_of(x, y, row, j):
    return (y // 2 + row) % 2 * 4 + (x + 4 - j) % 4


def row_behind(y, sign):
    return (y + 3) % 4 // 2 if sign == "+" else (y + 1) % 4 // 2


def feed(x, y, j, k, src):
    up = y // 2 == 1
    final, via1, via2 = ("par", name_of(x, y, 0, j), k), ("t1", j, k), ("t2", j, k)
    sends = []
    if x in (0, 1):
        sends.append((src, via1, "z" + sign_of(j, k)))
    if x == 1:
        sends.append((src, final, "ya"))
    if x in (2, 3):
        sends.append((src, final if x == 2 and not up else via1, "za"))
        sends.append((src, final if x == 2 and up else via2, "zb"))
    return sends


def expand(x, y, event):
    kind, args = event[0], event[1:]
    up = y // 2 == 1
    ops = []
    if kind == CROSSF:
        (k,) = args
        sign = "+-"[k]
        ops = [("tc", k), (("tc", k), ("own", row_behind(y, sign) * 4 + x, k), "y" + sign)]
    if kind == OWN:
        row, j, k = args
        here = ("own", name_of(x, y, row, j), k)
        ops = [here]
        if (row, j) == (1, 0) or (j == 1 and (k + row) % 2 == 0):
            ops.append((here, here, "x+"))
        if (row, j) == (1, 0) or (j == 3 and (k + row) % 2 == 1):
            ops.append((here, here, "x-"))
        if row == 0:
            ops += feed(x, y, j, k, here)
        ops.append((here, here, "core"))
    if kind == PASS_Z:
        j, k = args
        here = ("t1", j, k)
        there = ("par", name_of(x, y, 0, j), k) if x == 0 and up else ("t2", j, k)
        ops = [here, (here, there, "z" + sign_of(j, k))]
    if kind == FWD_Y:
        j, k = args
        final, there, way = ("par", name_of(x, y, 0, j), k), ("t3", j, k), "y" + sign_of(j, k)
        if x == 3 or (x == 2 and up):
            ops += [("t1", j, k), (("t1", j, k), final, "ya") if x == 3 else (("t1", j, k), there, way)]
        if x in (1, 3) or not up:
            ops += [("t2", j, k), (("t2", j, k), final, "yb") if x in (1, 3) else (("t2", j, k), there, way)]
    if kind == PASS_Y:
        j, k = args
        sign = sign_of(j, k)
        row = row_behind(y, sign)
        if x == 2 or row == 0:
            ops = [("t3", j, k), (("t3", j, k), ("par", row * 4 + (x + 4 - j) % 4, k), "y" + sign)]
    if kind == PAR:
        row, j, k = args
        here = ("par", name_of(x, y, row, j), k)
        ops = [here, (here, here, "core")]
    return ops


def slot(place, c):
    kind, rest = place[0], place[1:]
    if kind in ("own", "par"):
        q, k = rest
        return (PAR_AT if kind == "par" else 0) + q * 4 + c * 2 + k
    if kind == "tc":
        return TC_AT + rest[0]
    return {"t1": T1_AT, "t2": T2_AT, "t3": T3_AT}[kind] + rest[0] * 2 + rest[1]


def tables(x, y):
    per_core = []
    for c in range(2):
        ops, begins, sends, at = [], [], 0, dict(EVENTS[CLASSES.index((x, y))])
        for point in range(POINTS):
            begins.append(len(ops))
            for event in at.get(point, ()):
                for op in expand(x, y, event):
                    if isinstance(op[0], str):
                        ops.append(slot(op, c) + 2097152 * WAIT)
                    else:
                        src, dst, way = op
                        ops.append(slot(src, c) + 128 * slot(dst, c) + 16384 * sends + 2097152 * WAYS.index(way))
                        sends += 1
        per_core.append((ops, begins + [len(ops)], sends))
    return per_core


TABLES = {cls: tables(*cls) for cls in CLASSES}
MOST_OPS = max(len(ops) for cores in TABLES.values() for ops, _, _ in cores)
MOST_SENDS = max(sends for cores in TABLES.values() for _, _, sends in cores)
FIRST_SENDS = 12


def columns(t):
    first, last = t * 256, (t + 1) * 256
    cuts = [first] + [cut for cut in range(0, NI * V, V) if first < cut < last] + [last]
    return [(u - first, w - first, u // V, u % V) for u, w in zip(cuts, cuts[1:])]


def kernel(dims, mine, amps, out, out_own, out_par, buf, rc, half, acc, ops, begins, devs,
           ssem, first_sem, rsem, local_sem):
    sym, tile, c = lax.axis_index("sym"), lax.axis_index("tile"), lax.axis_index("occ")
    x, yhi = sym % 4, sym // 4
    x0, x1 = x % 2, x // 2
    z, ylo = tile // 2, tile % 2
    z0, z1 = z % 2, z // 2
    y = 2 * yhi + ylo
    none = sym == 0

    def dev(dx=0, dy=0, dz=0, dc=0):
        xx, yy, zz = (x + 4 + dx) % 4, (y + 4 + dy) % 4, (z + 4 + dz) % 4
        return ((yy // 2) * 4 + xx) * 16 + (zz * 2 + yy % 2) * 2 + (c + dc) % 2

    step_a = 1 - 2 * (yhi + ylo - 2 * yhi * ylo)
    step_z = 1 - 2 * z0
    to = {
        "x+": dev(dx=1), "x-": dev(dx=-1), "y+": dev(dy=1), "y-": dev(dy=-1), "z+": dev(dz=1), "z-": dev(dz=-1),
        "core": dev(dc=1), "ya": dev(dy=step_a), "yb": dev(dy=-step_a), "za": dev(dz=step_z), "zb": dev(dz=-step_z),
    }
    barrier = pltpu.get_barrier_semaphore()
    for way in WAYS[:7]:
        pl.semaphore_signal(barrier, inc=1, device_id=to[way], device_id_type=pl.DeviceIdType.LOGICAL)

    def own_slot(q, core, k):
        return q * 4 + core * 2 + k

    keep = []
    for k in range(PIECES):
        keep.append(pltpu.make_async_copy(mine.at[pl.ds(k * PV, PV)], buf.at[own_slot(sym, c, k)], local_sem.at[8 + k]))
        keep[-1].start()
    loads = [pltpu.make_async_copy(amps.at[i], rc.at[:, pl.ds(i * V, V)], local_sem.at[i]) for i in range(NI)]
    for load in loads:
        load.start()

    pl.semaphore_wait(barrier, 7)

    def remote(src, dst_slot, sem, where):
        return pltpu.make_async_remote_copy(
            src, buf.at[dst_slot], sem, rsem.at[dst_slot], device_id=where, device_id_type=pl.DeviceIdType.LOGICAL
        )

    def arrived(at):
        remote(buf.at[at], at, first_sem.at[0], to["core"]).wait_recv()

    firsts = []

    def first(src, place, where, cond=None):
        index = len(firsts)
        if cond is None:
            remote(src, place, first_sem.at[index], where).start()
        else:
            pl.when(cond)(lambda: remote(src, place, first_sem.at[index], where).start())
        firsts.append((src, place, cond, index))

    step_2 = {k: {"+": to["z+"], "-": to["z-"]}[sign_of(0, k)] for k in range(PIECES)}
    for k in range(PIECES):
        src = mine.at[pl.ds(k * PV, PV)]
        home = own_slot(sym, c, k)
        final, via1, via2 = PAR_AT + home, T1_AT + k, T2_AT + k
        first(src, home, to["core"])
        first(src, home, to["x+"])
        first(src, home, to["x-"])
        first(src, TC_AT + k, to["y" + "+-"[k]])
        direct_b, direct_a = x0 + 2 * (1 - x1) + (1 - yhi) == 0, x0 + 2 * (1 - x1) + yhi == 0
        where_b = x1 * to["zb"] + (1 - x1) * step_2[k]
        place_b = jnp.where(direct_b, final, x1 * via2 + (1 - x1) * via1)
        first(src, place_b, where_b)
        where_a = x1 * to["za"] + (1 - x1) * to["ya"]
        place_a = jnp.where(direct_a | (x1 == 0), final, via1)
        first(src, place_a, where_a, x > 0)

    for (at_x, at_y), cores in TABLES.items():
        @pl.when((x == at_x) & (y == at_y))
        def _():
            (ops0, begins0, _), (ops1, _, _) = cores
            for n, (op0, op1) in enumerate(zip(ops0, ops1)):
                ops[n] = op0 + (op1 - op0) * c if op0 != op1 else op0
            for n, begin in enumerate(begins0):
                begins[n] = begin
    for n, way in enumerate(WAYS):
        devs[n] = to[way]

    n_row = dims[tile]
    n_col = dims[(z1 + yhi - 2 * z1 * yhi) * 4 + (z0 + x1 - 2 * z0 * x1) * 2 + (ylo + x0 - 2 * ylo * x0)]
    live_r = jnp.where(lax.broadcasted_iota(jnp.int32, (V, V), 0) < n_row, 1.0, 0.0)
    live = jnp.where(lax.broadcasted_iota(jnp.int32, (V, V), 1) < n_col, live_r, 0.0).astype(jnp.bfloat16)
    acc[...] = jnp.zeros_like(acc)
    for load in loads:
        load.wait()
    for i in range(NI):
        rc[:, i * V:(i + 1) * V] = rc[:, i * V:(i + 1) * V] * live
    for copy in keep:
        copy.wait()

    def decoded(n):
        op = ops[n]
        src, rest = lax.rem(op, 128), lax.div(op, 128)
        dst, rest = lax.rem(rest, 128), lax.div(rest, 128)
        return src, dst, lax.rem(rest, 128), lax.div(rest, 128)

    def events(point):
        @pl.loop(begins[point], begins[point + 1])
        def _(n):
            src, dst, index, way = decoded(n)

            @pl.when(way == WAIT)
            def _():
                arrived(src)

            @pl.when(way != WAIT)
            def _():
                remote(buf.at[src], dst, ssem.at[index], devs[way]).start()

    digit = (1 + 7 * x0) * (1 + 63 * x1) * (1 + 4095 * yhi)

    def chosen(groups, n):
        code = 0
        for k, names in enumerate(groups):
            packed = [0, 0]
            for (at_x, at_y), (row, j) in zip(CLASSES, names):
                packed[at_y % 2] += (row * 4 + j) * 8 ** (at_y // 2 * 4 + at_x)
            code = code + (n == k) * 1 * (packed[0] + (packed[1] - packed[0]) * ylo)
        code = lax.rem(lax.div(code, digit), 8)
        return (yhi + code // 4) % 2 * 4 + (x + 4 - code % 4) % 4

    def unit(base, q, core):
        at = base + q * 4 + core * 2
        return buf[pl.ds(at, 2)].reshape(V, V)

    def first_stage(n, q):
        for k in range(PIECES):
            arrived(own_slot(q, 1 - c, k))

        @pl.when(none)
        def _():
            pltpu.make_async_copy(buf.at[pl.ds(q * 4, 4)], buf.at[pl.ds(PAR_AT + q * 4, 4)], local_sem.at[10 + q]).start()

        for h in range(PARTS):
            if h:
                events(PARTS * n + h)
            for t in range(h * 12 // PARTS, (h + 1) * 12 // PARTS):
                left = buf[pl.ds(q * 4, 4)].reshape(2 * V, V)
                r = jnp.dot(left, rc[:, t * 256:(t + 1) * 256], preferred_element_type=jnp.float32).astype(jnp.bfloat16)
                for lo_col, hi_col, pair, at in columns(t):
                    for p in range(2):
                        lanes = pl.ds(p * V + at, hi_col - lo_col)
                        half[q, pair * V:(pair + 1) * V, lanes] = r[p * V:(p + 1) * V, lo_col:hi_col]

    def second_stage(n, q):
        @pl.when(none)
        def _():
            pltpu.make_async_copy(buf.at[pl.ds(q * 4, 4)], buf.at[pl.ds(PAR_AT + q * 4, 4)], local_sem.at[10 + q]).wait()

        @pl.when(jnp.logical_not(none))
        def _():
            for k in range(PIECES):
                arrived(PAR_AT + own_slot(q, 1 - c, k))

        for h in range(2):
            if h and PARTS > 1:
                events(PARTS * n + h)
            rows = pl.ds(h * HALF, HALF)
            for b0, b1 in ((0, 256), (256, 384)):
                right = jnp.concatenate([unit(PAR_AT, q, p)[b0:b1] for p in range(2)], axis=1)
                acc[rows, b0:b1] += lax.dot_general(
                    half[q, rows, :], right, (((1,), (1,)), ((), ())), preferred_element_type=jnp.float32
                )

    @pl.loop(0, STAGES)
    def _(n):
        second = sum((n == k) * 1 for k, stage in enumerate(SEQUENCE) if stage == 2)
        q = chosen(UNITS, n)
        events(PARTS * n)
        pl.when(second == 0)(lambda: first_stage(n, q))
        pl.when(second == 1)(lambda: second_stage(n, q))

    for h in range(2):
        rows = pl.ds(h * HALF, HALF)
        pltpu.make_async_copy(acc.at[rows], out.at[rows], local_sem.at[h]).start()
    events(POINTS - 1)

    leaving = []
    for r in range(len(REST)):
        q = chosen(REST, jnp.int32(r))
        for k in range(PIECES):
            arrived(own_slot(q, 1 - c, k))

        @pl.when(jnp.logical_not(none))
        def _():
            for k in range(PIECES):
                arrived(PAR_AT + own_slot(q, 1 - c, k))

        par_at = jnp.where(none, 0, PAR_AT) + q * 4
        for source, target, sem in ((q * 4, out_own.at[r], 18 + 2 * r), (par_at, out_par.at[r], 19 + 2 * r)):
            leaving.append(pltpu.make_async_copy(buf.at[pl.ds(source, 4)], target, local_sem.at[sem]))
            leaving[-1].start()

    for src, place, cond, index in firsts:
        def sent(src=src, place=place, index=index):
            remote(src, place, first_sem.at[index], to["core"]).wait_send()

        if cond is None:
            sent()
        else:
            pl.when(cond)(sent)

    @pl.loop(0, begins[POINTS])
    def _(n):
        src, dst, index, way = decoded(n)

        @pl.when(way != WAIT)
        def _():
            remote(buf.at[src], dst, ssem.at[index], devs[way]).wait_send()

    for h in range(2):
        rows = pl.ds(h * HALF, HALF)
        pltpu.make_async_copy(acc.at[rows], out.at[rows], local_sem.at[h]).wait()
    for copy in leaving:
        copy.wait()


ALL = [(row, j) for j in (0, 1, 3, 2) for row in range(2)]


def left_over():
    by_class = []
    for at in range(len(CLASSES)):
        done = [names[at] for stage, names in zip(SEQUENCE, UNITS) if stage == 1]
        by_class.append([name for name in ALL if name not in done])
    return tuple(zip(*by_class))


REST = left_over()


def rest_kernel(dims, own_hbm, par_hbm, amps, raw, out, own, par, rc, half, acc, sems):
    sym, tile = lax.axis_index("sym"), lax.axis_index("tile")
    n, hi = len(REST), NI // 2
    get_own = pltpu.make_async_copy(own_hbm, own, sems.at[0])
    get_par = pltpu.make_async_copy(par_hbm, par, sems.at[1])
    get_amps = [pltpu.make_async_copy(amps.at[i], rc.at[:, pl.ds(i * V, V)], sems.at[2 + i]) for i in range(NI)]
    get_raw = [
        pltpu.make_async_copy(raw.at[pl.ds(h * HALF, HALF)], acc.at[pl.ds(h * HALF, HALF)], sems.at[2 + NI + h])
        for h in range(2)
    ]
    for copy in get_amps[:hi] + [get_own, get_par, get_raw[0]] + get_amps[hi:] + [get_raw[1]]:
        copy.start()
    n_row, n_col = dims[tile], dims[jnp.bitwise_xor(tile, sym)]
    live = (lax.broadcasted_iota(jnp.int32, (V, V), 0) < n_row) & (lax.broadcasted_iota(jnp.int32, (V, V), 1) < n_col)
    live_b = jnp.where(live, 1.0, 0.0).astype(jnp.bfloat16)
    puts = []
    for h in range(2):
        for i in range(h * hi, (h + 1) * hi):
            get_amps[i].wait()
            rc[:, i * V:(i + 1) * V] = rc[:, i * V:(i + 1) * V] * live_b
        if h == 0:
            get_own.wait()
        for t in range(6 * h, 6 * (h + 1)):
            left = own[...].reshape(n * 2 * V, V)
            r = jnp.dot(left, rc[:, t * 256:(t + 1) * 256], preferred_element_type=jnp.float32).astype(jnp.bfloat16)
            for lo_col, hi_col, pair, at in columns(t):
                for p in range(2 * n):
                    lanes = pl.ds(p * V + at, hi_col - lo_col)
                    half[(pair - h * hi) * V:(pair - h * hi + 1) * V, lanes] = r[p * V:(p + 1) * V, lo_col:hi_col]
        if h == 0:
            get_par.wait()
        get_raw[h].wait()
        rows = pl.ds(h * HALF, HALF)
        for b0, b1 in ((0, 256), (256, 384)):
            right = [par[r, pl.ds(2 * p, 2)].reshape(V, V)[b0:b1] for r in range(n) for p in range(2)]
            right = jnp.concatenate(right, axis=1)
            r = lax.dot_general(half[...], right, (((1,), (1,)), ((), ())), preferred_element_type=jnp.float32)
            r = r + acc[rows, b0:b1]
            for i in range(hi):
                at = pl.ds((h * hi + i) * V, V)
                acc[at, b0:b1] = jnp.where(live[:, b0:b1], r[i * V:(i + 1) * V], 0.0)
            lanes = pl.ds(b0, b1 - b0)
            puts.append(pltpu.make_async_copy(acc.at[rows, lanes], out.at[rows, lanes], sems.at[4 + NI + len(puts)]))
            puts[-1].start()
    for copy in puts:
        copy.wait()


def shards(irrep_dims, chol_vectors, amplitudes):
    bf, sem = jnp.bfloat16, pltpu.SemaphoreType.DMA
    n = len(REST)
    own, chol, amps = (n, 4, PV, V), chol_vectors.reshape(V, V), amplitudes.reshape(NI, V, V)
    anywhere = pl.BlockSpec(memory_space=pl.ANY)
    raw, rest_own, rest_par = pl.pallas_call(
        kernel,
        out_shape=[
            jax.ShapeDtypeStruct((NI * V, V), jnp.float32),
            jax.ShapeDtypeStruct(own, bf),
            jax.ShapeDtypeStruct(own, bf),
        ],
        in_specs=[pl.BlockSpec(memory_space=pltpu.SMEM), anywhere, anywhere],
        out_specs=[anywhere] * 3,
        scratch_shapes=[
            pltpu.VMEM((SLOTS, PV, V), bf),
            pltpu.VMEM((V, NI * V), bf),
            pltpu.VMEM((8, NI * V, 2 * V), bf),
            pltpu.VMEM((NI * V, V), jnp.float32),
            pltpu.SMEM((MOST_OPS,), jnp.int32),
            pltpu.SMEM((POINTS + 1,), jnp.int32),
            pltpu.SMEM((len(WAYS),), jnp.int32),
            sem((MOST_SENDS,)), sem((FIRST_SENDS,)), sem((SLOTS,)), sem((18 + 2 * n,)),
        ],
        compiler_params=pltpu.CompilerParams(
            collective_id=0, has_side_effects=True, vmem_limit_bytes=63 * 1024 * 1024
        ),
        cost_estimate=pl.CostEstimate(flops=(8 - n) * 3_600_000_000, bytes_accessed=12_000_000, transcendentals=0),
        name="ladder",
    )(irrep_dims, chol, amps)
    total = pl.pallas_call(
        rest_kernel,
        out_shape=jax.ShapeDtypeStruct((NI * V, V), jnp.float32),
        in_specs=[pl.BlockSpec(memory_space=pltpu.SMEM)] + [anywhere] * 4,
        out_specs=anywhere,
        scratch_shapes=[
            pltpu.VMEM(own, bf),
            pltpu.VMEM(own, bf),
            pltpu.VMEM((V, NI * V), bf),
            pltpu.VMEM((HALF, n * 2 * V), bf),
            pltpu.VMEM((NI * V, V), jnp.float32),
            sem((8 + NI,)),
        ],
        compiler_params=pltpu.CompilerParams(vmem_limit_bytes=60 * 1024 * 1024),
        cost_estimate=pl.CostEstimate(flops=n * 3_600_000_000, bytes_accessed=16_000_000, transcendentals=0),
        name="rest",
    )(irrep_dims, rest_own, rest_par, amps, raw)
    return total.reshape(1, NI, V, V)


def solution(mesh):
    return jax.shard_map(
        shards,
        mesh=mesh,
        in_specs=(P(), P(("sym", "occ"), "tile", None), P("sym", "occ", "tile", None)),
        out_specs=P("sym", "occ", "tile", None),
        check_vma=False,
    )
```

profile of v0, /device:TPU:17, one launch (start us, length us, event | category | flops | bytes accessed | tf_op | source)
XLA Modules:
  0.0 74.8 jit_solution(8106285860416858064)
XLA Ops:
  0.0 60.1 %ladder.1 = (f32[3072,384]{1,0:T(8,128)}, bf16[2,4,192,384]{3,2,1,0:T(8,128)(2,1)}, bf16[2,4,192,384]{3,2,1,0:T(8,128)(2,1)}) custom-call(s32[8]{0:T(128)} %dims.3, bf16[384,384]{1,0:T(8,128)(2,1)} %bitcast.5, bf16[8,384,384]{2,1,0:T(8,128)(2,1)} %bitcast.3), custom_call_target="tpu_custom_call" | custom-call | flops 21600000000 | bytes 12000000 | tf_op jit(solution)/shard_map/ladder/pallas_call | solution.py:747
  60.1 14.6 %rest.1 = f32[3072,384]{1,0:T(8,128)} custom-call(s32[8]{0:T(128)} %dims.3, bf16[2,4,192,384]{3,2,1,0:T(8,128)(2,1)} %get-tuple-element.8.own_hbm, bf16[2,4,192,384]{3,2,1,0:T(8,128)(2,1)} %get-tuple-element.9.par_hbm, bf16[8,384,384]{2,1,0:T(8,128)(2,1)} %bitcast.4, f32[3072,384]{1,0:T(8,128)} %get-tuple-element.10.raw), custom_call_target="tpu_custom_call" | custom-call | flops 7200000000 | bytes 16000000 | tf_op jit(solution)/shard_map/rest/pallas_call | solution.py:772
where the time goes:
time: 74.9 us; the launch traced here: 74.8 us
  Pallas kernels  74.7 us (100%)
    pallas_call x1, Pallas kernels, shards(): pl.pallas_call(kernel, out_shape=[jax.ShapeDtypeStruct((NI * V, V), jnp.f...  60.1 us
    pallas_call x1, Pallas kernels, shards(): pl.pallas_call(rest_kernel, out_shape=jax.ShapeDtypeStruct((NI * V, V), j...  14.6 us

commit v1 on v0

v1 whole, which is shorter than its diff:
```python
import jax
import jax.numpy as jnp
from jax import lax
from jax.experimental import pallas as pl
from jax.experimental.pallas import tpu as pltpu
from jax.sharding import PartitionSpec as P

V = 384
NI = 8
PIECES = 2
PV = V // PIECES
HALF = NI * V // 2
CROSSF, OWN, PASS_Z, FWD_Y, PASS_Y, PAR = range(6)
PARTS = {1: 2, 2: 1}
SEQUENCE = (1, 1, 1, 1, 1, 2, 1, 2, 1, 2, 2, 2, 2, 2)
UNITS = (
    (
        ((0, 0, 0), (0, 0, 0), (0, 0, 0), (0, 0, 0), (0, 0, 0), (0, 0, 0), (0, 0, 0), (0, 0, 0), (0, 0, 0), (0, 0, 0), (0, 0, 0), (0, 0, 0), (0, 0, 0), (0, 0, 0), (0, 0, 0), (0, 0, 0)),
        ((0, 1, 0), (0, 1, 0), (0, 1, 0), (0, 1, 0), (0, 1, 0), (0, 1, 0), (0, 1, 0), (0, 1, 0), (0, 1, 0), (0, 1, 0), (0, 1, 0), (0, 1, 0), (0, 1, 0), (0, 1, 0), (0, 1, 0), (0, 1, 0)),
        ((0, 1, 1), (0, 1, 1), (0, 1, 1), (0, 1, 1), (0, 1, 1), (0, 1, 1), (0, 1, 1), (0, 1, 1), (0, 1, 1), (0, 1, 1), (0, 1, 1), (0, 1, 1), (0, 1, 1), (0, 1, 1), (0, 1, 1), (0, 1, 1)),
        ((1, 0, 0), (1, 0, 0), (1, 0, 0), (1, 0, 0), (0, 2, 0), (0, 2, 0), (1, 0, 0), (1, 0, 0), (1, 0, 0), (1, 0, 0), (1, 0, 0), (1, 0, 0), (1, 0, 0), (1, 0, 0), (1, 0, 0), (1, 0, 0)),
        ((0, 2, 0), (0, 2, 0), (0, 2, 0), (0, 2, 0), (1, 0, 0), (1, 0, 0), (0, 2, 0), (1, 0, 1), (0, 2, 0), (0, 2, 0), (0, 2, 0), (0, 2, 0), (0, 2, 0), (0, 2, 0), (0, 2, 0), (0, 2, 0)),
        ((0, 0, 0), (0, 0, 0), (0, 0, 0), (0, 0, 0), (0, 0, 0), (0, 0, 0), (1, 0, 0), (1, 0, 0), (0, 0, 0), (0, 0, 0), (0, 0, 0), (0, 0, 0), (0, 0, 0), (0, 0, 0), (0, 0, 0), (0, 0, 0)),
        ((1, 1, 0), (1, 1, 0), (1, 1, 0), (1, 1, 0), (1, 3, 0), (1, 1, 0), (1, 1, 0), (1, 1, 0), (1, 3, 0), (1, 3, 0), (1, 1, 0), (1, 1, 0), (1, 1, 0), (1, 1, 0), (1, 1, 0), (1, 1, 0)),
        ((1, 0, 0), (1, 0, 0), (1, 0, 0), (1, 0, 0), (0, 1, 0), (1, 0, 0), (0, 0, 0), (0, 0, 0), (1, 0, 0), (1, 0, 0), (1, 0, 0), (1, 0, 0), (1, 0, 0), (1, 0, 0), (1, 0, 0), (1, 0, 0)),
        ((1, 3, 0), (1, 3, 0), (1, 1, 1), (1, 1, 1), (1, 0, 1), (1, 1, 1), (1, 1, 1), (1, 1, 1), (1, 1, 0), (1, 1, 0), (1, 1, 1), (1, 1, 1), (1, 1, 1), (1, 1, 1), (1, 1, 1), (1, 1, 1)),
        ((0, 1, 0), (0, 1, 0), (0, 1, 0), (0, 1, 0), (1, 0, 0), (0, 1, 0), (0, 1, 0), (0, 1, 0), (0, 1, 0), (0, 1, 0), (0, 1, 0), (0, 1, 0), (0, 1, 0), (0, 1, 0), (0, 1, 0), (0, 1, 0)),
        ((1, 1, 0), (1, 1, 0), (0, 3, 0), (0, 3, 0), (1, 1, 0), (1, 1, 0), (1, 1, 0), (1, 1, 0), (1, 1, 0), (1, 1, 0), (1, 1, 0), (1, 1, 0), (1, 1, 0), (1, 1, 0), (1, 1, 0), (1, 1, 0)),
        ((0, 3, 0), (0, 3, 0), (0, 2, 0), (0, 2, 0), (0, 3, 0), (0, 3, 0), (0, 3, 0), (0, 3, 0), (0, 3, 0), (0, 3, 0), (0, 3, 0), (0, 3, 0), (0, 3, 0), (0, 3, 0), (0, 3, 0), (0, 3, 0)),
        ((1, 3, 0), (1, 3, 0), (1, 3, 0), (1, 1, 0), (1, 3, 0), (1, 3, 0), (1, 3, 0), (1, 3, 0), (1, 3, 0), (1, 3, 0), (1, 3, 0), (1, 3, 0), (1, 3, 0), (1, 3, 0), (1, 3, 0), (1, 3, 0)),
        ((0, 2, 0), (0, 2, 0), (1, 1, 0), (1, 3, 0), (0, 2, 0), (0, 2, 0), (0, 2, 0), (0, 2, 0), (0, 2, 0), (0, 2, 0), (0, 2, 0), (0, 2, 0), (0, 2, 0), (0, 2, 0), (0, 2, 0), (0, 2, 0)),
    ),
    (
        ((0, 0, 1), (0, 0, 1), (0, 0, 1), (0, 0, 1), (0, 0, 1), (0, 0, 1), (0, 0, 1), (0, 0, 1), (0, 0, 1), (0, 0, 1), (0, 0, 1), (0, 0, 1), (0, 0, 1), (0, 0, 1), (0, 0, 1), (0, 0, 1)),
        ((0, 3, 0), (0, 3, 0), (0, 3, 0), (0, 3, 0), (0, 3, 0), (0, 3, 0), (0, 3, 0), (0, 3, 0), (0, 3, 0), (0, 3, 0), (0, 3, 0), (0, 3, 0), (0, 3, 0), (0, 3, 0), (0, 3, 0), (0, 3, 0)),
        ((0, 3, 1), (0, 3, 1), (0, 3, 1), (0, 3, 1), (0, 3, 1), (0, 3, 1), (0, 3, 1), (0, 3, 1), (0, 3, 1), (0, 3, 1), (0, 3, 1), (0, 3, 1), (0, 3, 1), (0, 3, 1), (0, 3, 1), (0, 3, 1)),
        ((1, 0, 1), (1, 0, 1), (1, 0, 1), (1, 0, 1), (0, 2, 1), (0, 2, 1), (1, 0, 1), (0, 2, 0), (1, 0, 1), (1, 0, 1), (1, 0, 1), (1, 0, 1), (1, 0, 1), (1, 0, 1), (1, 0, 1), (1, 0, 1)),
        ((0, 2, 1), (0, 2, 1), (0, 2, 1), (0, 2, 1), (1, 1, 0), (1, 0, 1), (0, 2, 1), (0, 2, 1), (0, 2, 1), (0, 2, 1), (0, 2, 1), (0, 2, 1), (0, 2, 1), (0, 2, 1), (0, 2, 1), (0, 2, 1)),
        ((0, 0, 0), (0, 0, 0), (0, 0, 0), (0, 0, 0), (0, 0, 0), (0, 0, 0), (1, 0, 0), (1, 0, 0), (0, 0, 0), (0, 0, 0), (0, 0, 0), (0, 0, 0), (0, 0, 0), (0, 0, 0), (0, 0, 0), (0, 0, 0)),
        ((1, 1, 1), (1, 1, 1), (1, 3, 0), (1, 3, 0), (1, 1, 1), (1, 3, 0), (1, 3, 0), (1, 3, 0), (1, 3, 1), (1, 3, 1), (1, 3, 0), (1, 3, 0), (1, 3, 0), (1, 3, 0), (1, 3, 0), (1, 3, 0)),
        ((1, 0, 0), (1, 0, 0), (1, 0, 0), (1, 0, 0), (0, 1, 0), (1, 0, 0), (0, 0, 0), (0, 0, 0), (1, 0, 0), (1, 0, 0), (1, 0, 0), (1, 0, 0), (1, 0, 0), (1, 0, 0), (1, 0, 0), (1, 0, 0)),
        ((1, 3, 1), (1, 3, 1), (1, 3, 1), (1, 3, 1), (1, 3, 1), (1, 3, 1), (1, 3, 1), (1, 3, 1), (1, 1, 1), (1, 1, 1), (1, 3, 1), (1, 3, 1), (1, 3, 1), (1, 3, 1), (1, 3, 1), (1, 3, 1)),
        ((0, 1, 0), (0, 1, 0), (0, 1, 0), (0, 1, 0), (1, 0, 0), (0, 1, 0), (0, 1, 0), (0, 1, 0), (0, 1, 0), (0, 1, 0), (0, 1, 0), (0, 1, 0), (0, 1, 0), (0, 1, 0), (0, 1, 0), (0, 1, 0)),
        ((1, 1, 0), (1, 1, 0), (0, 3, 0), (0, 3, 0), (1, 1, 0), (1, 1, 0), (1, 1, 0), (1, 1, 0), (1, 1, 0), (1, 1, 0), (1, 1, 0), (1, 1, 0), (1, 1, 0), (1, 1, 0), (1, 1, 0), (1, 1, 0)),
        ((0, 3, 0), (0, 3, 0), (0, 2, 0), (0, 2, 0), (0, 3, 0), (0, 3, 0), (0, 3, 0), (0, 3, 0), (0, 3, 0), (0, 3, 0), (0, 3, 0), (0, 3, 0), (0, 3, 0), (0, 3, 0), (0, 3, 0), (0, 3, 0)),
        ((1, 3, 0), (1, 3, 0), (1, 3, 0), (1, 1, 0), (1, 3, 0), (1, 3, 0), (1, 3, 0), (1, 3, 0), (1, 3, 0), (1, 3, 0), (1, 3, 0), (1, 3, 0), (1, 3, 0), (1, 3, 0), (1, 3, 0), (1, 3, 0)),
        ((0, 2, 0), (0, 2, 0), (1, 1, 0), (1, 3, 0), (0, 2, 0), (0, 2, 0), (0, 2, 0), (0, 2, 0), (0, 2, 0), (0, 2, 0), (0, 2, 0), (0, 2, 0), (0, 2, 0), (0, 2, 0), (0, 2, 0), (0, 2, 0)),
    ),
)
EVENTS = (
    (
        (2, ((CROSSF, 0), (CROSSF, 1), (OWN, 0, 1, 0), (OWN, 0, 3, 0), (PASS_Z, 0, 0), (PASS_Z, 0, 1),)),
        (3, ((OWN, 0, 1, 1), (OWN, 0, 3, 1),)),
        (4, ((OWN, 1, 0, 0), (OWN, 1, 0, 1), (PASS_Z, 1, 0), (PASS_Z, 3, 0),)),
        (5, ((OWN, 0, 2, 0),)),
        (6, ((OWN, 0, 2, 1), (FWD_Y, 0, 0), (FWD_Y, 0, 1),)),
        (8, ((OWN, 1, 1, 0), (PASS_Z, 1, 1), (PASS_Z, 3, 1),)),
        (9, ((PASS_Y, 0, 1),)),
        (10, ((OWN, 1, 1, 1),)),
        (11, ((OWN, 1, 3, 0), (FWD_Y, 1, 0), (FWD_Y, 3, 0),)),
        (12, ((OWN, 1, 2, 1), (PASS_Z, 2, 0), (PASS_Z, 2, 1),)),
        (13, ((OWN, 1, 2, 0),)),
        (14, ((FWD_Y, 1, 1), (FWD_Y, 3, 1), (PASS_Y, 1, 0), (OWN, 1, 3, 1),)),
        (15, ((FWD_Y, 2, 0), (FWD_Y, 2, 1),)),
        (17, ((PASS_Y, 3, 1),)),
        (18, ((PASS_Y, 2, 0),)),
    ),
    (
        (2, ((CROSSF, 0), (CROSSF, 1), (OWN, 0, 1, 0), (OWN, 0, 3, 0), (PASS_Z, 0, 0), (PASS_Z, 0, 1),)),
        (3, ((OWN, 0, 1, 1), (OWN, 0, 3, 1),)),
        (4, ((OWN, 1, 0, 0), (OWN, 1, 0, 1), (PASS_Z, 1, 0), (PASS_Z, 3, 0),)),
        (5, ((OWN, 0, 2, 0),)),
        (6, ((OWN, 0, 2, 1), (FWD_Y, 0, 0), (FWD_Y, 0, 1),)),
        (8, ((OWN, 1, 1, 0), (PASS_Z, 1, 1), (PASS_Z, 3, 1),)),
        (9, ((PASS_Y, 0, 0),)),
        (10, ((OWN, 1, 1, 1),)),
        (11, ((OWN, 1, 3, 0), (FWD_Y, 1, 0), (FWD_Y, 3, 0),)),
        (12, ((OWN, 1, 2, 1), (PASS_Z, 2, 0), (PASS_Z, 2, 1),)),
        (13, ((OWN, 1, 3, 1),)),
        (14, ((OWN, 1, 2, 0), (FWD_Y, 1, 1), (FWD_Y, 3, 1), (PASS_Y, 3, 0),)),
        (16, ((FWD_Y, 2, 0), (FWD_Y, 2, 1),)),
        (17, ((PASS_Y, 1, 1),)),
        (18, ((PASS_Y, 2, 1),)),
    ),
    (
        (2, ((CROSSF, 0), (CROSSF, 1), (OWN, 0, 1, 0), (OWN, 0, 3, 0), (PASS_Z, 0, 0), (PASS_Z, 0, 1),)),
        (3, ((OWN, 0, 1, 1), (OWN, 0, 3, 1),)),
        (4, ((OWN, 1, 0, 0), (OWN, 1, 0, 1), (PASS_Z, 1, 0), (PASS_Z, 3, 0),)),
        (5, ((OWN, 0, 2, 0),)),
        (6, ((OWN, 0, 2, 1), (PAR, 0, 0, 0), (PAR, 0, 0, 1),)),
        (8, ((OWN, 1, 1, 0), (OWN, 1, 3, 0), (PASS_Z, 1, 1), (PASS_Z, 3, 1),)),
        (9, ((PASS_Y, 0, 0),)),
        (10, ((OWN, 1, 1, 1),)),
        (11, ((OWN, 1, 3, 1), (PAR, 0, 1, 0), (PAR, 0, 3, 0),)),
        (12, ((OWN, 1, 2, 0), (OWN, 1, 2, 1), (PASS_Z, 2, 0), (PASS_Z, 2, 1), (PAR, 1, 0, 0), (PAR, 1, 0, 1),)),
        (13, ((PAR, 0, 3, 1), (PAR, 0, 1, 1),)),
        (14, ((PASS_Y, 3, 0),)),
        (15, ((PAR, 0, 2, 0), (PAR, 0, 2, 1),)),
        (17, ((PASS_Y, 1, 1), (PAR, 1, 1, 0),)),
        (18, ((PAR, 1, 3, 0),)),
        (19, ((PASS_Y, 2, 1), (PAR, 1, 3, 1),)),
        (20, ((PAR, 1, 1, 1), (PAR, 1, 2, 0),)),
        (21, ((PAR, 1, 2, 1),)),
    ),
    (
        (2, ((CROSSF, 0), (CROSSF, 1), (OWN, 0, 1, 0), (OWN, 0, 3, 0), (PASS_Z, 0, 0), (PASS_Z, 0, 1),)),
        (3, ((OWN, 0, 1, 1), (OWN, 0, 3, 1),)),
        (4, ((OWN, 1, 0, 0), (OWN, 1, 0, 1), (PASS_Z, 1, 0), (PASS_Z, 3, 0),)),
        (5, ((OWN, 0, 2, 0),)),
        (6, ((OWN, 0, 2, 1), (PAR, 0, 0, 0), (PAR, 0, 0, 1),)),
        (8, ((OWN, 1, 1, 0), (OWN, 1, 3, 0), (PASS_Z, 1, 1), (PASS_Z, 3, 1),)),
        (9, ((PASS_Y, 0, 1),)),
        (10, ((OWN, 1, 1, 1),)),
        (11, ((OWN, 1, 3, 1), (PAR, 0, 1, 0), (PAR, 0, 3, 0),)),
        (12, ((OWN, 1, 2, 0), (OWN, 1, 2, 1), (PASS_Z, 2, 0), (PASS_Z, 2, 1), (PAR, 1, 0, 0), (PAR, 1, 0, 1),)),
        (13, ((PAR, 0, 3, 1), (PAR, 0, 1, 1),)),
        (14, ((PASS_Y, 1, 0),)),
        (15, ((PAR, 0, 2, 0), (PAR, 0, 2, 1),)),
        (17, ((PASS_Y, 3, 1), (PAR, 1, 3, 0),)),
        (18, ((PAR, 1, 1, 0),)),
        (19, ((PASS_Y, 2, 0), (PAR, 1, 1, 1),)),
        (20, ((PAR, 1, 3, 1), (PAR, 1, 2, 1),)),
        (21, ((PAR, 1, 2, 0),)),
    ),
    (
        (2, ((CROSSF, 0), (OWN, 0, 1, 0), (OWN, 0, 3, 0), (PASS_Z, 0, 0), (PASS_Z, 0, 1), (PAR, 0, 0, 0),)),
        (3, ((CROSSF, 1), (OWN, 0, 1, 1), (OWN, 0, 3, 1), (PAR, 1, 0, 0),)),
        (4, ((PASS_Z, 1, 0), (PASS_Z, 3, 0),)),
        (5, ((OWN, 0, 2, 0), (PAR, 0, 0, 1), (PAR, 1, 0, 1),)),
        (6, ((OWN, 0, 2, 1), (FWD_Y, 0, 0), (FWD_Y, 0, 1),)),
        (7, ((OWN, 1, 0, 0), (OWN, 1, 1, 0), (PAR, 0, 1, 0),)),
        (8, ((OWN, 1, 3, 0), (PASS_Z, 1, 1), (PASS_Z, 3, 1),)),
        (9, ((OWN, 1, 1, 1), (PAR, 0, 3, 0), (PAR, 1, 1, 0),)),
        (10, ((OWN, 1, 3, 1), (FWD_Y, 1, 0), (FWD_Y, 3, 0),)),
        (11, ((OWN, 1, 0, 1), (OWN, 1, 2, 0), (PASS_Z, 2, 0), (PASS_Z, 2, 1), (PAR, 1, 3, 0),)),
        (12, ((OWN, 1, 2, 1), (PAR, 0, 1, 1), (PAR, 1, 1, 1),)),
        (13, ((FWD_Y, 1, 1), (FWD_Y, 3, 1),)),
        (14, ((FWD_Y, 2, 0), (PAR, 0, 3, 1), (PAR, 1, 3, 1),)),
        (15, ((FWD_Y, 2, 1),)),
        (16, ((PAR, 0, 2, 0), (PAR, 1, 2, 0),)),
        (17, ((PAR, 0, 2, 1), (PAR, 1, 2, 1),)),
    ),
    (
        (2, ((CROSSF, 0), (OWN, 0, 1, 0), (OWN, 0, 3, 0), (PASS_Z, 0, 0), (PASS_Z, 0, 1), (PAR, 1, 0, 0),)),
        (3, ((CROSSF, 1), (OWN, 0, 1, 1), (OWN, 0, 3, 1), (PAR, 0, 0, 0),)),
        (4, ((PASS_Z, 1, 0), (PASS_Z, 3, 0),)),
        (5, ((OWN, 0, 2, 0), (PAR, 0, 0, 1), (PAR, 1, 0, 1),)),
        (6, ((OWN, 0, 2, 1), (FWD_Y, 0, 0), (FWD_Y, 0, 1),)),
        (7, ((OWN, 1, 0, 0), (OWN, 1, 0, 1), (OWN, 1, 1, 0),)),
        (8, ((OWN, 1, 3, 0), (PASS_Z, 1, 1), (PASS_Z, 3, 1),)),
        (9, ((OWN, 1, 1, 1), (PAR, 0, 1, 0), (PAR, 1, 1, 0),)),
        (10, ((OWN, 1, 3, 1), (FWD_Y, 1, 0), (FWD_Y, 3, 0),)),
        (11, ((OWN, 1, 2, 0), (OWN, 1, 2, 1), (PASS_Z, 2, 0), (PASS_Z, 2, 1), (PAR, 0, 3, 0), (PAR, 1, 3, 0),)),
        (12, ((PAR, 0, 1, 1), (PAR, 1, 1, 1),)),
        (13, ((FWD_Y, 1, 1), (FWD_Y, 3, 1),)),
        (14, ((FWD_Y, 2, 0), (FWD_Y, 2, 1), (PAR, 0, 3, 1), (PAR, 1, 3, 1),)),
        (16, ((PAR, 0, 2, 0), (PAR, 1, 2, 0),)),
        (17, ((PAR, 0, 2, 1), (PAR, 1, 2, 1),)),
    ),
    (
        (2, ((CROSSF, 0), (CROSSF, 1), (OWN, 0, 1, 0), (OWN, 0, 3, 0), (PASS_Z, 0, 0), (PASS_Z, 0, 1),)),
        (3, ((OWN, 0, 1, 1), (OWN, 0, 3, 1),)),
        (4, ((OWN, 1, 0, 0), (OWN, 1, 0, 1), (PASS_Z, 1, 0), (PASS_Z, 3, 0),)),
        (5, ((OWN, 0, 2, 0),)),
        (6, ((OWN, 0, 2, 1), (FWD_Y, 0, 0), (FWD_Y, 0, 1),)),
        (7, ((OWN, 1, 1, 0),)),
        (8, ((OWN, 1, 3, 0), (PASS_Z, 1, 1), (PASS_Z, 3, 1),)),
        (9, ((OWN, 1, 1, 1), (PAR, 0, 0, 0), (PAR, 1, 0, 0),)),
        (10, ((OWN, 1, 3, 1), (FWD_Y, 1, 0), (FWD_Y, 3, 0), (PAR, 1, 0, 1), (PAR, 0, 0, 1),)),
        (11, ((OWN, 1, 2, 0), (OWN, 1, 2, 1), (PASS_Z, 2, 0), (PASS_Z, 2, 1), (PAR, 0, 1, 0),)),
        (12, ((FWD_Y, 1, 1), (FWD_Y, 3, 1), (PAR, 1, 1, 0),)),
        (13, ((PAR, 0, 3, 0),)),
        (14, ((FWD_Y, 2, 0), (FWD_Y, 2, 1), (PAR, 1, 3, 0),)),
        (15, ((PAR, 0, 1, 1), (PAR, 1, 1, 1),)),
        (17, ((PAR, 0, 3, 1), (PAR, 1, 3, 1),)),
        (18, ((PAR, 0, 2, 0), (PAR, 1, 2, 0),)),
        (19, ((PAR, 0, 2, 1),)),
        (20, ((PAR, 1, 2, 1),)),
    ),
    (
        (2, ((CROSSF, 0), (CROSSF, 1), (OWN, 0, 1, 0), (OWN, 0, 3, 0), (PASS_Z, 0, 0), (PASS_Z, 0, 1),)),
        (3, ((OWN, 0, 1, 1), (OWN, 0, 3, 1),)),
        (4, ((OWN, 1, 0, 0), (PASS_Z, 1, 0), (PASS_Z, 3, 0),)),
        (5, ((OWN, 0, 2, 0),)),
        (6, ((OWN, 0, 2, 1), (OWN, 1, 0, 1), (FWD_Y, 0, 0), (FWD_Y, 0, 1),)),
        (7, ((OWN, 1, 1, 0),)),
        (8, ((OWN, 1, 3, 0), (PASS_Z, 1, 1), (PASS_Z, 3, 1),)),
        (9, ((OWN, 1, 1, 1), (PAR, 0, 0, 0), (PAR, 1, 0, 0),)),
        (10, ((OWN, 1, 3, 1), (FWD_Y, 1, 0), (FWD_Y, 3, 0), (PAR, 1, 0, 1), (PAR, 0, 0, 1),)),
        (11, ((OWN, 1, 2, 0), (OWN, 1, 2, 1), (PASS_Z, 2, 0), (PASS_Z, 2, 1), (PAR, 0, 1, 0),)),
        (12, ((FWD_Y, 1, 1), (FWD_Y, 3, 1), (PAR, 1, 1, 0),)),
        (13, ((PAR, 0, 3, 0),)),
        (14, ((FWD_Y, 2, 0), (FWD_Y, 2, 1), (PAR, 1, 3, 0),)),
        (15, ((PAR, 0, 1, 1), (PAR, 1, 1, 1),)),
        (17, ((PAR, 0, 3, 1), (PAR, 1, 3, 1),)),
        (18, ((PAR, 0, 2, 0), (PAR, 1, 2, 0),)),
        (19, ((PAR, 0, 2, 1),)),
        (20, ((PAR, 1, 2, 1),)),
    ),
    (
        (2, ((CROSSF, 0), (CROSSF, 1), (OWN, 0, 1, 0), (OWN, 0, 3, 0), (FWD_Y, 0, 0), (PAR, 0, 0, 0),)),
        (3, ((OWN, 0, 1, 1), (OWN, 0, 3, 1), (FWD_Y, 0, 1), (PAR, 0, 0, 1),)),
        (4, ((OWN, 1, 0, 0), (OWN, 1, 0, 1),)),
        (5, ((OWN, 0, 2, 0), (FWD_Y, 1, 0), (PAR, 0, 1, 0),)),
        (6, ((OWN, 0, 2, 1), (PASS_Y, 0, 0), (PASS_Y, 0, 1),)),
        (7, ((FWD_Y, 3, 0), (PAR, 0, 3, 0),)),
        (8, ((OWN, 1, 3, 0), (PASS_Y, 1, 0),)),
        (9, ((FWD_Y, 1, 1), (PAR, 0, 1, 1), (PAR, 1, 0, 0),)),
        (10, ((OWN, 1, 3, 1), (PAR, 1, 0, 1),)),
        (11, ((OWN, 1, 1, 0), (FWD_Y, 3, 1), (PASS_Y, 3, 0), (PAR, 0, 3, 1),)),
        (12, ((OWN, 1, 2, 0), (OWN, 1, 2, 1), (PAR, 1, 1, 0),)),
        (13, ((FWD_Y, 2, 0), (PASS_Y, 1, 1), (PAR, 0, 2, 0),)),
        (14, ((OWN, 1, 1, 1), (FWD_Y, 2, 1), (PASS_Y, 3, 1), (PAR, 0, 2, 1), (PAR, 1, 3, 0),)),
        (15, ((PASS_Y, 2, 0),)),
        (16, ((PAR, 1, 1, 1),)),
        (17, ((PASS_Y, 2, 1), (PAR, 1, 3, 1),)),
        (18, ((PAR, 1, 2, 0),)),
        (20, ((PAR, 1, 2, 1),)),
    ),
    (
        (2, ((CROSSF, 0), (CROSSF, 1), (OWN, 0, 1, 0), (OWN, 0, 3, 0), (FWD_Y, 0, 0), (PAR, 0, 0, 0),)),
        (3, ((OWN, 0, 1, 1), (OWN, 0, 3, 1), (FWD_Y, 0, 1), (PAR, 0, 0, 1),)),
        (4, ((OWN, 1, 0, 0), (OWN, 1, 0, 1),)),
        (5, ((OWN, 0, 2, 0), (FWD_Y, 1, 0), (PAR, 0, 1, 0),)),
        (6, ((OWN, 0, 2, 1), (PASS_Y, 0, 0), (PASS_Y, 0, 1),)),
        (7, ((FWD_Y, 3, 0), (PAR, 0, 3, 0),)),
        (8, ((OWN, 1, 3, 0), (PASS_Y, 1, 0),)),
        (9, ((FWD_Y, 1, 1), (PAR, 0, 1, 1), (PAR, 1, 0, 0),)),
        (10, ((OWN, 1, 3, 1), (PAR, 1, 0, 1),)),
        (11, ((OWN, 1, 1, 0), (FWD_Y, 3, 1), (PASS_Y, 3, 0), (PAR, 0, 3, 1),)),
        (12, ((OWN, 1, 1, 1), (OWN, 1, 2, 0), (PAR, 1, 1, 0),)),
        (13, ((FWD_Y, 2, 0), (PASS_Y, 1, 1), (PAR, 0, 2, 0),)),
        (14, ((OWN, 1, 2, 1), (FWD_Y, 2, 1), (PASS_Y, 3, 1), (PAR, 0, 2, 1), (PAR, 1, 3, 0),)),
        (16, ((PASS_Y, 2, 0), (PAR, 1, 1, 1),)),
        (17, ((PAR, 1, 3, 1),)),
        (18, ((PASS_Y, 2, 1),)),
        (19, ((PAR, 1, 2, 0),)),
        (20, ((PAR, 1, 2, 1),)),
    ),
    (
        (2, ((CROSSF, 0), (CROSSF, 1), (OWN, 0, 1, 0), (OWN, 0, 3, 0), (FWD_Y, 0, 0), (PAR, 0, 0, 0),)),
        (3, ((OWN, 0, 1, 1), (OWN, 0, 3, 1), (FWD_Y, 0, 1), (PAR, 0, 0, 1),)),
        (4, ((OWN, 1, 0, 0), (OWN, 1, 0, 1),)),
        (5, ((OWN, 0, 2, 0), (FWD_Y, 1, 0), (PAR, 0, 1, 0),)),
        (6, ((OWN, 0, 2, 1), (PASS_Y, 0, 0), (PASS_Y, 0, 1),)),
        (7, ((OWN, 1, 1, 0), (FWD_Y, 3, 0), (PAR, 0, 3, 0),)),
        (8, ((OWN, 1, 3, 0), (PASS_Y, 1, 0),)),
        (9, ((OWN, 1, 1, 1), (FWD_Y, 1, 1), (PAR, 0, 1, 1), (PAR, 1, 0, 0),)),
        (10, ((OWN, 1, 3, 1), (PAR, 1, 0, 1),)),
        (11, ((OWN, 1, 2, 1), (FWD_Y, 3, 1), (PASS_Y, 3, 0), (PAR, 0, 3, 1),)),
        (12, ((OWN, 1, 2, 0), (PAR, 1, 1, 0),)),
        (13, ((FWD_Y, 2, 0), (PASS_Y, 1, 1), (PAR, 0, 2, 0),)),
        (14, ((FWD_Y, 2, 1), (PASS_Y, 3, 1), (PAR, 0, 2, 1), (PAR, 1, 3, 0),)),
        (16, ((PASS_Y, 2, 0), (PAR, 1, 1, 1),)),
        (17, ((PAR, 1, 3, 1),)),
        (18, ((PASS_Y, 2, 1),)),
        (19, ((PAR, 1, 2, 0),)),
        (20, ((PAR, 1, 2, 1),)),
    ),
    (
        (2, ((CROSSF, 0), (CROSSF, 1), (OWN, 0, 1, 0), (OWN, 0, 3, 0), (FWD_Y, 0, 0), (PAR, 0, 0, 0),)),
        (3, ((OWN, 0, 1, 1), (OWN, 0, 3, 1), (FWD_Y, 0, 1), (PAR, 0, 0, 1),)),
        (4, ((OWN, 1, 0, 0), (OWN, 1, 0, 1),)),
        (5, ((OWN, 0, 2, 0), (FWD_Y, 1, 0), (PAR, 0, 1, 0),)),
        (6, ((OWN, 0, 2, 1), (PASS_Y, 0, 0), (PASS_Y, 0, 1),)),
        (7, ((OWN, 1, 1, 0), (FWD_Y, 3, 0), (PAR, 0, 3, 0),)),
        (8, ((OWN, 1, 3, 0), (PASS_Y, 1, 0),)),
        (9, ((OWN, 1, 1, 1), (FWD_Y, 1, 1), (PAR, 0, 1, 1), (PAR, 1, 0, 0),)),
        (10, ((OWN, 1, 3, 1), (PAR, 1, 0, 1),)),
        (11, ((OWN, 1, 2, 1), (FWD_Y, 3, 1), (PASS_Y, 3, 0), (PAR, 0, 3, 1),)),
        (12, ((OWN, 1, 2, 0), (PAR, 1, 1, 0),)),
        (13, ((FWD_Y, 2, 0), (PASS_Y, 1, 1), (PAR, 0, 2, 0),)),
        (14, ((FWD_Y, 2, 1), (PASS_Y, 3, 1), (PAR, 0, 2, 1), (PAR, 1, 3, 0),)),
        (16, ((PASS_Y, 2, 0), (PAR, 1, 1, 1),)),
        (17, ((PAR, 1, 3, 1),)),
        (18, ((PASS_Y, 2, 1),)),
        (19, ((PAR, 1, 2, 0),)),
        (20, ((PAR, 1, 2, 1),)),
    ),
    (
        (2, ((CROSSF, 0), (CROSSF, 1), (OWN, 0, 1, 0), (OWN, 0, 3, 0), (FWD_Y, 0, 0),)),
        (3, ((OWN, 0, 1, 1), (OWN, 0, 3, 1), (FWD_Y, 0, 1),)),
        (4, ((OWN, 1, 0, 0), (OWN, 1, 0, 1),)),
        (5, ((OWN, 0, 2, 0), (FWD_Y, 1, 0),)),
        (6, ((OWN, 0, 2, 1), (PAR, 0, 0, 0), (PAR, 1, 0, 0),)),
        (7, ((OWN, 1, 1, 0), (FWD_Y, 3, 0),)),
        (8, ((OWN, 1, 3, 0), (PAR, 0, 0, 1), (PAR, 1, 0, 1),)),
        (9, ((OWN, 1, 1, 1), (FWD_Y, 1, 1),)),
        (10, ((OWN, 1, 3, 1), (PAR, 0, 1, 0), (PAR, 1, 1, 0),)),
        (11, ((FWD_Y, 3, 1),)),
        (12, ((PAR, 0, 3, 0), (PAR, 1, 3, 0),)),
        (13, ((FWD_Y, 2, 0),)),
        (14, ((OWN, 1, 2, 0), (FWD_Y, 2, 1), (PAR, 0, 1, 1), (PAR, 1, 1, 1),)),
        (15, ((PAR, 0, 3, 1), (PAR, 1, 3, 1),)),
        (17, ((OWN, 1, 2, 1), (PAR, 0, 2, 0), (PAR, 1, 2, 0),)),
        (18, ((PAR, 0, 2, 1), (PAR, 1, 2, 1),)),
    ),
    (
        (2, ((CROSSF, 0), (CROSSF, 1), (OWN, 0, 1, 0), (OWN, 0, 3, 0), (FWD_Y, 0, 0),)),
        (3, ((OWN, 0, 1, 1), (OWN, 0, 3, 1), (FWD_Y, 0, 1),)),
        (4, ((OWN, 1, 0, 0), (OWN, 1, 0, 1),)),
        (5, ((OWN, 0, 2, 0), (FWD_Y, 1, 0),)),
        (6, ((OWN, 0, 2, 1), (PAR, 0, 0, 0), (PAR, 1, 0, 0),)),
        (7, ((OWN, 1, 1, 0), (FWD_Y, 3, 0),)),
        (8, ((OWN, 1, 3, 0), (PAR, 0, 0, 1), (PAR, 1, 0, 1),)),
        (9, ((OWN, 1, 1, 1), (FWD_Y, 1, 1),)),
        (10, ((OWN, 1, 3, 1), (PAR, 0, 1, 0), (PAR, 1, 1, 0),)),
        (11, ((FWD_Y, 3, 1),)),
        (12, ((PAR, 0, 3, 0), (PAR, 1, 3, 0),)),
        (13, ((FWD_Y, 2, 0),)),
        (14, ((OWN, 1, 2, 0), (FWD_Y, 2, 1), (PAR, 0, 1, 1), (PAR, 1, 1, 1),)),
        (15, ((OWN, 1, 2, 1), (PAR, 0, 3, 1), (PAR, 1, 3, 1),)),
        (17, ((PAR, 0, 2, 0), (PAR, 1, 2, 0),)),
        (18, ((PAR, 0, 2, 1), (PAR, 1, 2, 1),)),
    ),
    (
        (2, ((CROSSF, 0), (CROSSF, 1), (OWN, 0, 1, 0), (OWN, 0, 3, 0), (FWD_Y, 0, 0),)),
        (3, ((OWN, 0, 1, 1), (OWN, 0, 3, 1), (FWD_Y, 0, 1),)),
        (4, ((OWN, 1, 0, 0), (OWN, 1, 0, 1),)),
        (5, ((OWN, 0, 2, 0), (FWD_Y, 1, 0),)),
        (6, ((OWN, 0, 2, 1), (PAR, 0, 0, 0), (PAR, 1, 0, 0),)),
        (7, ((OWN, 1, 1, 0), (FWD_Y, 3, 0),)),
        (8, ((OWN, 1, 3, 0), (PAR, 0, 0, 1), (PAR, 1, 0, 1),)),
        (9, ((OWN, 1, 1, 1), (FWD_Y, 1, 1),)),
        (10, ((OWN, 1, 3, 1), (PAR, 0, 1, 0), (PAR, 1, 1, 0),)),
        (11, ((OWN, 1, 2, 1), (FWD_Y, 3, 1),)),
        (12, ((OWN, 1, 2, 0), (PAR, 0, 3, 0), (PAR, 1, 3, 0),)),
        (13, ((FWD_Y, 2, 0),)),
        (14, ((FWD_Y, 2, 1), (PAR, 0, 1, 1), (PAR, 1, 1, 1),)),
        (15, ((PAR, 0, 3, 1), (PAR, 1, 3, 1),)),
        (17, ((PAR, 0, 2, 0), (PAR, 1, 2, 0),)),
        (18, ((PAR, 0, 2, 1), (PAR, 1, 2, 1),)),
    ),
    (
        (2, ((CROSSF, 0), (CROSSF, 1), (OWN, 0, 1, 0), (OWN, 0, 3, 0), (FWD_Y, 0, 0),)),
        (3, ((OWN, 0, 1, 1), (OWN, 0, 3, 1), (FWD_Y, 0, 1),)),
        (4, ((OWN, 1, 0, 0), (OWN, 1, 0, 1),)),
        (5, ((OWN, 0, 2, 0), (FWD_Y, 1, 0),)),
        (6, ((OWN, 0, 2, 1), (PAR, 0, 0, 0), (PAR, 1, 0, 0),)),
        (7, ((OWN, 1, 1, 0), (FWD_Y, 3, 0),)),
        (8, ((OWN, 1, 3, 0), (PAR, 0, 0, 1), (PAR, 1, 0, 1),)),
        (9, ((OWN, 1, 1, 1), (FWD_Y, 1, 1),)),
        (10, ((OWN, 1, 3, 1), (PAR, 0, 1, 0), (PAR, 1, 1, 0),)),
        (11, ((OWN, 1, 2, 1), (FWD_Y, 3, 1),)),
        (12, ((OWN, 1, 2, 0), (PAR, 0, 3, 0), (PAR, 1, 3, 0),)),
        (13, ((FWD_Y, 2, 0),)),
        (14, ((FWD_Y, 2, 1), (PAR, 0, 1, 1), (PAR, 1, 1, 1),)),
        (15, ((PAR, 0, 3, 1), (PAR, 1, 3, 1),)),
        (17, ((PAR, 0, 2, 0), (PAR, 1, 2, 0),)),
        (18, ((PAR, 0, 2, 1), (PAR, 1, 2, 1),)),
    ),
)

STAGES = len(SEQUENCE)
BASES = [sum(PARTS[stage] for stage in SEQUENCE[:n]) for n in range(STAGES + 1)]
POINTS = BASES[-1] + 1
PAR_AT, T1_AT, T2_AT, T3_AT, TC_AT, SLOTS = 32, 64, 72, 80, 88, 90
WAYS = ("x+", "x-", "y+", "y-", "z+", "z-", "core", "ya", "yb", "za", "zb")
WAIT = 15
CLASSES = [(x, y) for x in range(4) for y in range(4)]


def sign_of(j, k):
    return "+" if (k + (0, 1, 1, 0)[j]) % 2 == 0 else "-"


def name_of(x, y, row, j):
    return (y // 2 + row) % 2 * 4 + (x + 4 - j) % 4


def row_behind(y, sign):
    return (y + 3) % 4 // 2 if sign == "+" else (y + 1) % 4 // 2


def feed(x, y, j, k, src):
    up = y // 2 == 1
    final, via1, via2 = ("par", name_of(x, y, 0, j), k), ("t1", j, k), ("t2", j, k)
    sends = []
    if x in (0, 1):
        sends.append((src, via1, "z" + sign_of(j, k)))
    if x == 1:
        sends.append((src, final, "ya"))
    if x in (2, 3):
        sends.append((src, final if x == 2 and not up else via1, "za"))
        sends.append((src, final if x == 2 and up else via2, "zb"))
    return sends


def expand(x, y, event):
    kind, args = event[0], event[1:]
    up = y // 2 == 1
    ops = []
    if kind == CROSSF:
        (k,) = args
        sign = "+-"[k]
        ops = [("tc", k), (("tc", k), ("own", row_behind(y, sign) * 4 + x, k), "y" + sign)]
    if kind == OWN:
        row, j, k = args
        here = ("own", name_of(x, y, row, j), k)
        ops = [here]
        if (row, j) == (1, 0) or (j == 1 and (k + row) % 2 == 0):
            ops.append((here, here, "x+"))
        if (row, j) == (1, 0) or (j == 3 and (k + row) % 2 == 1):
            ops.append((here, here, "x-"))
        if row == 0:
            ops += feed(x, y, j, k, here)
        ops.append((here, here, "core"))
    if kind == PASS_Z:
        j, k = args
        here = ("t1", j, k)
        there = ("par", name_of(x, y, 0, j), k) if x == 0 and up else ("t2", j, k)
        ops = [here, (here, there, "z" + sign_of(j, k))]
    if kind == FWD_Y:
        j, k = args
        final, there, way = ("par", name_of(x, y, 0, j), k), ("t3", j, k), "y" + sign_of(j, k)
        if x == 3 or (x == 2 and up):
            ops += [("t1", j, k), (("t1", j, k), final, "ya") if x == 3 else (("t1", j, k), there, way)]
        if x in (1, 3) or not up:
            ops += [("t2", j, k), (("t2", j, k), final, "yb") if x in (1, 3) else (("t2", j, k), there, way)]
    if kind == PASS_Y:
        j, k = args
        sign = sign_of(j, k)
        row = row_behind(y, sign)
        if x == 2 or row == 0:
            ops = [("t3", j, k), (("t3", j, k), ("par", row * 4 + (x + 4 - j) % 4, k), "y" + sign)]
    if kind == PAR:
        row, j, k = args
        here = ("par", name_of(x, y, row, j), k)
        ops = [here, (here, here, "core")]
    return ops


def slot(place, c):
    kind, rest = place[0], place[1:]
    if kind in ("own", "par"):
        q, k = rest
        return (PAR_AT if kind == "par" else 0) + q * 4 + c * 2 + k
    if kind == "tc":
        return TC_AT + rest[0]
    return {"t1": T1_AT, "t2": T2_AT, "t3": T3_AT}[kind] + rest[0] * 2 + rest[1]


def tables(x, y):
    per_core = []
    for c in range(2):
        ops, begins, sends, at = [], [], 0, dict(EVENTS[CLASSES.index((x, y))])
        for point in range(POINTS):
            begins.append(len(ops))
            for event in at.get(point, ()):
                for op in expand(x, y, event):
                    if isinstance(op[0], str):
                        ops.append(slot(op, c) + 2097152 * WAIT)
                    else:
                        src, dst, way = op
                        ops.append(slot(src, c) + 128 * slot(dst, c) + 16384 * sends + 2097152 * WAYS.index(way))
                        sends += 1
        per_core.append((ops, begins + [len(ops)], sends))
    return per_core


TABLES = {cls: tables(*cls) for cls in CLASSES}
MOST_OPS = max(len(ops) for cores in TABLES.values() for ops, _, _ in cores)
MOST_SENDS = max(sends for cores in TABLES.values() for _, _, sends in cores)
FIRST_SENDS = 12


def columns(t):
    first, last = t * 256, (t + 1) * 256
    cuts = [first] + [cut for cut in range(0, NI * V, V) if first < cut < last] + [last]
    return [(u - first, w - first, u // V, u % V) for u, w in zip(cuts, cuts[1:])]


def kernel(dims, mine, amps, out, out_own, out_par, buf, rc, half, acc, ops, begins, devs,
           ssem, first_sem, rsem, local_sem):
    sym, tile, c = lax.axis_index("sym"), lax.axis_index("tile"), lax.axis_index("occ")
    x, yhi = sym % 4, sym // 4
    x0, x1 = x % 2, x // 2
    z, ylo = tile // 2, tile % 2
    z0, z1 = z % 2, z // 2
    y = 2 * yhi + ylo
    none = sym == 0

    def dev(dx=0, dy=0, dz=0, dc=0):
        xx, yy, zz = (x + 4 + dx) % 4, (y + 4 + dy) % 4, (z + 4 + dz) % 4
        return ((yy // 2) * 4 + xx) * 16 + (zz * 2 + yy % 2) * 2 + (c + dc) % 2

    step_a = 1 - 2 * (yhi + ylo - 2 * yhi * ylo)
    step_z = 1 - 2 * z0
    to = {
        "x+": dev(dx=1), "x-": dev(dx=-1), "y+": dev(dy=1), "y-": dev(dy=-1), "z+": dev(dz=1), "z-": dev(dz=-1),
        "core": dev(dc=1), "ya": dev(dy=step_a), "yb": dev(dy=-step_a), "za": dev(dz=step_z), "zb": dev(dz=-step_z),
    }
    barrier = pltpu.get_barrier_semaphore()
    for way in WAYS[:7]:
        pl.semaphore_signal(barrier, inc=1, device_id=to[way], device_id_type=pl.DeviceIdType.LOGICAL)

    def own_slot(q, core, k):
        return q * 4 + core * 2 + k

    keep = []
    for k in range(PIECES):
        keep.append(pltpu.make_async_copy(mine.at[pl.ds(k * PV, PV)], buf.at[own_slot(sym, c, k)], local_sem.at[8 + k]))
        keep[-1].start()
    loads = [pltpu.make_async_copy(amps.at[i], rc.at[:, pl.ds(i * V, V)], local_sem.at[i]) for i in range(NI)]
    for load in loads:
        load.start()

    pl.semaphore_wait(barrier, 7)

    def remote(src, dst_slot, sem, where):
        return pltpu.make_async_remote_copy(
            src, buf.at[dst_slot], sem, rsem.at[dst_slot], device_id=where, device_id_type=pl.DeviceIdType.LOGICAL
        )

    def arrived(at):
        remote(buf.at[at], at, first_sem.at[0], to["core"]).wait_recv()

    firsts = []

    def first(src, place, where, cond=None):
        index = len(firsts)
        if cond is None:
            remote(src, place, first_sem.at[index], where).start()
        else:
            pl.when(cond)(lambda: remote(src, place, first_sem.at[index], where).start())
        firsts.append((src, place, cond, index))

    step_2 = {k: {"+": to["z+"], "-": to["z-"]}[sign_of(0, k)] for k in range(PIECES)}
    for k in range(PIECES):
        src = mine.at[pl.ds(k * PV, PV)]
        home = own_slot(sym, c, k)
        final, via1, via2 = PAR_AT + home, T1_AT + k, T2_AT + k
        first(src, home, to["core"])
        first(src, home, to["x+"])
        first(src, home, to["x-"])
        first(src, TC_AT + k, to["y" + "+-"[k]])
        direct_b, direct_a = x0 + 2 * (1 - x1) + (1 - yhi) == 0, x0 + 2 * (1 - x1) + yhi == 0
        where_b = x1 * to["zb"] + (1 - x1) * step_2[k]
        place_b = jnp.where(direct_b, final, x1 * via2 + (1 - x1) * via1)
        first(src, place_b, where_b)
        where_a = x1 * to["za"] + (1 - x1) * to["ya"]
        place_a = jnp.where(direct_a | (x1 == 0), final, via1)
        first(src, place_a, where_a, x > 0)

    for (at_x, at_y), cores in TABLES.items():
        @pl.when((x == at_x) & (y == at_y))
        def _():
            (ops0, begins0, _), (ops1, _, _) = cores
            for n, (op0, op1) in enumerate(zip(ops0, ops1)):
                ops[n] = op0 + (op1 - op0) * c if op0 != op1 else op0
            for n, begin in enumerate(begins0):
                begins[n] = begin
    for n, way in enumerate(WAYS):
        devs[n] = to[way]

    n_row = dims[tile]
    n_col = dims[(z1 + yhi - 2 * z1 * yhi) * 4 + (z0 + x1 - 2 * z0 * x1) * 2 + (ylo + x0 - 2 * ylo * x0)]
    live_r = jnp.where(lax.broadcasted_iota(jnp.int32, (V, V), 0) < n_row, 1.0, 0.0)
    live = jnp.where(lax.broadcasted_iota(jnp.int32, (V, V), 1) < n_col, live_r, 0.0).astype(jnp.bfloat16)
    acc[...] = jnp.zeros_like(acc)
    for load in loads:
        load.wait()
    for i in range(NI):
        rc[:, i * V:(i + 1) * V] = rc[:, i * V:(i + 1) * V] * live
    for copy in keep:
        copy.wait()

    def decoded(n):
        op = ops[n]
        src, rest = lax.rem(op, 128), lax.div(op, 128)
        dst, rest = lax.rem(rest, 128), lax.div(rest, 128)
        return src, dst, lax.rem(rest, 128), lax.div(rest, 128)

    def events(point):
        @pl.loop(begins[point], begins[point + 1])
        def _(n):
            src, dst, index, way = decoded(n)

            @pl.when(way == WAIT)
            def _():
                arrived(src)

            @pl.when(way != WAIT)
            def _():
                remote(buf.at[src], dst, ssem.at[index], devs[way]).start()

    digit = (1 + 15 * x0) * (1 + 255 * x1)

    def chosen(groups, n):
        code = 0
        for number, names in enumerate(groups):
            of_y = [0] * 4
            for (at_x, at_y), (row, j, k) in zip(CLASSES, names):
                of_y[at_y] += (row * 8 + j * 2 + k) * 16 ** at_x
            value = of_y[0]
            if len(set(of_y)) > 1:
                value = value + (of_y[1] - of_y[0]) * ylo + (of_y[2] - of_y[0]) * yhi
                value = value + (of_y[3] - of_y[2] - of_y[1] + of_y[0]) * (yhi * ylo)
            code = code + (n == number) * 1 * value
        code = lax.rem(lax.div(code, digit), 16)
        return (yhi + code // 8) % 2 * 4 + (x + 4 - code // 2 % 4) % 4, code % 2

    def base_of(n):
        return sum((n == number) * base for number, base in enumerate(BASES[:-1]) if base)

    par_base = PAR_AT * (1 - (sym == 0) * 1)

    def unit(base, q, core):
        at = base + q * 4 + core * 2
        return buf[pl.ds(at, 2)].reshape(V, V)

    def first_stage(base, halves):
        for q, k in halves:
            arrived(own_slot(q, 1 - c, k))
        for h in range(PARTS[1]):
            if h:
                events(base + h)
            for t in range(h * 12 // PARTS[1], (h + 1) * 12 // PARTS[1]):
                left = jnp.concatenate([buf[q * 4 + 2 * p + k] for q, k in halves for p in range(2)], axis=0)
                r = jnp.dot(left, rc[:, t * 256:(t + 1) * 256], preferred_element_type=jnp.float32).astype(jnp.bfloat16)
                for lo_col, hi_col, pair, at in columns(t):
                    for number, (q, k) in enumerate(halves):
                        rows = pl.ds(pl.multiple_of(pair * V + k * PV, PV), PV)
                        for p in range(2):
                            lanes = pl.ds(p * V + at, hi_col - lo_col)
                            first = (2 * number + p) * PV
                            half[q, rows, lanes] = r[first:first + PV, lo_col:hi_col]

    def second_stage(base, q):
        @pl.when(jnp.logical_not(none))
        def _():
            for k in range(PIECES):
                arrived(PAR_AT + own_slot(q, 1 - c, k))

        for h in range(2):
            if h and PARTS[2] > 1:
                events(base + h)
            rows = pl.ds(h * HALF, HALF)
            for b0, b1 in ((0, 256), (256, 384)):
                right = jnp.concatenate([unit(par_base, q, p)[b0:b1] for p in range(2)], axis=1)
                acc[rows, b0:b1] += lax.dot_general(
                    half[q, rows, :], right, (((1,), (1,)), ((), ())), preferred_element_type=jnp.float32
                )

    @pl.loop(0, STAGES)
    def _(n):
        second = sum((n == k) * 1 for k, stage in enumerate(SEQUENCE) if stage == 2)
        halves = [chosen(group, n) for group in UNITS]
        base = base_of(n)
        events(base)
        pl.when(second == 0)(lambda: first_stage(base, halves))
        pl.when(second == 1)(lambda: second_stage(base, halves[0][0]))

    for h in range(2):
        rows = pl.ds(h * HALF, HALF)
        pltpu.make_async_copy(acc.at[rows], out.at[rows], local_sem.at[h]).start()
    events(POINTS - 1)

    leaving = []
    for r in range(len(REST)):
        q, _ = chosen(REST, jnp.int32(r))
        for k in range(PIECES):
            arrived(own_slot(q, 1 - c, k))

        @pl.when(jnp.logical_not(none))
        def _():
            for k in range(PIECES):
                arrived(PAR_AT + own_slot(q, 1 - c, k))

        par_at = par_base + q * 4
        for source, target, sem in ((q * 4, out_own.at[r], 18 + 2 * r), (par_at, out_par.at[r], 19 + 2 * r)):
            leaving.append(pltpu.make_async_copy(buf.at[pl.ds(source, 4)], target, local_sem.at[sem - 8]))
            leaving[-1].start()

    for src, place, cond, index in firsts:
        def sent(src=src, place=place, index=index):
            remote(src, place, first_sem.at[index], to["core"]).wait_send()

        if cond is None:
            sent()
        else:
            pl.when(cond)(sent)

    @pl.loop(0, begins[POINTS])
    def _(n):
        src, dst, index, way = decoded(n)

        @pl.when(way != WAIT)
        def _():
            remote(buf.at[src], dst, ssem.at[index], devs[way]).wait_send()

    for h in range(2):
        rows = pl.ds(h * HALF, HALF)
        pltpu.make_async_copy(acc.at[rows], out.at[rows], local_sem.at[h]).wait()
    for copy in leaving:
        copy.wait()


ALL = [(row, j) for j in (0, 1, 3, 2) for row in range(2)]


def left_over():
    by_class = []
    for at in range(len(CLASSES)):
        done = [names[at][:2] for group in UNITS for stage, names in zip(SEQUENCE, group) if stage == 1]
        by_class.append([name + (0,) for name in ALL if name not in done])
    return tuple(zip(*by_class))


REST = left_over()


def rest_kernel(dims, own_hbm, par_hbm, amps, raw, out, own, par, rc, half, acc, sems):
    sym, tile = lax.axis_index("sym"), lax.axis_index("tile")
    n, hi = len(REST), NI // 2
    get_own = pltpu.make_async_copy(own_hbm, own, sems.at[0])
    get_par = pltpu.make_async_copy(par_hbm, par, sems.at[1])
    get_amps = [pltpu.make_async_copy(amps.at[i], rc.at[:, pl.ds(i * V, V)], sems.at[2 + i]) for i in range(NI)]
    get_raw = [
        pltpu.make_async_copy(raw.at[pl.ds(h * HALF, HALF)], acc.at[pl.ds(h * HALF, HALF)], sems.at[2 + NI + h])
        for h in range(2)
    ]
    for copy in get_amps[:hi] + [get_own, get_par, get_raw[0]] + get_amps[hi:] + [get_raw[1]]:
        copy.start()
    n_row, n_col = dims[tile], dims[jnp.bitwise_xor(tile, sym)]
    live = (lax.broadcasted_iota(jnp.int32, (V, V), 0) < n_row) & (lax.broadcasted_iota(jnp.int32, (V, V), 1) < n_col)
    live_b = jnp.where(live, 1.0, 0.0).astype(jnp.bfloat16)
    puts = []
    for h in range(2):
        for i in range(h * hi, (h + 1) * hi):
            get_amps[i].wait()
            rc[:, i * V:(i + 1) * V] = rc[:, i * V:(i + 1) * V] * live_b
        if h == 0:
            get_own.wait()
        for t in range(6 * h, 6 * (h + 1)):
            left = own[...].reshape(n * 2 * V, V)
            r = jnp.dot(left, rc[:, t * 256:(t + 1) * 256], preferred_element_type=jnp.float32).astype(jnp.bfloat16)
            for lo_col, hi_col, pair, at in columns(t):
                for p in range(2 * n):
                    lanes = pl.ds(p * V + at, hi_col - lo_col)
                    half[(pair - h * hi) * V:(pair - h * hi + 1) * V, lanes] = r[p * V:(p + 1) * V, lo_col:hi_col]
        if h == 0:
            get_par.wait()
        get_raw[h].wait()
        rows = pl.ds(h * HALF, HALF)
        for b0, b1 in ((0, 256), (256, 384)):
            right = [par[r, pl.ds(2 * p, 2)].reshape(V, V)[b0:b1] for r in range(n) for p in range(2)]
            right = jnp.concatenate(right, axis=1)
            r = lax.dot_general(half[...], right, (((1,), (1,)), ((), ())), preferred_element_type=jnp.float32)
            r = r + acc[rows, b0:b1]
            for i in range(hi):
                at = pl.ds((h * hi + i) * V, V)
                acc[at, b0:b1] = jnp.where(live[:, b0:b1], r[i * V:(i + 1) * V], 0.0)
            lanes = pl.ds(b0, b1 - b0)
            puts.append(pltpu.make_async_copy(acc.at[rows, lanes], out.at[rows, lanes], sems.at[4 + NI + len(puts)]))
            puts[-1].start()
    for copy in puts:
        copy.wait()


def shards(irrep_dims, chol_vectors, amplitudes):
    bf, sem = jnp.bfloat16, pltpu.SemaphoreType.DMA
    n = len(REST)
    own, chol, amps = (n, 4, PV, V), chol_vectors.reshape(V, V), amplitudes.reshape(NI, V, V)
    anywhere = pl.BlockSpec(memory_space=pl.ANY)
    raw, rest_own, rest_par = pl.pallas_call(
        kernel,
        out_shape=[
            jax.ShapeDtypeStruct((NI * V, V), jnp.float32),
            jax.ShapeDtypeStruct(own, bf),
            jax.ShapeDtypeStruct(own, bf),
        ],
        in_specs=[pl.BlockSpec(memory_space=pltpu.SMEM), anywhere, anywhere],
        out_specs=[anywhere] * 3,
        scratch_shapes=[
            pltpu.VMEM((SLOTS, PV, V), bf),
            pltpu.VMEM((V, NI * V), bf),
            pltpu.VMEM((8, NI * V, 2 * V), bf),
            pltpu.VMEM((NI * V, V), jnp.float32),
            pltpu.SMEM((MOST_OPS,), jnp.int32),
            pltpu.SMEM((POINTS + 1,), jnp.int32),
            pltpu.SMEM((len(WAYS),), jnp.int32),
            sem((MOST_SENDS,)), sem((FIRST_SENDS,)), sem((SLOTS,)), sem((10 + 2 * n,)),
        ],
        compiler_params=pltpu.CompilerParams(
            collective_id=0, has_side_effects=True, vmem_limit_bytes=63 * 1024 * 1024
        ),
        cost_estimate=pl.CostEstimate(flops=(8 - n) * 3_600_000_000, bytes_accessed=12_000_000, transcendentals=0),
        name="ladder",
    )(irrep_dims, chol, amps)
    total = pl.pallas_call(
        rest_kernel,
        out_shape=jax.ShapeDtypeStruct((NI * V, V), jnp.float32),
        in_specs=[pl.BlockSpec(memory_space=pltpu.SMEM)] + [anywhere] * 4,
        out_specs=anywhere,
        scratch_shapes=[
            pltpu.VMEM(own, bf),
            pltpu.VMEM(own, bf),
            pltpu.VMEM((V, NI * V), bf),
            pltpu.VMEM((HALF, n * 2 * V), bf),
            pltpu.VMEM((NI * V, V), jnp.float32),
            sem((8 + NI,)),
        ],
        compiler_params=pltpu.CompilerParams(vmem_limit_bytes=60 * 1024 * 1024),
        cost_estimate=pl.CostEstimate(flops=n * 3_600_000_000, bytes_accessed=16_000_000, transcendentals=0),
        name="rest",
    )(irrep_dims, rest_own, rest_par, amps, raw)
    return total.reshape(1, NI, V, V)


def solution(mesh):
    return jax.shard_map(
        shards,
        mesh=mesh,
        in_specs=(P(), P(("sym", "occ"), "tile", None), P("sym", "occ", "tile", None)),
        out_specs=P("sym", "occ", "tile", None),
        check_vma=False,
    )
```

time: 74.9 us -> 72.8 us (0.972)
  the two profiles are of different devices: /device:TPU:17 before, /device:TPU:3 now
where the time goes in v1:
time: 72.8 us; the launch traced here: 71.7 us
  Pallas kernels  71.5 us (98%)
    pallas_call x1, Pallas kernels, shards(): pl.pallas_call(kernel, out_shape=[jax.ShapeDtypeStruct((NI * V, V), jnp.f...  62.1 us
    pallas_call x1, Pallas kernels, shards(): pl.pallas_call(rest_kernel, out_shape=jax.ShapeDtypeStruct((NI * V, V), j...  9.47 us

profile of v1, /device:TPU:3, one launch (start us, length us, event | category | flops | bytes accessed | tf_op | source)
XLA Modules:
  0.0 71.7 jit_solution(2422014048259589586)
XLA Ops:
  0.0 62.1 %ladder.1 = (f32[3072,384]{1,0:T(8,128)}, bf16[1,4,192,384]{3,2,1,0:T(8,128)(2,1)}, bf16[1,4,192,384]{3,2,1,0:T(8,128)(2,1)}) custom-call(s32[8]{0:T(128)} %dims.3, bf16[384,384]{1,0:T(8,128)(2,1)} %bitcast.5, bf16[8,384,384]{2,1,0:T(8,128)(2,1)} %bitcast.3), custom_call_target="tpu_custom_call" | custom-call | flops 25200001024 | bytes 12000000 | tf_op jit(solution)/shard_map/ladder/pallas_call | solution.py:766
  62.1 9.5 %rest.1 = f32[3072,384]{1,0:T(8,128)} custom-call(s32[8]{0:T(128)} %dims.3, bf16[1,4,192,384]{3,2,1,0:T(8,128)(2,1)} %get-tuple-element.8.own_hbm, bf16[1,4,192,384]{3,2,1,0:T(8,128)(2,1)} %get-tuple-element.9.par_hbm, bf16[8,384,384]{2,1,0:T(8,128)(2,1)} %bitcast.4, f32[3072,384]{1,0:T(8,128)} %get-tuple-element.10.raw), custom_call_target="tpu_custom_call" | custom-call | flops 3600000000 | bytes 16000000 | tf_op jit(solution)/shard_map/rest/pallas_call | solution.py:791

commit v2 on v1

v2 whole, which is shorter than its diff:
```python
import jax
import jax.numpy as jnp
from jax import lax
from jax.experimental import pallas as pl
from jax.experimental.pallas import tpu as pltpu
from jax.sharding import PartitionSpec as P

V = 384
NI = 8
PIECES = 2
PV = V // PIECES
HALF = NI * V // 2
CROSSF, OWN, PASS_Z, FWD_Y, PASS_Y, PAR = range(6)
PARTS = {1: 2, 2: 1, 3: 1}
SEQUENCE = (1, 1, 1, 1, 1, 1, 2, 2, 1, 2, 2, 2, 2, 2)
UNITS = (
    (
        ((0, 0, 0), (0, 0, 0), (0, 0, 0), (0, 0, 0), (0, 0, 0), (0, 0, 0), (0, 0, 0), (0, 0, 0), (0, 0, 0), (0, 0, 0), (0, 0, 0), (0, 0, 0), (0, 0, 0), (0, 0, 0), (0, 0, 0), (0, 0, 0)),
        ((0, 3, 0), (0, 3, 0), (0, 3, 0), (0, 3, 0), (0, 3, 0), (0, 3, 0), (0, 3, 0), (0, 3, 0), (0, 3, 0), (0, 3, 0), (0, 3, 0), (0, 3, 0), (0, 3, 0), (0, 3, 0), (0, 3, 0), (0, 3, 0)),
        ((0, 3, 1), (0, 3, 1), (0, 3, 1), (0, 3, 1), (0, 3, 1), (0, 3, 1), (0, 3, 1), (0, 3, 1), (0, 3, 1), (0, 3, 1), (0, 3, 1), (0, 3, 1), (0, 3, 1), (0, 3, 1), (0, 3, 1), (0, 3, 1)),
        ((1, 0, 0), (1, 0, 0), (1, 0, 0), (1, 0, 0), (0, 2, 0), (0, 2, 0), (1, 0, 0), (1, 0, 0), (1, 0, 0), (1, 0, 0), (1, 0, 0), (1, 0, 0), (1, 0, 0), (1, 0, 0), (1, 0, 0), (1, 0, 0)),
        ((0, 2, 0), (0, 2, 0), (0, 2, 0), (0, 2, 0), (1, 0, 0), (1, 0, 0), (0, 2, 0), (0, 2, 1), (0, 2, 0), (0, 2, 0), (0, 2, 0), (0, 2, 0), (0, 2, 1), (0, 2, 1), (0, 2, 1), (0, 2, 1)),
        ((1, 1, 1), (1, 1, 1), (1, 3, 0), (1, 3, 0), (1, 1, 1), (1, 1, 1), (1, 3, 0), (1, 3, 0), (1, 3, 0), (1, 3, 0), (1, 3, 0), (1, 3, 0), (1, 3, 0), (1, 3, 0), (1, 3, 0), (1, 3, 0)),
        ((0, 3, 0), (0, 3, 0), (0, 0, 0), (0, 0, 0), (0, 0, 0), (0, 0, 0), (1, 0, 0), (1, 0, 0), (0, 3, 0), (0, 3, 0), (0, 3, 0), (0, 3, 0), (1, 0, 0), (1, 0, 0), (1, 0, 0), (1, 0, 0)),
        ((1, 0, 0), (1, 0, 0), (0, 1, 0), (0, 1, 0), (1, 1, 0), (1, 1, 0), (0, 0, 0), (0, 0, 0), (1, 0, 0), (1, 0, 0), (1, 0, 0), (1, 0, 0), (0, 0, 0), (0, 0, 0), (0, 0, 0), (0, 0, 0)),
        ((1, 3, 1), (1, 3, 1), (1, 3, 1), (1, 3, 1), (1, 3, 1), (1, 3, 1), (1, 3, 1), (1, 3, 1), (1, 3, 1), (1, 3, 1), (1, 3, 1), (1, 3, 1), (1, 3, 1), (1, 3, 1), (1, 3, 1), (1, 3, 1)),
        ((0, 2, 0), (0, 2, 0), (0, 3, 0), (0, 3, 0), (0, 3, 0), (0, 3, 0), (0, 1, 0), (0, 1, 0), (0, 2, 0), (0, 2, 0), (0, 2, 0), (0, 2, 0), (0, 3, 0), (0, 3, 0), (0, 3, 0), (0, 3, 0)),
        ((1, 1, 0), (1, 1, 0), (1, 0, 0), (1, 0, 0), (1, 0, 0), (1, 0, 0), (1, 1, 0), (1, 1, 0), (1, 1, 0), (1, 1, 0), (1, 1, 0), (1, 1, 0), (1, 1, 0), (1, 1, 0), (1, 1, 0), (1, 1, 0)),
        ((1, 3, 0), (1, 3, 0), (0, 2, 0), (0, 2, 0), (0, 2, 0), (0, 2, 0), (0, 3, 0), (0, 3, 0), (1, 3, 0), (1, 3, 0), (1, 3, 0), (1, 3, 0), (0, 2, 0), (0, 2, 0), (0, 2, 0), (0, 2, 0)),
        ((0, 1, 0), (0, 1, 0), (1, 3, 0), (1, 1, 0), (1, 3, 0), (1, 3, 0), (1, 3, 0), (1, 3, 0), (0, 1, 0), (0, 1, 0), (0, 1, 0), (0, 1, 0), (1, 3, 0), (1, 3, 0), (1, 3, 0), (1, 3, 0)),
        ((0, 0, 0), (0, 0, 0), (1, 1, 0), (1, 3, 0), (0, 1, 0), (0, 1, 0), (0, 2, 0), (0, 2, 0), (0, 0, 0), (0, 0, 0), (0, 0, 0), (0, 0, 0), (0, 1, 0), (0, 1, 0), (0, 1, 0), (0, 1, 0)),
    ),
    (
        ((0, 0, 1), (0, 0, 1), (0, 0, 1), (0, 0, 1), (0, 0, 1), (0, 0, 1), (0, 0, 1), (0, 0, 1), (0, 0, 1), (0, 0, 1), (0, 0, 1), (0, 0, 1), (0, 0, 1), (0, 0, 1), (0, 0, 1), (0, 0, 1)),
        ((0, 1, 0), (0, 1, 0), (0, 1, 0), (0, 1, 0), (0, 1, 0), (0, 1, 0), (0, 1, 0), (0, 1, 0), (0, 1, 0), (0, 1, 0), (0, 1, 0), (0, 1, 0), (0, 1, 0), (0, 1, 0), (0, 1, 0), (0, 1, 0)),
        ((0, 1, 1), (0, 1, 1), (0, 1, 1), (0, 1, 1), (0, 1, 1), (0, 1, 1), (0, 1, 1), (0, 1, 1), (0, 1, 1), (0, 1, 1), (0, 1, 1), (0, 1, 1), (0, 1, 1), (0, 1, 1), (0, 1, 1), (0, 1, 1)),
        ((1, 0, 1), (1, 0, 1), (1, 0, 1), (1, 0, 1), (0, 2, 1), (0, 2, 1), (1, 0, 1), (0, 2, 0), (1, 0, 1), (1, 0, 1), (1, 0, 1), (1, 0, 1), (0, 2, 0), (0, 2, 0), (0, 2, 0), (0, 2, 0)),
        ((0, 2, 1), (0, 2, 1), (0, 2, 1), (0, 2, 1), (1, 1, 0), (1, 1, 0), (0, 2, 1), (1, 0, 1), (0, 2, 1), (0, 2, 1), (0, 2, 1), (0, 2, 1), (1, 0, 1), (1, 0, 1), (1, 0, 1), (1, 0, 1)),
        ((1, 1, 0), (1, 1, 0), (1, 1, 0), (1, 1, 0), (1, 3, 0), (1, 3, 0), (1, 1, 0), (1, 1, 0), (1, 1, 0), (1, 1, 0), (1, 1, 0), (1, 1, 0), (1, 1, 0), (1, 1, 0), (1, 1, 0), (1, 1, 0)),
        ((0, 3, 0), (0, 3, 0), (0, 0, 0), (0, 0, 0), (0, 0, 0), (0, 0, 0), (1, 0, 0), (1, 0, 0), (0, 3, 0), (0, 3, 0), (0, 3, 0), (0, 3, 0), (1, 0, 0), (1, 0, 0), (1, 0, 0), (1, 0, 0)),
        ((1, 0, 0), (1, 0, 0), (0, 1, 0), (0, 1, 0), (1, 1, 0), (1, 1, 0), (0, 0, 0), (0, 0, 0), (1, 0, 0), (1, 0, 0), (1, 0, 0), (1, 0, 0), (0, 0, 0), (0, 0, 0), (0, 0, 0), (0, 0, 0)),
        ((1, 3, 0), (1, 3, 0), (1, 1, 1), (1, 1, 1), (1, 0, 1), (1, 0, 1), (1, 1, 1), (1, 1, 1), (1, 1, 1), (1, 1, 1), (1, 1, 1), (1, 1, 1), (1, 1, 1), (1, 1, 1), (1, 1, 1), (1, 1, 1)),
        ((0, 2, 0), (0, 2, 0), (0, 3, 0), (0, 3, 0), (0, 3, 0), (0, 3, 0), (0, 1, 0), (0, 1, 0), (0, 2, 0), (0, 2, 0), (0, 2, 0), (0, 2, 0), (0, 3, 0), (0, 3, 0), (0, 3, 0), (0, 3, 0)),
        ((1, 1, 0), (1, 1, 0), (1, 0, 0), (1, 0, 0), (1, 0, 0), (1, 0, 0), (1, 1, 0), (1, 1, 0), (1, 1, 0), (1, 1, 0), (1, 1, 0), (1, 1, 0), (1, 1, 0), (1, 1, 0), (1, 1, 0), (1, 1, 0)),
        ((1, 3, 0), (1, 3, 0), (0, 2, 0), (0, 2, 0), (0, 2, 0), (0, 2, 0), (0, 3, 0), (0, 3, 0), (1, 3, 0), (1, 3, 0), (1, 3, 0), (1, 3, 0), (0, 2, 0), (0, 2, 0), (0, 2, 0), (0, 2, 0)),
        ((0, 1, 0), (0, 1, 0), (1, 3, 0), (1, 1, 0), (1, 3, 0), (1, 3, 0), (1, 3, 0), (1, 3, 0), (0, 1, 0), (0, 1, 0), (0, 1, 0), (0, 1, 0), (1, 3, 0), (1, 3, 0), (1, 3, 0), (1, 3, 0)),
        ((0, 0, 0), (0, 0, 0), (1, 1, 0), (1, 3, 0), (0, 1, 0), (0, 1, 0), (0, 2, 0), (0, 2, 0), (0, 0, 0), (0, 0, 0), (0, 0, 0), (0, 0, 0), (0, 1, 0), (0, 1, 0), (0, 1, 0), (0, 1, 0)),
    ),
)
EVENTS = (
    (
        (2, ((CROSSF, 0), (CROSSF, 1), (PASS_Z, 0, 1), (OWN, 0, 1, 0), (OWN, 0, 3, 0), (PASS_Z, 0, 0),)),
        (3, ((OWN, 0, 1, 1), (OWN, 0, 3, 1),)),
        (4, ((OWN, 1, 0, 0), (OWN, 1, 0, 1), (PASS_Z, 1, 0), (PASS_Z, 3, 0),)),
        (5, ((OWN, 0, 2, 0), (OWN, 0, 2, 1), (FWD_Y, 0, 0), (FWD_Y, 0, 1),)),
        (6, ((OWN, 1, 1, 0), (PASS_Z, 1, 1), (PASS_Z, 3, 1),)),
        (7, ((OWN, 1, 1, 1), (OWN, 1, 3, 0), (FWD_Y, 1, 0), (FWD_Y, 3, 0), (PASS_Y, 0, 1),)),
        (8, ((PASS_Z, 2, 0),)),
        (9, ((OWN, 1, 2, 0), (PASS_Z, 2, 1),)),
        (10, ((OWN, 1, 3, 1), (OWN, 1, 2, 1), (FWD_Y, 1, 1), (FWD_Y, 3, 1), (PASS_Y, 1, 0),)),
        (11, ((FWD_Y, 2, 0), (FWD_Y, 2, 1),)),
        (12, ((PASS_Y, 3, 1),)),
        (14, ((PASS_Y, 2, 0),)),
    ),
    (
        (2, ((CROSSF, 0), (CROSSF, 1), (PASS_Z, 0, 1), (OWN, 0, 1, 0), (OWN, 0, 3, 0), (PASS_Z, 0, 0),)),
        (3, ((OWN, 0, 1, 1), (OWN, 0, 3, 1),)),
        (4, ((OWN, 1, 0, 0), (OWN, 1, 0, 1), (PASS_Z, 1, 0), (PASS_Z, 3, 0),)),
        (5, ((OWN, 0, 2, 0), (OWN, 0, 2, 1), (FWD_Y, 0, 0), (FWD_Y, 0, 1),)),
        (6, ((OWN, 1, 1, 0), (PASS_Z, 1, 1), (PASS_Z, 3, 1),)),
        (7, ((OWN, 1, 1, 1), (OWN, 1, 3, 0), (FWD_Y, 1, 0), (FWD_Y, 3, 0), (PASS_Y, 0, 0),)),
        (8, ((PASS_Z, 2, 0),)),
        (9, ((OWN, 1, 2, 0), (PASS_Z, 2, 1),)),
        (10, ((OWN, 1, 3, 1), (OWN, 1, 2, 1), (FWD_Y, 1, 1), (FWD_Y, 3, 1), (PASS_Y, 3, 0),)),
        (11, ((FWD_Y, 2, 0), (FWD_Y, 2, 1),)),
        (12, ((PASS_Y, 1, 1),)),
        (14, ((PASS_Y, 2, 1),)),
    ),
    (
        (2, ((CROSSF, 0), (CROSSF, 1), (PASS_Z, 0, 1), (OWN, 0, 1, 0), (OWN, 0, 3, 0), (PASS_Z, 0, 0),)),
        (3, ((OWN, 0, 1, 1), (OWN, 0, 3, 1),)),
        (4, ((OWN, 1, 0, 0), (OWN, 1, 0, 1), (PASS_Z, 1, 0), (PASS_Z, 3, 0),)),
        (5, ((OWN, 0, 2, 0), (OWN, 0, 2, 1), (PAR, 0, 0, 0), (PAR, 0, 0, 1),)),
        (6, ((OWN, 1, 1, 0), (OWN, 1, 3, 0), (PASS_Z, 1, 1), (PASS_Z, 3, 1),)),
        (7, ((OWN, 1, 1, 1), (OWN, 1, 3, 1), (PASS_Y, 0, 0), (PAR, 0, 1, 0), (PAR, 0, 3, 0),)),
        (9, ((OWN, 1, 2, 0), (PASS_Z, 2, 0), (PASS_Z, 2, 1),)),
        (10, ((OWN, 1, 2, 1), (PASS_Y, 3, 0), (PAR, 0, 1, 1), (PAR, 0, 3, 1), (PAR, 1, 0, 1), (PAR, 1, 0, 0),)),
        (11, ((PAR, 0, 2, 0), (PAR, 0, 2, 1),)),
        (12, ((PASS_Y, 1, 1), (PAR, 1, 1, 0),)),
        (14, ((PAR, 1, 3, 0), (PAR, 1, 3, 1),)),
        (15, ((PASS_Y, 2, 1),)),
        (16, ((PAR, 1, 1, 1),)),
        (17, ((PAR, 1, 2, 0), (PAR, 1, 2, 1),)),
    ),
    (
        (2, ((CROSSF, 0), (CROSSF, 1), (PASS_Z, 0, 1), (OWN, 0, 1, 0), (OWN, 0, 3, 0), (PASS_Z, 0, 0),)),
        (3, ((OWN, 0, 1, 1), (OWN, 0, 3, 1),)),
        (4, ((OWN, 1, 0, 0), (OWN, 1, 0, 1), (PASS_Z, 1, 0), (PASS_Z, 3, 0),)),
        (5, ((OWN, 0, 2, 0), (OWN, 0, 2, 1), (PAR, 0, 0, 0), (PAR, 0, 0, 1),)),
        (6, ((OWN, 1, 1, 0), (OWN, 1, 3, 0), (PASS_Z, 1, 1), (PASS_Z, 3, 1),)),
        (7, ((OWN, 1, 1, 1), (OWN, 1, 3, 1), (PASS_Y, 0, 1), (PAR, 0, 1, 0), (PAR, 0, 3, 0),)),
        (9, ((OWN, 1, 2, 0), (PASS_Z, 2, 0), (PASS_Z, 2, 1),)),
        (10, ((OWN, 1, 2, 1), (PASS_Y, 1, 0), (PAR, 0, 1, 1), (PAR, 0, 3, 1), (PAR, 1, 0, 0), (PAR, 1, 0, 1),)),
        (11, ((PAR, 0, 2, 0), (PAR, 0, 2, 1),)),
        (12, ((PASS_Y, 3, 1), (PAR, 1, 3, 0),)),
        (14, ((PAR, 1, 1, 0), (PAR, 1, 1, 1),)),
        (15, ((PASS_Y, 2, 0),)),
        (16, ((PAR, 1, 3, 1),)),
        (17, ((PAR, 1, 2, 0), (PAR, 1, 2, 1),)),
    ),
    (
        (2, ((CROSSF, 0), (PASS_Z, 0, 1), (OWN, 0, 1, 0), (OWN, 0, 3, 0), (PASS_Z, 0, 0), (PAR, 0, 0, 0),)),
        (3, ((CROSSF, 1), (OWN, 0, 1, 1), (OWN, 0, 3, 1), (PAR, 1, 0, 0),)),
        (4, ((PASS_Z, 1, 0), (PASS_Z, 3, 0),)),
        (5, ((OWN, 0, 2, 0), (OWN, 0, 2, 1), (FWD_Y, 0, 0), (FWD_Y, 0, 1), (PAR, 0, 0, 1), (PAR, 1, 0, 1), (OWN, 1, 1, 0), (OWN, 1, 0, 0), (PAR, 0, 1, 0),)),
        (6, ((OWN, 1, 1, 1), (OWN, 1, 3, 0), (PASS_Z, 1, 1), (PASS_Z, 3, 1), (PAR, 0, 3, 0), (PAR, 1, 1, 0),)),
        (7, ((OWN, 1, 0, 1), (OWN, 1, 3, 1), (FWD_Y, 1, 0), (FWD_Y, 3, 0), (PAR, 1, 3, 0),)),
        (8, ((OWN, 1, 2, 0), (PASS_Z, 2, 0), (PASS_Z, 2, 1),)),
        (9, ((OWN, 1, 2, 1), (PAR, 0, 1, 1), (PAR, 1, 1, 1),)),
        (10, ((FWD_Y, 1, 1), (FWD_Y, 3, 1), (PAR, 0, 3, 1), (PAR, 1, 3, 1),)),
        (11, ((FWD_Y, 2, 0), (FWD_Y, 2, 1), (PAR, 0, 2, 0), (PAR, 1, 2, 0),)),
        (13, ((PAR, 0, 2, 1), (PAR, 1, 2, 1),)),
    ),
    (
        (2, ((CROSSF, 0), (PASS_Z, 0, 1), (OWN, 0, 1, 0), (OWN, 0, 3, 0), (PASS_Z, 0, 0), (PAR, 1, 0, 0),)),
        (3, ((CROSSF, 1), (OWN, 0, 1, 1), (OWN, 0, 3, 1), (PAR, 0, 0, 0),)),
        (4, ((PASS_Z, 1, 0), (PASS_Z, 3, 0),)),
        (5, ((OWN, 0, 2, 0), (OWN, 0, 2, 1), (FWD_Y, 0, 0), (FWD_Y, 0, 1), (PAR, 0, 0, 1), (PAR, 1, 0, 1), (OWN, 1, 1, 0), (OWN, 1, 0, 0), (PAR, 1, 1, 0),)),
        (6, ((OWN, 1, 1, 1), (OWN, 1, 3, 0), (PASS_Z, 1, 1), (PASS_Z, 3, 1), (PAR, 0, 1, 0), (PAR, 1, 3, 0),)),
        (7, ((OWN, 1, 0, 1), (OWN, 1, 3, 1), (FWD_Y, 1, 0), (FWD_Y, 3, 0), (PAR, 0, 3, 0),)),
        (8, ((OWN, 1, 2, 0), (PASS_Z, 2, 0), (PASS_Z, 2, 1),)),
        (9, ((OWN, 1, 2, 1), (PAR, 0, 1, 1), (PAR, 1, 1, 1),)),
        (10, ((FWD_Y, 1, 1), (FWD_Y, 3, 1), (PAR, 0, 3, 1), (PAR, 1, 3, 1),)),
        (11, ((FWD_Y, 2, 0), (FWD_Y, 2, 1), (PAR, 0, 2, 0), (PAR, 1, 2, 0),)),
        (13, ((PAR, 0, 2, 1), (PAR, 1, 2, 1),)),
    ),
    (
        (2, ((CROSSF, 0), (CROSSF, 1), (PASS_Z, 0, 1), (OWN, 0, 1, 0), (OWN, 0, 3, 0), (PASS_Z, 0, 0),)),
        (3, ((OWN, 0, 1, 1), (OWN, 0, 3, 1),)),
        (4, ((OWN, 1, 0, 0), (OWN, 1, 0, 1), (PASS_Z, 1, 0), (PASS_Z, 3, 0),)),
        (5, ((OWN, 0, 2, 0), (OWN, 0, 2, 1), (FWD_Y, 0, 0), (FWD_Y, 0, 1),)),
        (6, ((OWN, 1, 1, 0), (OWN, 1, 3, 0), (PASS_Z, 1, 1), (PASS_Z, 3, 1),)),
        (7, ((OWN, 1, 1, 1), (OWN, 1, 3, 1), (FWD_Y, 1, 0), (FWD_Y, 3, 0), (PAR, 0, 0, 0), (PAR, 1, 0, 0),)),
        (8, ((PAR, 0, 0, 1), (PAR, 1, 0, 1),)),
        (9, ((OWN, 1, 2, 0), (PASS_Z, 2, 0), (PASS_Z, 2, 1),)),
        (10, ((OWN, 1, 2, 1), (FWD_Y, 1, 1), (FWD_Y, 3, 1), (PAR, 0, 1, 0), (PAR, 1, 1, 0),)),
        (11, ((FWD_Y, 2, 0), (FWD_Y, 2, 1), (PAR, 0, 3, 0), (PAR, 1, 3, 0),)),
        (12, ((PAR, 0, 1, 1),)),
        (13, ((PAR, 1, 1, 1),)),
        (14, ((PAR, 0, 3, 1), (PAR, 1, 3, 1),)),
        (15, ((PAR, 0, 2, 0),)),
        (16, ((PAR, 0, 2, 1), (PAR, 1, 2, 0),)),
        (17, ((PAR, 1, 2, 1),)),
    ),
    (
        (2, ((CROSSF, 0), (CROSSF, 1), (PASS_Z, 0, 1), (OWN, 0, 1, 0), (OWN, 0, 3, 0), (PASS_Z, 0, 0),)),
        (3, ((OWN, 0, 1, 1), (OWN, 0, 3, 1),)),
        (4, ((OWN, 1, 0, 0), (PASS_Z, 1, 0), (PASS_Z, 3, 0),)),
        (5, ((OWN, 0, 2, 0), (OWN, 0, 2, 1), (OWN, 1, 0, 1), (FWD_Y, 0, 0), (FWD_Y, 0, 1), (OWN, 1, 1, 0),)),
        (6, ((OWN, 1, 3, 0), (PASS_Z, 1, 1), (PASS_Z, 3, 1),)),
        (7, ((OWN, 1, 1, 1), (OWN, 1, 3, 1), (FWD_Y, 1, 0), (FWD_Y, 3, 0), (PAR, 0, 0, 0), (PAR, 1, 0, 0),)),
        (8, ((PASS_Z, 2, 0), (PASS_Z, 2, 1), (PAR, 0, 0, 1), (PAR, 1, 0, 1),)),
        (9, ((OWN, 1, 2, 0), (OWN, 1, 2, 1),)),
        (10, ((FWD_Y, 1, 1), (FWD_Y, 3, 1), (PAR, 0, 1, 0), (PAR, 1, 1, 0),)),
        (11, ((FWD_Y, 2, 0), (FWD_Y, 2, 1), (PAR, 0, 3, 0), (PAR, 1, 3, 0),)),
        (12, ((PAR, 0, 1, 1),)),
        (13, ((PAR, 1, 1, 1),)),
        (14, ((PAR, 0, 3, 1), (PAR, 1, 3, 1),)),
        (15, ((PAR, 0, 2, 0), (PAR, 1, 2, 0),)),
        (16, ((PAR, 0, 2, 1),)),
        (17, ((PAR, 1, 2, 1),)),
    ),
    (
        (2, ((CROSSF, 0), (CROSSF, 1), (OWN, 0, 1, 0), (OWN, 0, 3, 0), (FWD_Y, 0, 0), (PAR, 0, 0, 0),)),
        (3, ((OWN, 0, 1, 1), (OWN, 0, 3, 1), (FWD_Y, 0, 1), (PAR, 0, 0, 1),)),
        (4, ((OWN, 1, 0, 0), (OWN, 1, 0, 1),)),
        (5, ((OWN, 0, 2, 0), (OWN, 0, 2, 1), (FWD_Y, 1, 0), (PASS_Y, 0, 0), (PASS_Y, 0, 1), (PAR, 0, 1, 0),)),
        (6, ((OWN, 1, 3, 0), (FWD_Y, 3, 0), (PAR, 0, 3, 0),)),
        (7, ((OWN, 1, 1, 0), (OWN, 1, 3, 1), (FWD_Y, 1, 1), (PASS_Y, 1, 0), (PAR, 0, 1, 1), (PAR, 1, 0, 0), (PAR, 0, 3, 1), (FWD_Y, 3, 1),)),
        (8, ((OWN, 1, 2, 0), (OWN, 1, 2, 1), (PASS_Y, 3, 0), (PAR, 1, 0, 1),)),
        (9, ((FWD_Y, 2, 0), (PAR, 0, 2, 0),)),
        (10, ((OWN, 1, 1, 1), (PASS_Y, 1, 1), (PAR, 0, 2, 1), (PAR, 1, 1, 0),)),
        (11, ((FWD_Y, 2, 1), (PASS_Y, 3, 1), (PAR, 1, 3, 0),)),
        (12, ((PASS_Y, 2, 0), (PAR, 1, 1, 1),)),
        (14, ((PASS_Y, 2, 1), (PAR, 1, 3, 1),)),
        (15, ((PAR, 1, 2, 0),)),
        (16, ((PAR, 1, 2, 1),)),
    ),
    (
        (2, ((CROSSF, 0), (CROSSF, 1), (OWN, 0, 1, 0), (OWN, 0, 3, 0), (FWD_Y, 0, 0), (PAR, 0, 0, 0),)),
        (3, ((OWN, 0, 1, 1), (OWN, 0, 3, 1), (FWD_Y, 0, 1), (PAR, 0, 0, 1),)),
        (4, ((OWN, 1, 0, 0), (OWN, 1, 0, 1),)),
        (5, ((OWN, 0, 2, 0), (OWN, 0, 2, 1), (FWD_Y, 1, 0), (PASS_Y, 0, 0), (PASS_Y, 0, 1), (PAR, 0, 1, 0),)),
        (6, ((OWN, 1, 3, 0), (FWD_Y, 3, 0), (PAR, 0, 3, 0),)),
        (7, ((OWN, 1, 1, 0), (OWN, 1, 3, 1), (FWD_Y, 1, 1), (PASS_Y, 1, 0), (PAR, 0, 1, 1), (PAR, 1, 0, 0), (PAR, 0, 3, 1), (FWD_Y, 3, 1),)),
        (8, ((OWN, 1, 2, 0), (OWN, 1, 2, 1), (PASS_Y, 3, 0), (PAR, 1, 0, 1),)),
        (9, ((FWD_Y, 2, 0), (PAR, 0, 2, 0),)),
        (10, ((OWN, 1, 1, 1), (PASS_Y, 1, 1), (PAR, 0, 2, 1), (PAR, 1, 1, 0),)),
        (11, ((FWD_Y, 2, 1), (PASS_Y, 3, 1), (PAR, 1, 3, 0),)),
        (12, ((PASS_Y, 2, 0), (PAR, 1, 1, 1),)),
        (14, ((PASS_Y, 2, 1), (PAR, 1, 3, 1),)),
        (15, ((PAR, 1, 2, 0),)),
        (16, ((PAR, 1, 2, 1),)),
    ),
    (
        (2, ((CROSSF, 0), (CROSSF, 1), (OWN, 0, 1, 0), (OWN, 0, 3, 0), (FWD_Y, 0, 0), (PAR, 0, 0, 0),)),
        (3, ((OWN, 0, 1, 1), (OWN, 0, 3, 1), (FWD_Y, 0, 1), (PAR, 0, 0, 1),)),
        (4, ((OWN, 1, 0, 0), (OWN, 1, 0, 1),)),
        (5, ((OWN, 0, 2, 0), (OWN, 0, 2, 1), (FWD_Y, 1, 0), (PASS_Y, 0, 0), (PASS_Y, 0, 1), (PAR, 0, 1, 0),)),
        (6, ((OWN, 1, 1, 0), (OWN, 1, 3, 0), (FWD_Y, 3, 0), (PAR, 0, 3, 0),)),
        (7, ((OWN, 1, 1, 1), (OWN, 1, 3, 1), (FWD_Y, 1, 1), (PASS_Y, 1, 0), (PAR, 0, 1, 1), (PAR, 1, 0, 0),)),
        (8, ((FWD_Y, 3, 1), (PASS_Y, 3, 0), (PAR, 0, 3, 1), (PAR, 1, 0, 1),)),
        (9, ((OWN, 1, 2, 0),)),
        (10, ((OWN, 1, 2, 1), (FWD_Y, 2, 0), (PASS_Y, 1, 1), (PAR, 0, 2, 0), (PAR, 1, 1, 0),)),
        (11, ((FWD_Y, 2, 1), (PASS_Y, 3, 1), (PAR, 0, 2, 1), (PAR, 1, 3, 0),)),
        (12, ((PASS_Y, 2, 0),)),
        (13, ((PAR, 1, 1, 1),)),
        (14, ((PASS_Y, 2, 1), (PAR, 1, 3, 1),)),
        (15, ((PAR, 1, 2, 0),)),
        (16, ((PAR, 1, 2, 1),)),
    ),
    (
        (2, ((CROSSF, 0), (CROSSF, 1), (OWN, 0, 1, 0), (OWN, 0, 3, 0), (FWD_Y, 0, 0), (PAR, 0, 0, 0),)),
        (3, ((OWN, 0, 1, 1), (OWN, 0, 3, 1), (FWD_Y, 0, 1), (PAR, 0, 0, 1),)),
        (4, ((OWN, 1, 0, 0), (OWN, 1, 0, 1),)),
        (5, ((OWN, 0, 2, 0), (OWN, 0, 2, 1), (FWD_Y, 1, 0), (PASS_Y, 0, 0), (PASS_Y, 0, 1), (PAR, 0, 1, 0),)),
        (6, ((OWN, 1, 1, 0), (OWN, 1, 3, 0), (FWD_Y, 3, 0), (PAR, 0, 3, 0),)),
        (7, ((OWN, 1, 1, 1), (OWN, 1, 3, 1), (FWD_Y, 1, 1), (PASS_Y, 1, 0), (PAR, 0, 1, 1), (PAR, 1, 0, 0),)),
        (8, ((FWD_Y, 3, 1), (PASS_Y, 3, 0), (PAR, 0, 3, 1), (PAR, 1, 0, 1),)),
        (9, ((OWN, 1, 2, 0),)),
        (10, ((OWN, 1, 2, 1), (FWD_Y, 2, 0), (PASS_Y, 1, 1), (PAR, 0, 2, 0), (PAR, 1, 1, 0),)),
        (11, ((FWD_Y, 2, 1), (PASS_Y, 3, 1), (PAR, 0, 2, 1), (PAR, 1, 3, 0),)),
        (12, ((PASS_Y, 2, 0), (PAR, 1, 1, 1),)),
        (14, ((PASS_Y, 2, 1), (PAR, 1, 3, 1),)),
        (15, ((PAR, 1, 2, 0),)),
        (16, ((PAR, 1, 2, 1),)),
    ),
    (
        (2, ((CROSSF, 0), (CROSSF, 1), (OWN, 0, 1, 0), (OWN, 0, 3, 0), (FWD_Y, 0, 0),)),
        (3, ((OWN, 0, 1, 1), (OWN, 0, 3, 1), (FWD_Y, 0, 1),)),
        (4, ((OWN, 1, 0, 0), (PAR, 0, 0, 0),)),
        (5, ((OWN, 0, 2, 0), (OWN, 0, 2, 1), (OWN, 1, 0, 1), (FWD_Y, 1, 0), (PAR, 1, 0, 0), (FWD_Y, 3, 0), (OWN, 1, 1, 0),)),
        (6, ((OWN, 1, 3, 0), (PAR, 0, 0, 1), (PAR, 1, 0, 1),)),
        (7, ((OWN, 1, 1, 1), (OWN, 1, 3, 1), (FWD_Y, 1, 1), (PAR, 0, 1, 0), (PAR, 1, 1, 0),)),
        (8, ((FWD_Y, 3, 1), (PAR, 1, 3, 0),)),
        (9, ((OWN, 1, 2, 0), (FWD_Y, 2, 0), (PAR, 0, 3, 0),)),
        (10, ((PAR, 0, 1, 1), (PAR, 1, 1, 1),)),
        (11, ((FWD_Y, 2, 1), (PAR, 0, 3, 1), (PAR, 1, 3, 1),)),
        (12, ((OWN, 1, 2, 1), (PAR, 1, 2, 0),)),
        (13, ((PAR, 0, 2, 0),)),
        (14, ((PAR, 0, 2, 1), (PAR, 1, 2, 1),)),
    ),
    (
        (2, ((CROSSF, 0), (CROSSF, 1), (OWN, 0, 1, 0), (OWN, 0, 3, 0), (FWD_Y, 0, 0),)),
        (3, ((OWN, 0, 1, 1), (OWN, 0, 3, 1), (FWD_Y, 0, 1),)),
        (4, ((OWN, 1, 0, 0), (PAR, 1, 0, 0),)),
        (5, ((OWN, 0, 2, 0), (OWN, 0, 2, 1), (OWN, 1, 0, 1), (FWD_Y, 1, 0), (PAR, 0, 0, 0), (FWD_Y, 3, 0), (OWN, 1, 1, 0),)),
        (6, ((OWN, 1, 3, 0), (PAR, 0, 0, 1), (PAR, 1, 0, 1),)),
        (7, ((OWN, 1, 1, 1), (OWN, 1, 3, 1), (FWD_Y, 1, 1), (PAR, 0, 1, 0), (PAR, 1, 1, 0),)),
        (8, ((FWD_Y, 3, 1), (PAR, 0, 3, 0),)),
        (9, ((OWN, 1, 2, 0), (FWD_Y, 2, 0), (PAR, 1, 3, 0),)),
        (10, ((PAR, 0, 1, 1), (PAR, 1, 1, 1),)),
        (11, ((FWD_Y, 2, 1), (PAR, 0, 3, 1), (PAR, 1, 3, 1),)),
        (12, ((OWN, 1, 2, 1), (PAR, 0, 2, 0),)),
        (13, ((PAR, 1, 2, 0),)),
        (14, ((PAR, 0, 2, 1), (PAR, 1, 2, 1),)),
    ),
    (
        (2, ((CROSSF, 0), (CROSSF, 1), (OWN, 0, 1, 0), (OWN, 0, 3, 0), (FWD_Y, 0, 0),)),
        (3, ((OWN, 0, 1, 1), (OWN, 0, 3, 1), (FWD_Y, 0, 1),)),
        (4, ((OWN, 1, 0, 0), (PAR, 0, 0, 0),)),
        (5, ((OWN, 0, 2, 0), (OWN, 0, 2, 1), (OWN, 1, 0, 1), (FWD_Y, 1, 0), (PAR, 1, 0, 0), (FWD_Y, 3, 0), (OWN, 1, 1, 0),)),
        (6, ((OWN, 1, 3, 0), (PAR, 0, 0, 1), (PAR, 1, 0, 1),)),
        (7, ((OWN, 1, 1, 1), (OWN, 1, 3, 1), (FWD_Y, 1, 1), (PAR, 0, 1, 0), (PAR, 1, 1, 0),)),
        (8, ((OWN, 1, 2, 0), (FWD_Y, 3, 1), (PAR, 1, 3, 0),)),
        (9, ((OWN, 1, 2, 1), (FWD_Y, 2, 0), (PAR, 0, 3, 0),)),
        (10, ((PAR, 0, 1, 1), (PAR, 1, 1, 1),)),
        (11, ((FWD_Y, 2, 1), (PAR, 0, 3, 1), (PAR, 1, 3, 1),)),
        (12, ((PAR, 1, 2, 0),)),
        (13, ((PAR, 0, 2, 0),)),
        (14, ((PAR, 0, 2, 1), (PAR, 1, 2, 1),)),
    ),
    (
        (2, ((CROSSF, 0), (CROSSF, 1), (OWN, 0, 1, 0), (OWN, 0, 3, 0), (FWD_Y, 0, 0),)),
        (3, ((OWN, 0, 1, 1), (OWN, 0, 3, 1), (FWD_Y, 0, 1),)),
        (4, ((OWN, 1, 0, 0), (PAR, 1, 0, 0),)),
        (5, ((OWN, 0, 2, 0), (OWN, 0, 2, 1), (OWN, 1, 0, 1), (FWD_Y, 1, 0), (PAR, 0, 0, 0), (FWD_Y, 3, 0), (OWN, 1, 1, 0),)),
        (6, ((OWN, 1, 3, 0), (PAR, 0, 0, 1), (PAR, 1, 0, 1),)),
        (7, ((OWN, 1, 1, 1), (OWN, 1, 3, 1), (FWD_Y, 1, 1), (PAR, 0, 1, 0), (PAR, 1, 1, 0),)),
        (8, ((OWN, 1, 2, 0), (FWD_Y, 3, 1), (PAR, 0, 3, 0),)),
        (9, ((OWN, 1, 2, 1), (FWD_Y, 2, 0), (PAR, 1, 3, 0),)),
        (10, ((PAR, 0, 1, 1), (PAR, 1, 1, 1),)),
        (11, ((FWD_Y, 2, 1), (PAR, 0, 3, 1), (PAR, 1, 3, 1),)),
        (12, ((PAR, 0, 2, 0),)),
        (13, ((PAR, 1, 2, 0),)),
        (14, ((PAR, 0, 2, 1), (PAR, 1, 2, 1),)),
    ),
)

STAGES = len(SEQUENCE)
BASES = [sum(PARTS[stage] for stage in SEQUENCE[:n]) for n in range(STAGES + 1)]
POINTS = BASES[-1] + 1
PAR_AT, T1_AT, T2_AT, T3_AT, TC_AT, SLOTS = 32, 64, 72, 80, 88, 90
WAYS = ("x+", "x-", "y+", "y-", "z+", "z-", "core", "ya", "yb", "za", "zb")
WAIT = 15
CLASSES = [(x, y) for x in range(4) for y in range(4)]


def sign_of(j, k):
    return "+" if (k + (0, 1, 1, 0)[j]) % 2 == 0 else "-"


def name_of(x, y, row, j):
    return (y // 2 + row) % 2 * 4 + (x + 4 - j) % 4


def row_behind(y, sign):
    return (y + 3) % 4 // 2 if sign == "+" else (y + 1) % 4 // 2


def feed(x, y, j, k, src):
    up = y // 2 == 1
    final, via1, via2 = ("par", name_of(x, y, 0, j), k), ("t1", j, k), ("t2", j, k)
    sends = []
    if x in (0, 1):
        sends.append((src, via1, "z" + sign_of(j, k)))
    if x == 1:
        sends.append((src, final, "ya"))
    if x in (2, 3):
        sends.append((src, final if x == 2 and not up else via1, "za"))
        sends.append((src, final if x == 2 and up else via2, "zb"))
    return sends


def expand(x, y, event):
    kind, args = event[0], event[1:]
    up = y // 2 == 1
    ops = []
    if kind == CROSSF:
        (k,) = args
        sign = "+-"[k]
        ops = [("tc", k), (("tc", k), ("own", row_behind(y, sign) * 4 + x, k), "y" + sign)]
    if kind == OWN:
        row, j, k = args
        here = ("own", name_of(x, y, row, j), k)
        ops = [here]
        if (row, j) == (1, 0) or (j == 1 and (k + row) % 2 == 0):
            ops.append((here, here, "x+"))
        if (row, j) == (1, 0) or (j == 3 and (k + row) % 2 == 1):
            ops.append((here, here, "x-"))
        if row == 0:
            ops += feed(x, y, j, k, here)
        ops.append((here, here, "core"))
    if kind == PASS_Z:
        j, k = args
        here = ("t1", j, k)
        there = ("par", name_of(x, y, 0, j), k) if x == 0 and up else ("t2", j, k)
        ops = [here, (here, there, "z" + sign_of(j, k))]
    if kind == FWD_Y:
        j, k = args
        final, there, way = ("par", name_of(x, y, 0, j), k), ("t3", j, k), "y" + sign_of(j, k)
        if x == 3 or (x == 2 and up):
            ops += [("t1", j, k), (("t1", j, k), final, "ya") if x == 3 else (("t1", j, k), there, way)]
        if x in (1, 3) or not up:
            ops += [("t2", j, k), (("t2", j, k), final, "yb") if x in (1, 3) else (("t2", j, k), there, way)]
    if kind == PASS_Y:
        j, k = args
        sign = sign_of(j, k)
        row = row_behind(y, sign)
        if x == 2 or row == 0:
            ops = [("t3", j, k), (("t3", j, k), ("par", row * 4 + (x + 4 - j) % 4, k), "y" + sign)]
    if kind == PAR:
        row, j, k = args
        here = ("par", name_of(x, y, row, j), k)
        ops = [here, (here, here, "core")]
    return ops


def slot(place, c):
    kind, rest = place[0], place[1:]
    if kind in ("own", "par"):
        q, k = rest
        return (PAR_AT if kind == "par" else 0) + q * 4 + c * 2 + k
    if kind == "tc":
        return TC_AT + rest[0]
    return {"t1": T1_AT, "t2": T2_AT, "t3": T3_AT}[kind] + rest[0] * 2 + rest[1]


def tables(x, y):
    per_core = []
    for c in range(2):
        ops, begins, sends, at = [], [], 0, dict(EVENTS[CLASSES.index((x, y))])
        for point in range(POINTS):
            begins.append(len(ops))
            for event in at.get(point, ()):
                for op in expand(x, y, event):
                    if isinstance(op[0], str):
                        ops.append(slot(op, c) + 2097152 * WAIT)
                    else:
                        src, dst, way = op
                        ops.append(slot(src, c) + 128 * slot(dst, c) + 16384 * sends + 2097152 * WAYS.index(way))
                        sends += 1
        per_core.append((ops, begins + [len(ops), sends], sends))
    return per_core


TABLES = {cls: tables(*cls) for cls in CLASSES}
MOST_OPS = max(len(ops) for cores in TABLES.values() for ops, _, _ in cores)
MOST_SENDS = max(sends for cores in TABLES.values() for _, _, sends in cores)
FIRST_SENDS = 12


def columns(t):
    first, last = t * 256, (t + 1) * 256
    cuts = [first] + [cut for cut in range(0, NI * V, V) if first < cut < last] + [last]
    return [(u - first, w - first, u // V, u % V) for u, w in zip(cuts, cuts[1:])]


def kernel(dims, mine, amps, out, out_own, out_par, buf, rc, half, acc, ops, begins, devs,
           ssem, first_sem, rsem, local_sem):
    sym, tile, c = lax.axis_index("sym"), lax.axis_index("tile"), lax.axis_index("occ")
    x, yhi = sym % 4, sym // 4
    x0, x1 = x % 2, x // 2
    z, ylo = tile // 2, tile % 2
    z0, z1 = z % 2, z // 2
    y = 2 * yhi + ylo
    none = sym == 0

    def dev(dx=0, dy=0, dz=0, dc=0):
        xx, yy, zz = (x + 4 + dx) % 4, (y + 4 + dy) % 4, (z + 4 + dz) % 4
        return ((yy // 2) * 4 + xx) * 16 + (zz * 2 + yy % 2) * 2 + (c + dc) % 2

    step_a = 1 - 2 * (yhi + ylo - 2 * yhi * ylo)
    step_z = 1 - 2 * z0
    to = {
        "x+": dev(dx=1), "x-": dev(dx=-1), "y+": dev(dy=1), "y-": dev(dy=-1), "z+": dev(dz=1), "z-": dev(dz=-1),
        "core": dev(dc=1), "ya": dev(dy=step_a), "yb": dev(dy=-step_a), "za": dev(dz=step_z), "zb": dev(dz=-step_z),
    }
    barrier = pltpu.get_barrier_semaphore()
    for way in WAYS[:7]:
        pl.semaphore_signal(barrier, inc=1, device_id=to[way], device_id_type=pl.DeviceIdType.LOGICAL)

    def own_slot(q, core, k):
        return q * 4 + core * 2 + k

    keep = []
    for k in range(PIECES):
        keep.append(pltpu.make_async_copy(mine.at[pl.ds(k * PV, PV)], buf.at[own_slot(sym, c, k)], local_sem.at[8 + k]))
        keep[-1].start()
    loads = [pltpu.make_async_copy(amps.at[i], rc.at[:, pl.ds(i * V, V)], local_sem.at[i]) for i in range(NI)]
    for load in loads:
        load.start()

    pl.semaphore_wait(barrier, 7)

    def remote(src, dst_slot, sem, where):
        return pltpu.make_async_remote_copy(
            src, buf.at[dst_slot], sem, rsem.at[dst_slot], device_id=where, device_id_type=pl.DeviceIdType.LOGICAL
        )

    def arrived(at):
        remote(buf.at[at], at, first_sem.at[0], to["core"]).wait_recv()

    firsts = []

    def first(src, place, where, cond=None):
        index = len(firsts)
        if cond is None:
            remote(src, place, first_sem.at[index], where).start()
        else:
            pl.when(cond)(lambda: remote(src, place, first_sem.at[index], where).start())
        firsts.append((src, place, cond, index))

    step_2 = {k: {"+": to["z+"], "-": to["z-"]}[sign_of(0, k)] for k in range(PIECES)}
    for k in range(PIECES):
        src = mine.at[pl.ds(k * PV, PV)]
        home = own_slot(sym, c, k)
        final, via1, via2 = PAR_AT + home, T1_AT + k, T2_AT + k
        first(src, home, to["core"])
        first(src, home, to["x+"])
        first(src, home, to["x-"])
        first(src, TC_AT + k, to["y" + "+-"[k]])
        direct_b, direct_a = x0 + 2 * (1 - x1) + (1 - yhi) == 0, x0 + 2 * (1 - x1) + yhi == 0
        where_b = x1 * to["zb"] + (1 - x1) * step_2[k]
        place_b = jnp.where(direct_b, final, x1 * via2 + (1 - x1) * via1)
        first(src, place_b, where_b)
        where_a = x1 * to["za"] + (1 - x1) * to["ya"]
        place_a = jnp.where(direct_a | (x1 == 0), final, via1)
        first(src, place_a, where_a, x > 0)

    for (at_x, at_y), cores in TABLES.items():
        @pl.when((x == at_x) & (y == at_y))
        def _():
            (ops0, begins0, _), (ops1, _, _) = cores
            for n, (op0, op1) in enumerate(zip(ops0, ops1)):
                ops[n] = op0 + (op1 - op0) * c if op0 != op1 else op0
            for n, begin in enumerate(begins0):
                begins[n] = begin
    for n, way in enumerate(WAYS):
        devs[n] = to[way]

    n_row = dims[tile]
    n_col = dims[(z1 + yhi - 2 * z1 * yhi) * 4 + (z0 + x1 - 2 * z0 * x1) * 2 + (ylo + x0 - 2 * ylo * x0)]
    live_r = jnp.where(lax.broadcasted_iota(jnp.int32, (V, V), 0) < n_row, 1.0, 0.0)
    live = jnp.where(lax.broadcasted_iota(jnp.int32, (V, V), 1) < n_col, live_r, 0.0).astype(jnp.bfloat16)
    acc[...] = jnp.zeros_like(acc)
    for load in loads:
        load.wait()
    for i in range(NI):
        rc[:, i * V:(i + 1) * V] = rc[:, i * V:(i + 1) * V] * live
    for copy in keep:
        copy.wait()

    def decoded(n):
        op = ops[n]
        src, rest = lax.rem(op, 128), lax.div(op, 128)
        dst, rest = lax.rem(rest, 128), lax.div(rest, 128)
        return src, dst, lax.rem(rest, 128), lax.div(rest, 128)

    def events(point):
        @pl.loop(begins[point], begins[point + 1])
        def _(n):
            src, dst, index, way = decoded(n)

            @pl.when(way == WAIT)
            def _():
                arrived(src)

            @pl.when(way != WAIT)
            def _():
                remote(buf.at[src], dst, ssem.at[index], devs[way]).start()

    digit = (1 + 15 * x0) * (1 + 255 * x1)

    def chosen(groups, n):
        code = 0
        for number, names in enumerate(groups):
            of_y = [0] * 4
            for (at_x, at_y), (row, j, k) in zip(CLASSES, names):
                of_y[at_y] += (row * 8 + j * 2 + k) * 16 ** at_x
            value = of_y[0]
            if len(set(of_y)) > 1:
                value = value + (of_y[1] - of_y[0]) * ylo + (of_y[2] - of_y[0]) * yhi
                value = value + (of_y[3] - of_y[2] - of_y[1] + of_y[0]) * (yhi * ylo)
            code = code + (n == number) * 1 * value
        code = lax.rem(lax.div(code, digit), 16)
        return (yhi + code // 8) % 2 * 4 + (x + 4 - code // 2 % 4) % 4, code % 2

    def base_of(n):
        return sum((n == number) * base for number, base in enumerate(BASES[:-1]) if base)

    par_base = PAR_AT * (1 - (sym == 0) * 1)

    def unit(base, q, core):
        at = base + q * 4 + core * 2
        return buf[pl.ds(at, 2)].reshape(V, V)

    def first_stage(base, halves, parts):
        for q, k in halves:
            arrived(own_slot(q, 1 - c, k))
        for h in range(parts):
            if h:
                events(base + h)
            for t in range(h * 12 // parts, (h + 1) * 12 // parts):
                left = jnp.concatenate([buf[q * 4 + 2 * p + k] for q, k in halves for p in range(2)], axis=0)
                r = jnp.dot(left, rc[:, t * 256:(t + 1) * 256], preferred_element_type=jnp.float32).astype(jnp.bfloat16)
                for lo_col, hi_col, pair, at in columns(t):
                    for number, (q, k) in enumerate(halves):
                        rows = pl.ds(pl.multiple_of(pair * V + k * PV, PV), PV)
                        for p in range(2):
                            lanes = pl.ds(p * V + at, hi_col - lo_col)
                            first = (2 * number + p) * PV
                            half[q, rows, lanes] = r[first:first + PV, lo_col:hi_col]

    def second_stage(base, q):
        @pl.when(jnp.logical_not(none))
        def _():
            for k in range(PIECES):
                arrived(PAR_AT + own_slot(q, 1 - c, k))

        for h in range(2):
            if h and PARTS[2] > 1:
                events(base + h)
            rows = pl.ds(h * HALF, HALF)
            for b0, b1 in ((0, 256), (256, 384)):
                right = jnp.concatenate([unit(par_base, q, p)[b0:b1] for p in range(2)], axis=1)
                acc[rows, b0:b1] += lax.dot_general(
                    half[q, rows, :], right, (((1,), (1,)), ((), ())), preferred_element_type=jnp.float32
                )

    @pl.loop(0, STAGES)
    def _(n):
        kind = sum((n == k) * 1 * stage for k, stage in enumerate(SEQUENCE))
        halves = [chosen(group, n) for group in UNITS]
        base = base_of(n)
        events(base)
        for stage in set(SEQUENCE) - {2}:
            pl.when(kind == stage)(lambda stage=stage: first_stage(base, halves, PARTS[stage]))
        pl.when(kind == 2)(lambda: second_stage(base, halves[0][0]))

    for h in range(2):
        rows = pl.ds(h * HALF, HALF)
        pltpu.make_async_copy(acc.at[rows], out.at[rows], local_sem.at[h]).start()
    events(POINTS - 1)

    leaving = []
    for r in range(len(REST)):
        q, _ = chosen(REST, jnp.int32(r))
        for k in range(PIECES):
            arrived(own_slot(q, 1 - c, k))

        @pl.when(jnp.logical_not(none))
        def _():
            for k in range(PIECES):
                arrived(PAR_AT + own_slot(q, 1 - c, k))

        par_at = par_base + q * 4
        for source, target, sem in ((q * 4, out_own.at[r], 18 + 2 * r), (par_at, out_par.at[r], 19 + 2 * r)):
            leaving.append(pltpu.make_async_copy(buf.at[pl.ds(source, 4)], target, local_sem.at[sem - 8]))
            leaving[-1].start()

    for src, place, cond, index in firsts:
        def sent(src=src, place=place, index=index):
            remote(src, place, first_sem.at[index], to["core"]).wait_send()

        if cond is None:
            sent()
        else:
            pl.when(cond)(sent)

    @pl.loop(0, begins[POINTS + 1])
    def _(n):
        remote(buf.at[0], 0, ssem.at[n], to["core"]).wait_send()

    for h in range(2):
        rows = pl.ds(h * HALF, HALF)
        pltpu.make_async_copy(acc.at[rows], out.at[rows], local_sem.at[h]).wait()
    for copy in leaving:
        copy.wait()


ALL = [(row, j) for j in (0, 1, 3, 2) for row in range(2)]


def left_over():
    by_class = []
    for at in range(len(CLASSES)):
        done = [names[at][:2] for group in UNITS for stage, names in zip(SEQUENCE, group) if stage != 2]
        by_class.append([name + (0,) for name in ALL if name not in done])
    return tuple(zip(*by_class))


REST = left_over()


def rest_kernel(dims, own_hbm, par_hbm, amps, raw, out, own, par, rc, half, acc, sems):
    sym, tile = lax.axis_index("sym"), lax.axis_index("tile")
    n, hi = len(REST), NI // 2
    get_own = pltpu.make_async_copy(own_hbm, own, sems.at[0])
    get_par = pltpu.make_async_copy(par_hbm, par, sems.at[1])
    get_amps = [pltpu.make_async_copy(amps.at[i], rc.at[:, pl.ds(i * V, V)], sems.at[2 + i]) for i in range(NI)]
    get_raw = [
        pltpu.make_async_copy(raw.at[pl.ds(h * HALF, HALF)], acc.at[pl.ds(h * HALF, HALF)], sems.at[2 + NI + h])
        for h in range(2)
    ]
    for copy in get_amps[:hi] + [get_own, get_par, get_raw[0]] + get_amps[hi:] + [get_raw[1]]:
        copy.start()
    n_row, n_col = dims[tile], dims[jnp.bitwise_xor(tile, sym)]
    live = (lax.broadcasted_iota(jnp.int32, (V, V), 0) < n_row) & (lax.broadcasted_iota(jnp.int32, (V, V), 1) < n_col)
    live_b = jnp.where(live, 1.0, 0.0).astype(jnp.bfloat16)
    puts = []
    for h in range(2):
        for i in range(h * hi, (h + 1) * hi):
            get_amps[i].wait()
            rc[:, i * V:(i + 1) * V] = rc[:, i * V:(i + 1) * V] * live_b
        if h == 0:
            get_own.wait()
        for t in range(6 * h, 6 * (h + 1)):
            left = own[...].reshape(n * 2 * V, V)
            r = jnp.dot(left, rc[:, t * 256:(t + 1) * 256], preferred_element_type=jnp.float32).astype(jnp.bfloat16)
            for lo_col, hi_col, pair, at in columns(t):
                for p in range(2 * n):
                    lanes = pl.ds(p * V + at, hi_col - lo_col)
                    half[(pair - h * hi) * V:(pair - h * hi + 1) * V, lanes] = r[p * V:(p + 1) * V, lo_col:hi_col]
        if h == 0:
            get_par.wait()
        get_raw[h].wait()
        rows = pl.ds(h * HALF, HALF)
        for b0, b1 in ((0, 256), (256, 384)):
            right = [par[r, pl.ds(2 * p, 2)].reshape(V, V)[b0:b1] for r in range(n) for p in range(2)]
            right = jnp.concatenate(right, axis=1)
            r = lax.dot_general(half[...], right, (((1,), (1,)), ((), ())), preferred_element_type=jnp.float32)
            r = r + acc[rows, b0:b1]
            for i in range(hi):
                at = pl.ds((h * hi + i) * V, V)
                acc[at, b0:b1] = jnp.where(live[:, b0:b1], r[i * V:(i + 1) * V], 0.0)
            lanes = pl.ds(b0, b1 - b0)
            puts.append(pltpu.make_async_copy(acc.at[rows, lanes], out.at[rows, lanes], sems.at[4 + NI + len(puts)]))
            puts[-1].start()
    for copy in puts:
        copy.wait()


def shards(irrep_dims, chol_vectors, amplitudes):
    bf, sem = jnp.bfloat16, pltpu.SemaphoreType.DMA
    n = len(REST)
    own, chol, amps = (n, 4, PV, V), chol_vectors.reshape(V, V), amplitudes.reshape(NI, V, V)
    anywhere = pl.BlockSpec(memory_space=pl.ANY)
    raw, rest_own, rest_par = pl.pallas_call(
        kernel,
        out_shape=[
            jax.ShapeDtypeStruct((NI * V, V), jnp.float32),
            jax.ShapeDtypeStruct(own, bf),
            jax.ShapeDtypeStruct(own, bf),
        ],
        in_specs=[pl.BlockSpec(memory_space=pltpu.SMEM), anywhere, anywhere],
        out_specs=[anywhere] * 3,
        scratch_shapes=[
            pltpu.VMEM((SLOTS, PV, V), bf),
            pltpu.VMEM((V, NI * V), bf),
            pltpu.VMEM((8, NI * V, 2 * V), bf),
            pltpu.VMEM((NI * V, V), jnp.float32),
            pltpu.SMEM((MOST_OPS,), jnp.int32),
            pltpu.SMEM((POINTS + 2,), jnp.int32),
            pltpu.SMEM((len(WAYS),), jnp.int32),
            sem((MOST_SENDS,)), sem((FIRST_SENDS,)), sem((SLOTS,)), sem((10 + 2 * n,)),
        ],
        compiler_params=pltpu.CompilerParams(
            collective_id=0, has_side_effects=True, vmem_limit_bytes=63 * 1024 * 1024
        ),
        cost_estimate=pl.CostEstimate(flops=(8 - n) * 3_600_000_000, bytes_accessed=12_000_000, transcendentals=0),
        name="ladder",
    )(irrep_dims, chol, amps)
    total = pl.pallas_call(
        rest_kernel,
        out_shape=jax.ShapeDtypeStruct((NI * V, V), jnp.float32),
        in_specs=[pl.BlockSpec(memory_space=pltpu.SMEM)] + [anywhere] * 4,
        out_specs=anywhere,
        scratch_shapes=[
            pltpu.VMEM(own, bf),
            pltpu.VMEM(own, bf),
            pltpu.VMEM((V, NI * V), bf),
            pltpu.VMEM((HALF, n * 2 * V), bf),
            pltpu.VMEM((NI * V, V), jnp.float32),
            sem((8 + NI,)),
        ],
        compiler_params=pltpu.CompilerParams(vmem_limit_bytes=60 * 1024 * 1024),
        cost_estimate=pl.CostEstimate(flops=n * 3_600_000_000, bytes_accessed=16_000_000, transcendentals=0),
        name="rest",
    )(irrep_dims, rest_own, rest_par, amps, raw)
    return total.reshape(1, NI, V, V)


def solution(mesh):
    return jax.shard_map(
        shards,
        mesh=mesh,
        in_specs=(P(), P(("sym", "occ"), "tile", None), P("sym", "occ", "tile", None)),
        out_specs=P("sym", "occ", "tile", None),
        check_vma=False,
    )
```

time: 72.8 us -> 77.2 us (1.060)
  the two profiles are of different devices: /device:TPU:3 before, /device:TPU:4 now
where the time goes in v2:
time: 77.2 us; the launch traced here: 77.1 us
  Pallas kernels  76.9 us (100%)
    pallas_call x1, Pallas kernels, shards(): pl.pallas_call(kernel, out_shape=[jax.ShapeDtypeStruct((NI * V, V), jnp.f...  67.5 us
    pallas_call x1, Pallas kernels, shards(): pl.pallas_call(rest_kernel, out_shape=jax.ShapeDtypeStruct((NI * V, V), j...  9.46 us

profile of v2, /device:TPU:4, one launch (start us, length us, event | category | flops | bytes accessed | tf_op | source)
XLA Modules:
  0.0 77.1 jit_solution(15860653365642323763)
XLA Ops:
  0.0 67.5 %ladder.1 = (f32[3072,384]{1,0:T(8,128)}, bf16[1,4,192,384]{3,2,1,0:T(8,128)(2,1)}, bf16[1,4,192,384]{3,2,1,0:T(8,128)(2,1)}) custom-call(s32[8]{0:T(128)} %dims.3, bf16[384,384]{1,0:T(8,128)(2,1)} %bitcast.5, bf16[8,384,384]{2,1,0:T(8,128)(2,1)} %bitcast.3), custom_call_target="tpu_custom_call" | custom-call | flops 25200001024 | bytes 12000000 | tf_op jit(solution)/shard_map/ladder/pallas_call | solution.py:709
  67.5 9.5 %rest.1 = f32[3072,384]{1,0:T(8,128)} custom-call(s32[8]{0:T(128)} %dims.3, bf16[1,4,192,384]{3,2,1,0:T(8,128)(2,1)} %get-tuple-element.8.own_hbm, bf16[1,4,192,384]{3,2,1,0:T(8,128)(2,1)} %get-tuple-element.9.par_hbm, bf16[8,384,384]{2,1,0:T(8,128)(2,1)} %bitcast.4, f32[3072,384]{1,0:T(8,128)} %get-tuple-element.10.raw), custom_call_target="tpu_custom_call" | custom-call | flops 3600000000 | bytes 16000000 | tf_op jit(solution)/shard_map/rest/pallas_call | solution.py:734

commit v3 on v1

--- a/solution.py
+++ b/solution.py
@@ -454,7 +454,7 @@
                         src, dst, way = op
                         ops.append(slot(src, c) + 128 * slot(dst, c) + 16384 * sends + 2097152 * WAYS.index(way))
                         sends += 1
-        per_core.append((ops, begins + [len(ops)], sends))
+        per_core.append((ops, begins + [len(ops), sends], sends))
     return per_core
 
 
@@ -626,7 +626,7 @@
                             first = (2 * number + p) * PV
                             half[q, rows, lanes] = r[first:first + PV, lo_col:hi_col]
 
-    def second_stage(base, q):
+    def second_stage(base, q, last=False):
         @pl.when(jnp.logical_not(none))
         def _():
             for k in range(PIECES):
@@ -641,8 +641,10 @@
                 acc[rows, b0:b1] += lax.dot_general(
                     half[q, rows, :], right, (((1,), (1,)), ((), ())), preferred_element_type=jnp.float32
                 )
-
-    @pl.loop(0, STAGES)
+            if last:
+                pltpu.make_async_copy(acc.at[rows], out.at[rows], local_sem.at[h]).start()
+
+    @pl.loop(0, STAGES - 1)
     def _(n):
         second = sum((n == k) * 1 for k, stage in enumerate(SEQUENCE) if stage == 2)
         halves = [chosen(group, n) for group in UNITS]
@@ -651,9 +653,8 @@
         pl.when(second == 0)(lambda: first_stage(base, halves))
         pl.when(second == 1)(lambda: second_stage(base, halves[0][0]))
 
-    for h in range(2):
-        rows = pl.ds(h * HALF, HALF)
-        pltpu.make_async_copy(acc.at[rows], out.at[rows], local_sem.at[h]).start()
+    events(BASES[-2])
+    second_stage(BASES[-2], chosen(UNITS[0], jnp.int32(STAGES - 1))[0], last=True)
     events(POINTS - 1)
 
     leaving = []
@@ -681,13 +682,9 @@
         else:
             pl.when(cond)(sent)
 
-    @pl.loop(0, begins[POINTS])
+    @pl.loop(0, begins[POINTS + 1])
     def _(n):
-        src, dst, index, way = decoded(n)
-
-        @pl.when(way != WAIT)
-        def _():
-            remote(buf.at[src], dst, ssem.at[index], devs[way]).wait_send()
+        remote(buf.at[0], 0, ssem.at[n], to["core"]).wait_send()
 
     for h in range(2):
         rows = pl.ds(h * HALF, HALF)
@@ -778,7 +775,7 @@
             pltpu.VMEM((8, NI * V, 2 * V), bf),
             pltpu.VMEM((NI * V, V), jnp.float32),
             pltpu.SMEM((MOST_OPS,), jnp.int32),
-            pltpu.SMEM((POINTS + 1,), jnp.int32),
+            pltpu.SMEM((POINTS + 2,), jnp.int32),
             pltpu.SMEM((len(WAYS),), jnp.int32),
             sem((MOST_SENDS,)), sem((FIRST_SENDS,)), sem((SLOTS,)), sem((10 + 2 * n,)),
         ],

time: 72.8 us -> 71.8 us (0.986)
  Pallas kernels: 71.5 us -> 70.7 us
    pallas_call x1, Pallas kernels: 62.1 us -> 61.2 us  [shards(): pl.pallas_call(kernel, out_shape=[jax.ShapeDtypeStruct((NI * V, V), jnp.f...]
where the time goes in v3:
time: 71.8 us; the launch traced here: 70.9 us
  Pallas kernels  70.7 us (98%)
    pallas_call x1, Pallas kernels, shards(): pl.pallas_call(kernel, out_shape=[jax.ShapeDtypeStruct((NI * V, V), jnp.f...  61.2 us
    pallas_call x1, Pallas kernels, shards(): pl.pallas_call(rest_kernel, out_shape=jax.ShapeDtypeStruct((NI * V, V), j...  9.46 us

profile of v3, /device:TPU:3, one launch (start us, length us, event | category | flops | bytes accessed | tf_op | source)
XLA Modules:
  0.0 70.9 jit_solution(14480274305473496187)
XLA Ops:
  0.0 61.2 %ladder.1 = (f32[3072,384]{1,0:T(8,128)}, bf16[1,4,192,384]{3,2,1,0:T(8,128)(2,1)}, bf16[1,4,192,384]{3,2,1,0:T(8,128)(2,1)}) custom-call(s32[8]{0:T(128)} %dims.3, bf16[384,384]{1,0:T(8,128)(2,1)} %bitcast.5, bf16[8,384,384]{2,1,0:T(8,128)(2,1)} %bitcast.3), custom_call_target="tpu_custom_call" | custom-call | flops 25200001024 | bytes 12000000 | tf_op jit(solution)/shard_map/ladder/pallas_call | solution.py:763
  61.2 9.5 %rest.1 = f32[3072,384]{1,0:T(8,128)} custom-call(s32[8]{0:T(128)} %dims.3, bf16[1,4,192,384]{3,2,1,0:T(8,128)(2,1)} %get-tuple-element.8.own_hbm, bf16[1,4,192,384]{3,2,1,0:T(8,128)(2,1)} %get-tuple-element.9.par_hbm, bf16[8,384,384]{2,1,0:T(8,128)(2,1)} %bitcast.4, f32[3072,384]{1,0:T(8,128)} %get-tuple-element.10.raw), custom_call_target="tpu_custom_call" | custom-call | flops 3600000000 | bytes 16000000 | tf_op jit(solution)/shard_map/rest/pallas_call | solution.py:788

commit v4 on v3

--- a/solution.py
+++ b/solution.py
@@ -636,10 +636,11 @@
             if h and PARTS[2] > 1:
                 events(base + h)
             rows = pl.ds(h * HALF, HALF)
-            for b0, b1 in ((0, 256), (256, 384)):
-                right = jnp.concatenate([unit(par_base, q, p)[b0:b1] for p in range(2)], axis=1)
-                acc[rows, b0:b1] += lax.dot_general(
-                    half[q, rows, :], right, (((1,), (1,)), ((), ())), preferred_element_type=jnp.float32
+            right = jnp.concatenate([unit(par_base, q, p) for p in range(2)], axis=1)
+            for m in range(2 * h, 2 * h + 2):
+                pairs = pl.ds(m * 2 * V, 2 * V)
+                acc[pairs, :] += lax.dot_general(
+                    half[q, pairs, :], right, (((1,), (1,)), ((), ())), preferred_element_type=jnp.float32
                 )
             if last:
                 pltpu.make_async_copy(acc.at[rows], out.at[rows], local_sem.at[h]).start()

time: 71.8 us -> 71.8 us (level)
  no operation moved by 1% of the time
where the time goes in v4:
time: 71.8 us; the launch traced here: 70.9 us
  Pallas kernels  70.7 us (98%)
    pallas_call x1, Pallas kernels, shards(): pl.pallas_call(kernel, out_shape=[jax.ShapeDtypeStruct((NI * V, V), jnp.f...  61.3 us
    pallas_call x1, Pallas kernels, shards(): pl.pallas_call(rest_kernel, out_shape=jax.ShapeDtypeStruct((NI * V, V), j...  9.46 us

profile of v4, /device:TPU:3, one launch (start us, length us, event | category | flops | bytes accessed | tf_op | source)
XLA Modules:
  0.0 70.9 jit_solution(5627575723271468207)
XLA Ops:
  0.0 61.3 %ladder.1 = (f32[3072,384]{1,0:T(8,128)}, bf16[1,4,192,384]{3,2,1,0:T(8,128)(2,1)}, bf16[1,4,192,384]{3,2,1,0:T(8,128)(2,1)}) custom-call(s32[8]{0:T(128)} %dims.3, bf16[384,384]{1,0:T(8,128)(2,1)} %bitcast.5, bf16[8,384,384]{2,1,0:T(8,128)(2,1)} %bitcast.3), custom_call_target="tpu_custom_call" | custom-call | flops 25200001024 | bytes 12000000 | tf_op jit(solution)/shard_map/ladder/pallas_call | solution.py:764
  61.3 9.5 %rest.1 = f32[3072,384]{1,0:T(8,128)} custom-call(s32[8]{0:T(128)} %dims.3, bf16[1,4,192,384]{3,2,1,0:T(8,128)(2,1)} %get-tuple-element.8.own_hbm, bf16[1,4,192,384]{3,2,1,0:T(8,128)(2,1)} %get-tuple-element.9.par_hbm, bf16[8,384,384]{2,1,0:T(8,128)(2,1)} %bitcast.4, f32[3072,384]{1,0:T(8,128)} %get-tuple-element.10.raw), custom_call_target="tpu_custom_call" | custom-call | flops 3600000000 | bytes 16000000 | tf_op jit(solution)/shard_map/rest/pallas_call | solution.py:789

commit v5 on v3

--- a/solution.py
+++ b/solution.py
@@ -11,8 +11,8 @@
 PV = V // PIECES
 HALF = NI * V // 2
 CROSSF, OWN, PASS_Z, FWD_Y, PASS_Y, PAR = range(6)
-PARTS = {1: 2, 2: 1}
-SEQUENCE = (1, 1, 1, 1, 1, 2, 1, 2, 1, 2, 2, 2, 2, 2)
+PARTS = {1: 2, 2: 2}
+SEQUENCE = (1, 1, 1, 1, 1, 1, 2, 2, 1, 2, 2, 2, 2, 2)
 UNITS = (
     (
         ((0, 0, 0), (0, 0, 0), (0, 0, 0), (0, 0, 0), (0, 0, 0), (0, 0, 0), (0, 0, 0), (0, 0, 0), (0, 0, 0), (0, 0, 0), (0, 0, 0), (0, 0, 0), (0, 0, 0), (0, 0, 0), (0, 0, 0), (0, 0, 0)),
@@ -20,15 +20,15 @@
         ((0, 1, 1), (0, 1, 1), (0, 1, 1), (0, 1, 1), (0, 1, 1), (0, 1, 1), (0, 1, 1), (0, 1, 1), (0, 1, 1), (0, 1, 1), (0, 1, 1), (0, 1, 1), (0, 1, 1), (0, 1, 1), (0, 1, 1), (0, 1, 1)),
         ((1, 0, 0), (1, 0, 0), (1, 0, 0), (1, 0, 0), (0, 2, 0), (0, 2, 0), (1, 0, 0), (1, 0, 0), (1, 0, 0), (1, 0, 0), (1, 0, 0), (1, 0, 0), (1, 0, 0), (1, 0, 0), (1, 0, 0), (1, 0, 0)),
         ((0, 2, 0), (0, 2, 0), (0, 2, 0), (0, 2, 0), (1, 0, 0), (1, 0, 0), (0, 2, 0), (1, 0, 1), (0, 2, 0), (0, 2, 0), (0, 2, 0), (0, 2, 0), (0, 2, 0), (0, 2, 0), (0, 2, 0), (0, 2, 0)),
-        ((0, 0, 0), (0, 0, 0), (0, 0, 0), (0, 0, 0), (0, 0, 0), (0, 0, 0), (1, 0, 0), (1, 0, 0), (0, 0, 0), (0, 0, 0), (0, 0, 0), (0, 0, 0), (0, 0, 0), (0, 0, 0), (0, 0, 0), (0, 0, 0)),
         ((1, 1, 0), (1, 1, 0), (1, 1, 0), (1, 1, 0), (1, 3, 0), (1, 1, 0), (1, 1, 0), (1, 1, 0), (1, 3, 0), (1, 3, 0), (1, 1, 0), (1, 1, 0), (1, 1, 0), (1, 1, 0), (1, 1, 0), (1, 1, 0)),
-        ((1, 0, 0), (1, 0, 0), (1, 0, 0), (1, 0, 0), (0, 1, 0), (1, 0, 0), (0, 0, 0), (0, 0, 0), (1, 0, 0), (1, 0, 0), (1, 0, 0), (1, 0, 0), (1, 0, 0), (1, 0, 0), (1, 0, 0), (1, 0, 0)),
+        ((0, 0, 0), (0, 0, 0), (0, 0, 0), (0, 0, 0), (0, 0, 0), (0, 0, 0), (0, 0, 0), (0, 0, 0), (0, 0, 0), (0, 0, 0), (0, 0, 0), (0, 0, 0), (0, 0, 0), (0, 0, 0), (0, 0, 0), (0, 0, 0)),
+        ((1, 0, 0), (1, 0, 0), (1, 0, 0), (1, 0, 0), (0, 1, 0), (1, 0, 0), (1, 0, 0), (1, 0, 0), (1, 0, 0), (1, 0, 0), (1, 0, 0), (1, 0, 0), (1, 0, 0), (1, 0, 0), (1, 0, 0), (1, 0, 0)),
         ((1, 3, 0), (1, 3, 0), (1, 1, 1), (1, 1, 1), (1, 0, 1), (1, 1, 1), (1, 1, 1), (1, 1, 1), (1, 1, 0), (1, 1, 0), (1, 1, 1), (1, 1, 1), (1, 1, 1), (1, 1, 1), (1, 1, 1), (1, 1, 1)),
-        ((0, 1, 0), (0, 1, 0), (0, 1, 0), (0, 1, 0), (1, 0, 0), (0, 1, 0), (0, 1, 0), (0, 1, 0), (0, 1, 0), (0, 1, 0), (0, 1, 0), (0, 1, 0), (0, 1, 0), (0, 1, 0), (0, 1, 0), (0, 1, 0)),
-        ((1, 1, 0), (1, 1, 0), (0, 3, 0), (0, 3, 0), (1, 1, 0), (1, 1, 0), (1, 1, 0), (1, 1, 0), (1, 1, 0), (1, 1, 0), (1, 1, 0), (1, 1, 0), (1, 1, 0), (1, 1, 0), (1, 1, 0), (1, 1, 0)),
-        ((0, 3, 0), (0, 3, 0), (0, 2, 0), (0, 2, 0), (0, 3, 0), (0, 3, 0), (0, 3, 0), (0, 3, 0), (0, 3, 0), (0, 3, 0), (0, 3, 0), (0, 3, 0), (0, 3, 0), (0, 3, 0), (0, 3, 0), (0, 3, 0)),
-        ((1, 3, 0), (1, 3, 0), (1, 3, 0), (1, 1, 0), (1, 3, 0), (1, 3, 0), (1, 3, 0), (1, 3, 0), (1, 3, 0), (1, 3, 0), (1, 3, 0), (1, 3, 0), (1, 3, 0), (1, 3, 0), (1, 3, 0), (1, 3, 0)),
-        ((0, 2, 0), (0, 2, 0), (1, 1, 0), (1, 3, 0), (0, 2, 0), (0, 2, 0), (0, 2, 0), (0, 2, 0), (0, 2, 0), (0, 2, 0), (0, 2, 0), (0, 2, 0), (0, 2, 0), (0, 2, 0), (0, 2, 0), (0, 2, 0)),
+        ((0, 1, 0), (0, 1, 0), (0, 1, 0), (0, 1, 0), (1, 0, 0), (0, 1, 0), (0, 3, 0), (0, 3, 0), (0, 1, 0), (0, 1, 0), (0, 1, 0), (0, 1, 0), (0, 1, 0), (0, 1, 0), (0, 1, 0), (0, 1, 0)),
+        ((1, 1, 0), (1, 1, 0), (0, 3, 0), (0, 3, 0), (1, 1, 0), (1, 1, 0), (0, 1, 0), (0, 1, 0), (1, 1, 0), (1, 1, 0), (1, 1, 0), (1, 1, 0), (1, 1, 0), (1, 1, 0), (1, 1, 0), (1, 1, 0)),
+        ((0, 3, 0), (0, 3, 0), (0, 2, 0), (0, 2, 0), (0, 3, 0), (0, 3, 0), (1, 1, 0), (1, 1, 0), (0, 3, 0), (0, 3, 0), (0, 3, 0), (0, 3, 0), (0, 3, 0), (0, 3, 0), (0, 3, 0), (0, 3, 0)),
+        ((1, 3, 0), (1, 3, 0), (1, 1, 0), (1, 1, 0), (1, 3, 0), (1, 3, 0), (1, 3, 0), (1, 3, 0), (1, 3, 0), (1, 3, 0), (1, 3, 0), (1, 3, 0), (1, 3, 0), (1, 3, 0), (1, 3, 0), (1, 3, 0)),
+        ((0, 2, 0), (0, 2, 0), (1, 3, 0), (1, 3, 0), (0, 2, 0), (0, 2, 0), (0, 2, 0), (0, 2, 0), (0, 2, 0), (0, 2, 0), (0, 2, 0), (0, 2, 0), (0, 2, 0), (0, 2, 0), (0, 2, 0), (0, 2, 0)),
     ),
     (
         ((0, 0, 1), (0, 0, 1), (0, 0, 1), (0, 0, 1), (0, 0, 1), (0, 0, 1), (0, 0, 1), (0, 0, 1), (0, 0, 1), (0, 0, 1), (0, 0, 1), (0, 0, 1), (0, 0, 1), (0, 0, 1), (0, 0, 1), (0, 0, 1)),
@@ -36,15 +36,15 @@
         ((0, 3, 1), (0, 3, 1), (0, 3, 1), (0, 3, 1), (0, 3, 1), (0, 3, 1), (0, 3, 1), (0, 3, 1), (0, 3, 1), (0, 3, 1), (0, 3, 1), (0, 3, 1), (0, 3, 1), (0, 3, 1), (0, 3, 1), (0, 3, 1)),
         ((1, 0, 1), (1, 0, 1), (1, 0, 1), (1, 0, 1), (0, 2, 1), (0, 2, 1), (1, 0, 1), (0, 2, 0), (1, 0, 1), (1, 0, 1), (1, 0, 1), (1, 0, 1), (1, 0, 1), (1, 0, 1), (1, 0, 1), (1, 0, 1)),
         ((0, 2, 1), (0, 2, 1), (0, 2, 1), (0, 2, 1), (1, 1, 0), (1, 0, 1), (0, 2, 1), (0, 2, 1), (0, 2, 1), (0, 2, 1), (0, 2, 1), (0, 2, 1), (0, 2, 1), (0, 2, 1), (0, 2, 1), (0, 2, 1)),
-        ((0, 0, 0), (0, 0, 0), (0, 0, 0), (0, 0, 0), (0, 0, 0), (0, 0, 0), (1, 0, 0), (1, 0, 0), (0, 0, 0), (0, 0, 0), (0, 0, 0), (0, 0, 0), (0, 0, 0), (0, 0, 0), (0, 0, 0), (0, 0, 0)),
         ((1, 1, 1), (1, 1, 1), (1, 3, 0), (1, 3, 0), (1, 1, 1), (1, 3, 0), (1, 3, 0), (1, 3, 0), (1, 3, 1), (1, 3, 1), (1, 3, 0), (1, 3, 0), (1, 3, 0), (1, 3, 0), (1, 3, 0), (1, 3, 0)),
-        ((1, 0, 0), (1, 0, 0), (1, 0, 0), (1, 0, 0), (0, 1, 0), (1, 0, 0), (0, 0, 0), (0, 0, 0), (1, 0, 0), (1, 0, 0), (1, 0, 0), (1, 0, 0), (1, 0, 0), (1, 0, 0), (1, 0, 0), (1, 0, 0)),
+        ((0, 0, 0), (0, 0, 0), (0, 0, 0), (0, 0, 0), (0, 0, 0), (0, 0, 0), (0, 0, 0), (0, 0, 0), (0, 0, 0), (0, 0, 0), (0, 0, 0), (0, 0, 0), (0, 0, 0), (0, 0, 0), (0, 0, 0), (0, 0, 0)),
+        ((1, 0, 0), (1, 0, 0), (1, 0, 0), (1, 0, 0), (0, 1, 0), (1, 0, 0), (1, 0, 0), (1, 0, 0), (1, 0, 0), (1, 0, 0), (1, 0, 0), (1, 0, 0), (1, 0, 0), (1, 0, 0), (1, 0, 0), (1, 0, 0)),
         ((1, 3, 1), (1, 3, 1), (1, 3, 1), (1, 3, 1), (1, 3, 1), (1, 3, 1), (1, 3, 1), (1, 3, 1), (1, 1, 1), (1, 1, 1), (1, 3, 1), (1, 3, 1), (1, 3, 1), (1, 3, 1), (1, 3, 1), (1, 3, 1)),
-        ((0, 1, 0), (0, 1, 0), (0, 1, 0), (0, 1, 0), (1, 0, 0), (0, 1, 0), (0, 1, 0), (0, 1, 0), (0, 1, 0), (0, 1, 0), (0, 1, 0), (0, 1, 0), (0, 1, 0), (0, 1, 0), (0, 1, 0), (0, 1, 0)),
-        ((1, 1, 0), (1, 1, 0), (0, 3, 0), (0, 3, 0), (1, 1, 0), (1, 1, 0), (1, 1, 0), (1, 1, 0), (1, 1, 0), (1, 1, 0), (1, 1, 0), (1, 1, 0), (1, 1, 0), (1, 1, 0), (1, 1, 0), (1, 1, 0)),
-        ((0, 3, 0), (0, 3, 0), (0, 2, 0), (0, 2, 0), (0, 3, 0), (0, 3, 0), (0, 3, 0), (0, 3, 0), (0, 3, 0), (0, 3, 0), (0, 3, 0), (0, 3, 0), (0, 3, 0), (0, 3, 0), (0, 3, 0), (0, 3, 0)),
-        ((1, 3, 0), (1, 3, 0), (1, 3, 0), (1, 1, 0), (1, 3, 0), (1, 3, 0), (1, 3, 0), (1, 3, 0), (1, 3, 0), (1, 3, 0), (1, 3, 0), (1, 3, 0), (1, 3, 0), (1, 3, 0), (1, 3, 0), (1, 3, 0)),
-        ((0, 2, 0), (0, 2, 0), (1, 1, 0), (1, 3, 0), (0, 2, 0), (0, 2, 0), (0, 2, 0), (0, 2, 0), (0, 2, 0), (0, 2, 0), (0, 2, 0), (0, 2, 0), (0, 2, 0), (0, 2, 0), (0, 2, 0), (0, 2, 0)),
+        ((0, 1, 0), (0, 1, 0), (0, 1, 0), (0, 1, 0), (1, 0, 0), (0, 1, 0), (0, 3, 0), (0, 3, 0), (0, 1, 0), (0, 1, 0), (0, 1, 0), (0, 1, 0), (0, 1, 0), (0, 1, 0), (0, 1, 0), (0, 1, 0)),
+        ((1, 1, 0), (1, 1, 0), (0, 3, 0), (0, 3, 0), (1, 1, 0), (1, 1, 0), (0, 1, 0), (0, 1, 0), (1, 1, 0), (1, 1, 0), (1, 1, 0), (1, 1, 0), (1, 1, 0), (1, 1, 0), (1, 1, 0), (1, 1, 0)),
+        ((0, 3, 0), (0, 3, 0), (0, 2, 0), (0, 2, 0), (0, 3, 0), (0, 3, 0), (1, 1, 0), (1, 1, 0), (0, 3, 0), (0, 3, 0), (0, 3, 0), (0, 3, 0), (0, 3, 0), (0, 3, 0), (0, 3, 0), (0, 3, 0)),
+        ((1, 3, 0), (1, 3, 0), (1, 1, 0), (1, 1, 0), (1, 3, 0), (1, 3, 0), (1, 3, 0), (1, 3, 0), (1, 3, 0), (1, 3, 0), (1, 3, 0), (1, 3, 0), (1, 3, 0), (1, 3, 0), (1, 3, 0), (1, 3, 0)),
+        ((0, 2, 0), (0, 2, 0), (1, 3, 0), (1, 3, 0), (0, 2, 0), (0, 2, 0), (0, 2, 0), (0, 2, 0), (0, 2, 0), (0, 2, 0), (0, 2, 0), (0, 2, 0), (0, 2, 0), (0, 2, 0), (0, 2, 0), (0, 2, 0)),
     ),
 )
 EVENTS = (
@@ -56,14 +56,14 @@
         (6, ((OWN, 0, 2, 1), (FWD_Y, 0, 0), (FWD_Y, 0, 1),)),
         (8, ((OWN, 1, 1, 0), (PASS_Z, 1, 1), (PASS_Z, 3, 1),)),
         (9, ((PASS_Y, 0, 1),)),
-        (10, ((OWN, 1, 1, 1),)),
-        (11, ((OWN, 1, 3, 0), (FWD_Y, 1, 0), (FWD_Y, 3, 0),)),
+        (10, ((OWN, 1, 1, 1), (FWD_Y, 1, 0), (FWD_Y, 3, 0), (OWN, 1, 3, 0),)),
         (12, ((OWN, 1, 2, 1), (PASS_Z, 2, 0), (PASS_Z, 2, 1),)),
-        (13, ((OWN, 1, 2, 0),)),
-        (14, ((FWD_Y, 1, 1), (FWD_Y, 3, 1), (PASS_Y, 1, 0), (OWN, 1, 3, 1),)),
-        (15, ((FWD_Y, 2, 0), (FWD_Y, 2, 1),)),
+        (13, ((OWN, 1, 2, 0), (PASS_Y, 1, 0),)),
+        (14, ((FWD_Y, 1, 1), (FWD_Y, 3, 1),)),
+        (15, ((OWN, 1, 3, 1),)),
+        (16, ((FWD_Y, 2, 0), (FWD_Y, 2, 1),)),
         (17, ((PASS_Y, 3, 1),)),
-        (18, ((PASS_Y, 2, 0),)),
+        (19, ((PASS_Y, 2, 0),)),
     ),
     (
         (2, ((CROSSF, 0), (CROSSF, 1), (OWN, 0, 1, 0), (OWN, 0, 3, 0), (PASS_Z, 0, 0), (PASS_Z, 0, 1),)),
@@ -73,14 +73,14 @@
         (6, ((OWN, 0, 2, 1), (FWD_Y, 0, 0), (FWD_Y, 0, 1),)),
         (8, ((OWN, 1, 1, 0), (PASS_Z, 1, 1), (PASS_Z, 3, 1),)),
         (9, ((PASS_Y, 0, 0),)),
-        (10, ((OWN, 1, 1, 1),)),
-        (11, ((OWN, 1, 3, 0), (FWD_Y, 1, 0), (FWD_Y, 3, 0),)),
+        (10, ((OWN, 1, 1, 1), (FWD_Y, 1, 0), (FWD_Y, 3, 0), (OWN, 1, 3, 0),)),
         (12, ((OWN, 1, 2, 1), (PASS_Z, 2, 0), (PASS_Z, 2, 1),)),
-        (13, ((OWN, 1, 3, 1),)),
-        (14, ((OWN, 1, 2, 0), (FWD_Y, 1, 1), (FWD_Y, 3, 1), (PASS_Y, 3, 0),)),
+        (13, ((OWN, 1, 3, 1), (PASS_Y, 3, 0),)),
+        (14, ((FWD_Y, 1, 1), (FWD_Y, 3, 1),)),
+        (15, ((OWN, 1, 2, 0),)),
         (16, ((FWD_Y, 2, 0), (FWD_Y, 2, 1),)),
         (17, ((PASS_Y, 1, 1),)),
-        (18, ((PASS_Y, 2, 1),)),
+        (19, ((PASS_Y, 2, 1),)),
     ),
     (
         (2, ((CROSSF, 0), (CROSSF, 1), (OWN, 0, 1, 0), (OWN, 0, 3, 0), (PASS_Z, 0, 0), (PASS_Z, 0, 1),)),
@@ -92,15 +92,17 @@
         (9, ((PASS_Y, 0, 0),)),
         (10, ((OWN, 1, 1, 1),)),
         (11, ((OWN, 1, 3, 1), (PAR, 0, 1, 0), (PAR, 0, 3, 0),)),
-        (12, ((OWN, 1, 2, 0), (OWN, 1, 2, 1), (PASS_Z, 2, 0), (PASS_Z, 2, 1), (PAR, 1, 0, 0), (PAR, 1, 0, 1),)),
-        (13, ((PAR, 0, 3, 1), (PAR, 0, 1, 1),)),
+        (12, ((PAR, 1, 0, 0), (PAR, 1, 0, 1),)),
+        (13, ((OWN, 1, 2, 0), (OWN, 1, 2, 1), (PASS_Z, 2, 0), (PASS_Z, 2, 1),)),
         (14, ((PASS_Y, 3, 0),)),
-        (15, ((PAR, 0, 2, 0), (PAR, 0, 2, 1),)),
-        (17, ((PASS_Y, 1, 1), (PAR, 1, 1, 0),)),
-        (18, ((PAR, 1, 3, 0),)),
-        (19, ((PASS_Y, 2, 1), (PAR, 1, 3, 1),)),
-        (20, ((PAR, 1, 1, 1), (PAR, 1, 2, 0),)),
-        (21, ((PAR, 1, 2, 1),)),
+        (15, ((PAR, 0, 1, 1), (PAR, 0, 3, 1),)),
+        (17, ((PAR, 0, 2, 0), (PAR, 0, 2, 1), (PAR, 1, 1, 0), (PAR, 1, 3, 0),)),
+        (19, ((PASS_Y, 1, 1),)),
+        (21, ((PASS_Y, 2, 1),)),
+        (22, ((PAR, 1, 3, 1),)),
+        (23, ((PAR, 1, 1, 1),)),
+        (24, ((PAR, 1, 2, 0),)),
+        (26, ((PAR, 1, 2, 1),)),
     ),
     (
         (2, ((CROSSF, 0), (CROSSF, 1), (OWN, 0, 1, 0), (OWN, 0, 3, 0), (PASS_Z, 0, 0), (PASS_Z, 0, 1),)),
@@ -112,15 +114,17 @@
         (9, ((PASS_Y, 0, 1),)),
         (10, ((OWN, 1, 1, 1),)),
         (11, ((OWN, 1, 3, 1), (PAR, 0, 1, 0), (PAR, 0, 3, 0),)),
-        (12, ((OWN, 1, 2, 0), (OWN, 1, 2, 1), (PASS_Z, 2, 0), (PASS_Z, 2, 1), (PAR, 1, 0, 0), (PAR, 1, 0, 1),)),
-        (13, ((PAR, 0, 3, 1), (PAR, 0, 1, 1),)),
+        (12, ((PAR, 1, 0, 0), (PAR, 1, 0, 1),)),
+        (13, ((OWN, 1, 2, 0), (OWN, 1, 2, 1), (PASS_Z, 2, 0), (PASS_Z, 2, 1),)),
         (14, ((PASS_Y, 1, 0),)),
-        (15, ((PAR, 0, 2, 0), (PAR, 0, 2, 1),)),
-        (17, ((PASS_Y, 3, 1), (PAR, 1, 3, 0),)),
-        (18, ((PAR, 1, 1, 0),)),
-        (19, ((PASS_Y, 2, 0), (PAR, 1, 1, 1),)),
-        (20, ((PAR, 1, 3, 1), (PAR, 1, 2, 1),)),
-        (21, ((PAR, 1, 2, 0),)),
+        (15, ((PAR, 0, 1, 1), (PAR, 0, 3, 1),)),
+        (17, ((PAR, 0, 2, 0), (PAR, 0, 2, 1), (PAR, 1, 1, 0), (PAR, 1, 3, 0),)),
+        (19, ((PASS_Y, 3, 1),)),
+        (21, ((PASS_Y, 2, 0),)),
+        (22, ((PAR, 1, 1, 1),)),
+        (23, ((PAR, 1, 3, 1),)),
+        (24, ((PAR, 1, 2, 1),)),
+        (26, ((PAR, 1, 2, 0),)),
     ),
     (
         (2, ((CROSSF, 0), (OWN, 0, 1, 0), (OWN, 0, 3, 0), (PASS_Z, 0, 0), (PASS_Z, 0, 1), (PAR, 0, 0, 0),)),
@@ -132,13 +136,14 @@
         (8, ((OWN, 1, 3, 0), (PASS_Z, 1, 1), (PASS_Z, 3, 1),)),
         (9, ((OWN, 1, 1, 1), (PAR, 0, 3, 0), (PAR, 1, 1, 0),)),
         (10, ((OWN, 1, 3, 1), (FWD_Y, 1, 0), (FWD_Y, 3, 0),)),
-        (11, ((OWN, 1, 0, 1), (OWN, 1, 2, 0), (PASS_Z, 2, 0), (PASS_Z, 2, 1), (PAR, 1, 3, 0),)),
-        (12, ((OWN, 1, 2, 1), (PAR, 0, 1, 1), (PAR, 1, 1, 1),)),
-        (13, ((FWD_Y, 1, 1), (FWD_Y, 3, 1),)),
-        (14, ((FWD_Y, 2, 0), (PAR, 0, 3, 1), (PAR, 1, 3, 1),)),
-        (15, ((FWD_Y, 2, 1),)),
-        (16, ((PAR, 0, 2, 0), (PAR, 1, 2, 0),)),
-        (17, ((PAR, 0, 2, 1), (PAR, 1, 2, 1),)),
+        (11, ((OWN, 1, 0, 1), (PAR, 1, 3, 0),)),
+        (12, ((OWN, 1, 2, 0), (OWN, 1, 2, 1), (PASS_Z, 2, 0), (PASS_Z, 2, 1),)),
+        (13, ((PAR, 0, 1, 1), (PAR, 1, 1, 1),)),
+        (14, ((FWD_Y, 1, 1), (FWD_Y, 3, 1),)),
+        (15, ((PAR, 0, 3, 1), (PAR, 1, 3, 1),)),
+        (16, ((FWD_Y, 2, 0), (FWD_Y, 2, 1),)),
+        (17, ((PAR, 0, 2, 0), (PAR, 1, 2, 0),)),
+        (19, ((PAR, 0, 2, 1), (PAR, 1, 2, 1),)),
     ),
     (
         (2, ((CROSSF, 0), (OWN, 0, 1, 0), (OWN, 0, 3, 0), (PASS_Z, 0, 0), (PASS_Z, 0, 1), (PAR, 1, 0, 0),)),
@@ -150,12 +155,14 @@
         (8, ((OWN, 1, 3, 0), (PASS_Z, 1, 1), (PASS_Z, 3, 1),)),
         (9, ((OWN, 1, 1, 1), (PAR, 0, 1, 0), (PAR, 1, 1, 0),)),
         (10, ((OWN, 1, 3, 1), (FWD_Y, 1, 0), (FWD_Y, 3, 0),)),
-        (11, ((OWN, 1, 2, 0), (OWN, 1, 2, 1), (PASS_Z, 2, 0), (PASS_Z, 2, 1), (PAR, 0, 3, 0), (PAR, 1, 3, 0),)),
-        (12, ((PAR, 0, 1, 1), (PAR, 1, 1, 1),)),
-        (13, ((FWD_Y, 1, 1), (FWD_Y, 3, 1),)),
-        (14, ((FWD_Y, 2, 0), (FWD_Y, 2, 1), (PAR, 0, 3, 1), (PAR, 1, 3, 1),)),
-        (16, ((PAR, 0, 2, 0), (PAR, 1, 2, 0),)),
-        (17, ((PAR, 0, 2, 1), (PAR, 1, 2, 1),)),
+        (11, ((PAR, 0, 3, 0), (PAR, 1, 3, 0),)),
+        (12, ((OWN, 1, 2, 0), (OWN, 1, 2, 1), (PASS_Z, 2, 0), (PASS_Z, 2, 1),)),
+        (13, ((PAR, 0, 1, 1), (PAR, 1, 1, 1),)),
+        (14, ((FWD_Y, 1, 1), (FWD_Y, 3, 1),)),
+        (15, ((PAR, 0, 3, 1), (PAR, 1, 3, 1),)),
+        (16, ((FWD_Y, 2, 0), (FWD_Y, 2, 1),)),
+        (17, ((PAR, 0, 2, 0), (PAR, 1, 2, 0),)),
+        (19, ((PAR, 0, 2, 1), (PAR, 1, 2, 1),)),
     ),
     (
         (2, ((CROSSF, 0), (CROSSF, 1), (OWN, 0, 1, 0), (OWN, 0, 3, 0), (PASS_Z, 0, 0), (PASS_Z, 0, 1),)),
@@ -166,16 +173,21 @@
         (7, ((OWN, 1, 1, 0),)),
         (8, ((OWN, 1, 3, 0), (PASS_Z, 1, 1), (PASS_Z, 3, 1),)),
         (9, ((OWN, 1, 1, 1), (PAR, 0, 0, 0), (PAR, 1, 0, 0),)),
-        (10, ((OWN, 1, 3, 1), (FWD_Y, 1, 0), (FWD_Y, 3, 0), (PAR, 1, 0, 1), (PAR, 0, 0, 1),)),
-        (11, ((OWN, 1, 2, 0), (OWN, 1, 2, 1), (PASS_Z, 2, 0), (PASS_Z, 2, 1), (PAR, 0, 1, 0),)),
-        (12, ((FWD_Y, 1, 1), (FWD_Y, 3, 1), (PAR, 1, 1, 0),)),
-        (13, ((PAR, 0, 3, 0),)),
-        (14, ((FWD_Y, 2, 0), (FWD_Y, 2, 1), (PAR, 1, 3, 0),)),
-        (15, ((PAR, 0, 1, 1), (PAR, 1, 1, 1),)),
-        (17, ((PAR, 0, 3, 1), (PAR, 1, 3, 1),)),
-        (18, ((PAR, 0, 2, 0), (PAR, 1, 2, 0),)),
-        (19, ((PAR, 0, 2, 1),)),
-        (20, ((PAR, 1, 2, 1),)),
+        (10, ((OWN, 1, 3, 1), (FWD_Y, 1, 0), (FWD_Y, 3, 0),)),
+        (11, ((PAR, 0, 0, 1), (PAR, 1, 0, 1),)),
+        (12, ((OWN, 1, 2, 0), (PASS_Z, 2, 0), (PASS_Z, 2, 1),)),
+        (13, ((OWN, 1, 2, 1), (PAR, 0, 1, 0),)),
+        (14, ((FWD_Y, 3, 1), (PAR, 1, 1, 0),)),
+        (15, ((FWD_Y, 1, 1),)),
+        (16, ((PAR, 0, 3, 0), (PAR, 1, 3, 0),)),
+        (17, ((FWD_Y, 2, 0), (FWD_Y, 2, 1),)),
+        (18, ((PAR, 0, 3, 1), (PAR, 1, 1, 1),)),
+        (19, ((PAR, 0, 1, 1),)),
+        (20, ((PAR, 1, 3, 1),)),
+        (21, ((PAR, 0, 2, 0),)),
+        (22, ((PAR, 1, 2, 0),)),
+        (23, ((PAR, 0, 2, 1),)),
+        (24, ((PAR, 1, 2, 1),)),
     ),
     (
         (2, ((CROSSF, 0), (CROSSF, 1), (OWN, 0, 1, 0), (OWN, 0, 3, 0), (PASS_Z, 0, 0), (PASS_Z, 0, 1),)),
@@ -186,16 +198,21 @@
         (7, ((OWN, 1, 1, 0),)),
         (8, ((OWN, 1, 3, 0), (PASS_Z, 1, 1), (PASS_Z, 3, 1),)),
         (9, ((OWN, 1, 1, 1), (PAR, 0, 0, 0), (PAR, 1, 0, 0),)),
-        (10, ((OWN, 1, 3, 1), (FWD_Y, 1, 0), (FWD_Y, 3, 0), (PAR, 1, 0, 1), (PAR, 0, 0, 1),)),
-        (11, ((OWN, 1, 2, 0), (OWN, 1, 2, 1), (PASS_Z, 2, 0), (PASS_Z, 2, 1), (PAR, 0, 1, 0),)),
-        (12, ((FWD_Y, 1, 1), (FWD_Y, 3, 1), (PAR, 1, 1, 0),)),
-        (13, ((PAR, 0, 3, 0),)),
-        (14, ((FWD_Y, 2, 0), (FWD_Y, 2, 1), (PAR, 1, 3, 0),)),
-        (15, ((PAR, 0, 1, 1), (PAR, 1, 1, 1),)),
-        (17, ((PAR, 0, 3, 1), (PAR, 1, 3, 1),)),
-        (18, ((PAR, 0, 2, 0), (PAR, 1, 2, 0),)),
-        (19, ((PAR, 0, 2, 1),)),
-        (20, ((PAR, 1, 2, 1),)),
+        (10, ((OWN, 1, 3, 1), (FWD_Y, 1, 0), (FWD_Y, 3, 0),)),
+        (11, ((PAR, 0, 0, 1), (PAR, 1, 0, 1),)),
+        (12, ((OWN, 1, 2, 0), (PASS_Z, 2, 0), (PASS_Z, 2, 1),)),
+        (13, ((OWN, 1, 2, 1), (PAR, 0, 1, 0),)),
+        (14, ((FWD_Y, 3, 1), (PAR, 1, 1, 0),)),
+        (15, ((FWD_Y, 1, 1),)),
+        (16, ((PAR, 0, 3, 0), (PAR, 1, 3, 0),)),
+        (17, ((FWD_Y, 2, 0), (FWD_Y, 2, 1),)),
+        (18, ((PAR, 0, 3, 1), (PAR, 1, 1, 1),)),
+        (19, ((PAR, 0, 1, 1),)),
+        (20, ((PAR, 1, 3, 1),)),
+        (21, ((PAR, 0, 2, 0),)),
+        (22, ((PAR, 1, 2, 0),)),
+        (23, ((PAR, 0, 2, 1),)),
+        (24, ((PAR, 1, 2, 1),)),
     ),
     (
         (2, ((CROSSF, 0), (CROSSF, 1), (OWN, 0, 1, 0), (OWN, 0, 3, 0), (FWD_Y, 0, 0), (PAR, 0, 0, 0),)),
@@ -206,16 +223,18 @@
         (7, ((FWD_Y, 3, 0), (PAR, 0, 3, 0),)),
         (8, ((OWN, 1, 3, 0), (PASS_Y, 1, 0),)),
         (9, ((FWD_Y, 1, 1), (PAR, 0, 1, 1), (PAR, 1, 0, 0),)),
-        (10, ((OWN, 1, 3, 1), (PAR, 1, 0, 1),)),
-        (11, ((OWN, 1, 1, 0), (FWD_Y, 3, 1), (PASS_Y, 3, 0), (PAR, 0, 3, 1),)),
+        (10, ((OWN, 1, 3, 1), (PAR, 1, 0, 1), (OWN, 1, 1, 0),)),
+        (11, ((FWD_Y, 3, 1), (PASS_Y, 3, 0), (PAR, 0, 3, 1),)),
         (12, ((OWN, 1, 2, 0), (OWN, 1, 2, 1), (PAR, 1, 1, 0),)),
         (13, ((FWD_Y, 2, 0), (PASS_Y, 1, 1), (PAR, 0, 2, 0),)),
-        (14, ((OWN, 1, 1, 1), (FWD_Y, 2, 1), (PASS_Y, 3, 1), (PAR, 0, 2, 1), (PAR, 1, 3, 0),)),
-        (15, ((PASS_Y, 2, 0),)),
-        (16, ((PAR, 1, 1, 1),)),
-        (17, ((PASS_Y, 2, 1), (PAR, 1, 3, 1),)),
-        (18, ((PAR, 1, 2, 0),)),
-        (20, ((PAR, 1, 2, 1),)),
+        (14, ((OWN, 1, 1, 1), (PASS_Y, 3, 1),)),
+        (15, ((FWD_Y, 2, 1), (PAR, 0, 2, 1), (PAR, 1, 3, 0),)),
+        (16, ((PASS_Y, 2, 0),)),
+        (17, ((PAR, 1, 1, 1),)),
+        (18, ((PAR, 1, 3, 1),)),
+        (19, ((PASS_Y, 2, 1),)),
+        (21, ((PAR, 1, 2, 0),)),
+        (23, ((PAR, 1, 2, 1),)),
     ),
     (
         (2, ((CROSSF, 0), (CROSSF, 1), (OWN, 0, 1, 0), (OWN, 0, 3, 0), (FWD_Y, 0, 0), (PAR, 0, 0, 0),)),
@@ -226,16 +245,16 @@
         (7, ((FWD_Y, 3, 0), (PAR, 0, 3, 0),)),
         (8, ((OWN, 1, 3, 0), (PASS_Y, 1, 0),)),
         (9, ((FWD_Y, 1, 1), (PAR, 0, 1, 1), (PAR, 1, 0, 0),)),
-        (10, ((OWN, 1, 3, 1), (PAR, 1, 0, 1),)),
-        (11, ((OWN, 1, 1, 0), (FWD_Y, 3, 1), (PASS_Y, 3, 0), (PAR, 0, 3, 1),)),
+        (10, ((OWN, 1, 3, 1), (PAR, 1, 0, 1), (OWN, 1, 1, 0),)),
+        (11, ((FWD_Y, 3, 1), (PASS_Y, 3, 0), (PAR, 0, 3, 1),)),
         (12, ((OWN, 1, 1, 1), (OWN, 1, 2, 0), (PAR, 1, 1, 0),)),
         (13, ((FWD_Y, 2, 0), (PASS_Y, 1, 1), (PAR, 0, 2, 0),)),
-        (14, ((OWN, 1, 2, 1), (FWD_Y, 2, 1), (PASS_Y, 3, 1), (PAR, 0, 2, 1), (PAR, 1, 3, 0),)),
-        (16, ((PASS_Y, 2, 0), (PAR, 1, 1, 1),)),
-        (17, ((PAR, 1, 3, 1),)),
-        (18, ((PASS_Y, 2, 1),)),
-        (19, ((PAR, 1, 2, 0),)),
-        (20, ((PAR, 1, 2, 1),)),
+        (14, ((OWN, 1, 2, 1), (PASS_Y, 3, 1),)),
+        (15, ((FWD_Y, 2, 1), (PAR, 0, 2, 1), (PAR, 1, 3, 0),)),
+        (17, ((PASS_Y, 2, 0), (PAR, 1, 1, 1),)),
+        (19, ((PASS_Y, 2, 1), (PAR, 1, 3, 1),)),
+        (21, ((PAR, 1, 2, 0),)),
+        (22, ((PAR, 1, 2, 1),)),
     ),
     (
         (2, ((CROSSF, 0), (CROSSF, 1), (OWN, 0, 1, 0), (OWN, 0, 3, 0), (FWD_Y, 0, 0), (PAR, 0, 0, 0),)),
@@ -247,15 +266,17 @@
         (8, ((OWN, 1, 3, 0), (PASS_Y, 1, 0),)),
         (9, ((OWN, 1, 1, 1), (FWD_Y, 1, 1), (PAR, 0, 1, 1), (PAR, 1, 0, 0),)),
         (10, ((OWN, 1, 3, 1), (PAR, 1, 0, 1),)),
-        (11, ((OWN, 1, 2, 1), (FWD_Y, 3, 1), (PASS_Y, 3, 0), (PAR, 0, 3, 1),)),
-        (12, ((OWN, 1, 2, 0), (PAR, 1, 1, 0),)),
-        (13, ((FWD_Y, 2, 0), (PASS_Y, 1, 1), (PAR, 0, 2, 0),)),
-        (14, ((FWD_Y, 2, 1), (PASS_Y, 3, 1), (PAR, 0, 2, 1), (PAR, 1, 3, 0),)),
-        (16, ((PASS_Y, 2, 0), (PAR, 1, 1, 1),)),
-        (17, ((PAR, 1, 3, 1),)),
-        (18, ((PASS_Y, 2, 1),)),
-        (19, ((PAR, 1, 2, 0),)),
-        (20, ((PAR, 1, 2, 1),)),
+        (11, ((FWD_Y, 3, 1), (PASS_Y, 3, 0),)),
+        (12, ((OWN, 1, 2, 0), (OWN, 1, 2, 1), (PAR, 0, 3, 1), (PAR, 1, 1, 0),)),
+        (13, ((PASS_Y, 1, 1),)),
+        (14, ((FWD_Y, 2, 0), (PASS_Y, 3, 1), (PAR, 0, 2, 0),)),
+        (16, ((FWD_Y, 2, 1), (PAR, 0, 2, 1), (PAR, 1, 3, 0),)),
+        (17, ((PASS_Y, 2, 0),)),
+        (18, ((PAR, 1, 1, 1),)),
+        (19, ((PAR, 1, 3, 1),)),
+        (20, ((PASS_Y, 2, 1),)),
+        (22, ((PAR, 1, 2, 0),)),
+        (23, ((PAR, 1, 2, 1),)),
     ),
     (
         (2, ((CROSSF, 0), (CROSSF, 1), (OWN, 0, 1, 0), (OWN, 0, 3, 0), (FWD_Y, 0, 0), (PAR, 0, 0, 0),)),
@@ -267,15 +288,18 @@
         (8, ((OWN, 1, 3, 0), (PASS_Y, 1, 0),)),
         (9, ((OWN, 1, 1, 1), (FWD_Y, 1, 1), (PAR, 0, 1, 1), (PAR, 1, 0, 0),)),
         (10, ((OWN, 1, 3, 1), (PAR, 1, 0, 1),)),
-        (11, ((OWN, 1, 2, 1), (FWD_Y, 3, 1), (PASS_Y, 3, 0), (PAR, 0, 3, 1),)),
-        (12, ((OWN, 1, 2, 0), (PAR, 1, 1, 0),)),
-        (13, ((FWD_Y, 2, 0), (PASS_Y, 1, 1), (PAR, 0, 2, 0),)),
-        (14, ((FWD_Y, 2, 1), (PASS_Y, 3, 1), (PAR, 0, 2, 1), (PAR, 1, 3, 0),)),
-        (16, ((PASS_Y, 2, 0), (PAR, 1, 1, 1),)),
-        (17, ((PAR, 1, 3, 1),)),
-        (18, ((PASS_Y, 2, 1),)),
-        (19, ((PAR, 1, 2, 0),)),
-        (20, ((PAR, 1, 2, 1),)),
+        (11, ((FWD_Y, 3, 1), (PASS_Y, 3, 0),)),
+        (12, ((OWN, 1, 2, 0), (OWN, 1, 2, 1), (PAR, 0, 3, 1), (PAR, 1, 1, 0),)),
+        (13, ((PASS_Y, 1, 1),)),
+        (14, ((FWD_Y, 2, 0), (PAR, 0, 2, 0),)),
+        (15, ((PASS_Y, 3, 1),)),
+        (16, ((FWD_Y, 2, 1), (PAR, 0, 2, 1), (PAR, 1, 3, 0),)),
+        (17, ((PASS_Y, 2, 0),)),
+        (18, ((PAR, 1, 1, 1),)),
+        (19, ((PAR, 1, 3, 1),)),
+        (20, ((PASS_Y, 2, 1),)),
+        (21, ((PAR, 1, 2, 0),)),
+        (23, ((PAR, 1, 2, 1),)),
     ),
     (
         (2, ((CROSSF, 0), (CROSSF, 1), (OWN, 0, 1, 0), (OWN, 0, 3, 0), (FWD_Y, 0, 0),)),
@@ -289,11 +313,12 @@
         (10, ((OWN, 1, 3, 1), (PAR, 0, 1, 0), (PAR, 1, 1, 0),)),
         (11, ((FWD_Y, 3, 1),)),
         (12, ((PAR, 0, 3, 0), (PAR, 1, 3, 0),)),
-        (13, ((FWD_Y, 2, 0),)),
-        (14, ((OWN, 1, 2, 0), (FWD_Y, 2, 1), (PAR, 0, 1, 1), (PAR, 1, 1, 1),)),
-        (15, ((PAR, 0, 3, 1), (PAR, 1, 3, 1),)),
-        (17, ((OWN, 1, 2, 1), (PAR, 0, 2, 0), (PAR, 1, 2, 0),)),
-        (18, ((PAR, 0, 2, 1), (PAR, 1, 2, 1),)),
+        (14, ((OWN, 1, 2, 0), (FWD_Y, 2, 0), (PAR, 0, 1, 1), (PAR, 1, 1, 1),)),
+        (16, ((FWD_Y, 2, 1),)),
+        (17, ((PAR, 0, 3, 1), (PAR, 1, 3, 1),)),
+        (18, ((OWN, 1, 2, 1),)),
+        (19, ((PAR, 0, 2, 0), (PAR, 1, 2, 0),)),
+        (21, ((PAR, 0, 2, 1), (PAR, 1, 2, 1),)),
     ),
     (
         (2, ((CROSSF, 0), (CROSSF, 1), (OWN, 0, 1, 0), (OWN, 0, 3, 0), (FWD_Y, 0, 0),)),
@@ -307,11 +332,11 @@
         (10, ((OWN, 1, 3, 1), (PAR, 0, 1, 0), (PAR, 1, 1, 0),)),
         (11, ((FWD_Y, 3, 1),)),
         (12, ((PAR, 0, 3, 0), (PAR, 1, 3, 0),)),
-        (13, ((FWD_Y, 2, 0),)),
-        (14, ((OWN, 1, 2, 0), (FWD_Y, 2, 1), (PAR, 0, 1, 1), (PAR, 1, 1, 1),)),
-        (15, ((OWN, 1, 2, 1), (PAR, 0, 3, 1), (PAR, 1, 3, 1),)),
-        (17, ((PAR, 0, 2, 0), (PAR, 1, 2, 0),)),
-        (18, ((PAR, 0, 2, 1), (PAR, 1, 2, 1),)),
+        (14, ((OWN, 1, 2, 0), (FWD_Y, 2, 0), (PAR, 0, 1, 1), (PAR, 1, 1, 1),)),
+        (16, ((OWN, 1, 2, 1), (FWD_Y, 2, 1),)),
+        (17, ((PAR, 0, 3, 1), (PAR, 1, 3, 1),)),
+        (19, ((PAR, 0, 2, 0), (PAR, 1, 2, 0),)),
+        (21, ((PAR, 0, 2, 1), (PAR, 1, 2, 1),)),
     ),
     (
         (2, ((CROSSF, 0), (CROSSF, 1), (OWN, 0, 1, 0), (OWN, 0, 3, 0), (FWD_Y, 0, 0),)),
@@ -323,13 +348,13 @@
         (8, ((OWN, 1, 3, 0), (PAR, 0, 0, 1), (PAR, 1, 0, 1),)),
         (9, ((OWN, 1, 1, 1), (FWD_Y, 1, 1),)),
         (10, ((OWN, 1, 3, 1), (PAR, 0, 1, 0), (PAR, 1, 1, 0),)),
-        (11, ((OWN, 1, 2, 1), (FWD_Y, 3, 1),)),
-        (12, ((OWN, 1, 2, 0), (PAR, 0, 3, 0), (PAR, 1, 3, 0),)),
-        (13, ((FWD_Y, 2, 0),)),
-        (14, ((FWD_Y, 2, 1), (PAR, 0, 1, 1), (PAR, 1, 1, 1),)),
-        (15, ((PAR, 0, 3, 1), (PAR, 1, 3, 1),)),
-        (17, ((PAR, 0, 2, 0), (PAR, 1, 2, 0),)),
-        (18, ((PAR, 0, 2, 1), (PAR, 1, 2, 1),)),
+        (11, ((FWD_Y, 3, 1),)),
+        (12, ((OWN, 1, 2, 0), (OWN, 1, 2, 1), (PAR, 0, 3, 0), (PAR, 1, 3, 0),)),
+        (14, ((FWD_Y, 2, 0), (PAR, 0, 1, 1), (PAR, 1, 1, 1),)),
+        (16, ((FWD_Y, 2, 1),)),
+        (17, ((PAR, 0, 3, 1), (PAR, 1, 3, 1),)),
+        (19, ((PAR, 0, 2, 0), (PAR, 1, 2, 0),)),
+        (21, ((PAR, 0, 2, 1), (PAR, 1, 2, 1),)),
     ),
     (
         (2, ((CROSSF, 0), (CROSSF, 1), (OWN, 0, 1, 0), (OWN, 0, 3, 0), (FWD_Y, 0, 0),)),
@@ -341,13 +366,13 @@
         (8, ((OWN, 1, 3, 0), (PAR, 0, 0, 1), (PAR, 1, 0, 1),)),
         (9, ((OWN, 1, 1, 1), (FWD_Y, 1, 1),)),
         (10, ((OWN, 1, 3, 1), (PAR, 0, 1, 0), (PAR, 1, 1, 0),)),
-        (11, ((OWN, 1, 2, 1), (FWD_Y, 3, 1),)),
-        (12, ((OWN, 1, 2, 0), (PAR, 0, 3, 0), (PAR, 1, 3, 0),)),
-        (13, ((FWD_Y, 2, 0),)),
-        (14, ((FWD_Y, 2, 1), (PAR, 0, 1, 1), (PAR, 1, 1, 1),)),
-        (15, ((PAR, 0, 3, 1), (PAR, 1, 3, 1),)),
-        (17, ((PAR, 0, 2, 0), (PAR, 1, 2, 0),)),
-        (18, ((PAR, 0, 2, 1), (PAR, 1, 2, 1),)),
+        (11, ((FWD_Y, 3, 1),)),
+        (12, ((OWN, 1, 2, 0), (OWN, 1, 2, 1), (PAR, 0, 3, 0), (PAR, 1, 3, 0),)),
+        (14, ((FWD_Y, 2, 0), (PAR, 0, 1, 1), (PAR, 1, 1, 1),)),
+        (16, ((FWD_Y, 2, 1),)),
+        (17, ((PAR, 0, 3, 1), (PAR, 1, 3, 1),)),
+        (19, ((PAR, 0, 2, 0), (PAR, 1, 2, 0),)),
+        (21, ((PAR, 0, 2, 1), (PAR, 1, 2, 1),)),
     ),
 )
 
@@ -717,19 +742,20 @@
         pltpu.make_async_copy(raw.at[pl.ds(h * HALF, HALF)], acc.at[pl.ds(h * HALF, HALF)], sems.at[2 + NI + h])
         for h in range(2)
     ]
-    for copy in get_amps[:hi] + [get_own, get_par, get_raw[0]] + get_amps[hi:] + [get_raw[1]]:
+    for copy in [get_own] + get_amps[:hi] + [get_par, get_raw[0]] + get_amps[hi:] + [get_raw[1]]:
         copy.start()
     n_row, n_col = dims[tile], dims[jnp.bitwise_xor(tile, sym)]
     live = (lax.broadcasted_iota(jnp.int32, (V, V), 0) < n_row) & (lax.broadcasted_iota(jnp.int32, (V, V), 1) < n_col)
     live_b = jnp.where(live, 1.0, 0.0).astype(jnp.bfloat16)
-    puts = []
+    puts, masked = [], 0
     for h in range(2):
-        for i in range(h * hi, (h + 1) * hi):
-            get_amps[i].wait()
-            rc[:, i * V:(i + 1) * V] = rc[:, i * V:(i + 1) * V] * live_b
         if h == 0:
             get_own.wait()
         for t in range(6 * h, 6 * (h + 1)):
+            while masked <= columns(t)[-1][2]:
+                get_amps[masked].wait()
+                rc[:, masked * V:(masked + 1) * V] = rc[:, masked * V:(masked + 1) * V] * live_b
+                masked += 1
             left = own[...].reshape(n * 2 * V, V)
             r = jnp.dot(left, rc[:, t * 256:(t + 1) * 256], preferred_element_type=jnp.float32).astype(jnp.bfloat16)
             for lo_col, hi_col, pair, at in columns(t):

time: 71.8 us -> 74.5 us (1.038)
  Pallas kernels: 70.7 us -> 73.8 us
    pallas_call x1, Pallas kernels: 61.2 us -> 62.8 us  [shards(): pl.pallas_call(kernel, out_shape=[jax.ShapeDtypeStruct((NI * V, V), jnp.f...]
    pallas_call x1, Pallas kernels: 9.46 us -> 11 us  [shards(): pl.pallas_call(rest_kernel, out_shape=jax.ShapeDtypeStruct((NI * V, V), j...]
where the time goes in v5:
time: 74.5 us; the launch traced here: 74 us
  Pallas kernels  73.8 us (99%)
    pallas_call x1, Pallas kernels, shards(): pl.pallas_call(kernel, out_shape=[jax.ShapeDtypeStruct((NI * V, V), jnp.f...  62.8 us
    pallas_call x1, Pallas kernels, shards(): pl.pallas_call(rest_kernel, out_shape=jax.ShapeDtypeStruct((NI * V, V), j...  11 us

profile of v5, /device:TPU:3, one launch (start us, length us, event | category | flops | bytes accessed | tf_op | source)
XLA Modules:
  0.0 74.0 jit_solution(11154647672642230814)
XLA Ops:
  0.0 62.8 %ladder.1 = (f32[3072,384]{1,0:T(8,128)}, bf16[1,4,192,384]{3,2,1,0:T(8,128)(2,1)}, bf16[1,4,192,384]{3,2,1,0:T(8,128)(2,1)}) custom-call(s32[8]{0:T(128)} %dims.3, bf16[384,384]{1,0:T(8,128)(2,1)} %bitcast.5, bf16[8,384,384]{2,1,0:T(8,128)(2,1)} %bitcast.3), custom_call_target="tpu_custom_call" | custom-call | flops 25200001024 | bytes 12000000 | tf_op jit(solution)/shard_map/ladder/pallas_call | solution.py:789
  62.8 11.0 %rest.1 = f32[3072,384]{1,0:T(8,128)} custom-call(s32[8]{0:T(128)} %dims.3, bf16[1,4,192,384]{3,2,1,0:T(8,128)(2,1)} %get-tuple-element.8.own_hbm, bf16[1,4,192,384]{3,2,1,0:T(8,128)(2,1)} %get-tuple-element.9.par_hbm, bf16[8,384,384]{2,1,0:T(8,128)(2,1)} %bitcast.4, f32[3072,384]{1,0:T(8,128)} %get-tuple-element.10.raw), custom_call_target="tpu_custom_call" | custom-call | flops 3600000000 | bytes 16000000 | tf_op jit(solution)/shard_map/rest/pallas_call | solution.py:814

commit v6 on v3

--- a/solution.py
+++ b/solution.py
@@ -717,19 +717,20 @@
         pltpu.make_async_copy(raw.at[pl.ds(h * HALF, HALF)], acc.at[pl.ds(h * HALF, HALF)], sems.at[2 + NI + h])
         for h in range(2)
     ]
-    for copy in get_amps[:hi] + [get_own, get_par, get_raw[0]] + get_amps[hi:] + [get_raw[1]]:
+    for copy in [get_own] + get_amps[:hi] + [get_par, get_raw[0]] + get_amps[hi:] + [get_raw[1]]:
         copy.start()
     n_row, n_col = dims[tile], dims[jnp.bitwise_xor(tile, sym)]
     live = (lax.broadcasted_iota(jnp.int32, (V, V), 0) < n_row) & (lax.broadcasted_iota(jnp.int32, (V, V), 1) < n_col)
     live_b = jnp.where(live, 1.0, 0.0).astype(jnp.bfloat16)
-    puts = []
+    puts, masked = [], 0
     for h in range(2):
-        for i in range(h * hi, (h + 1) * hi):
-            get_amps[i].wait()
-            rc[:, i * V:(i + 1) * V] = rc[:, i * V:(i + 1) * V] * live_b
         if h == 0:
             get_own.wait()
         for t in range(6 * h, 6 * (h + 1)):
+            while masked <= columns(t)[-1][2]:
+                get_amps[masked].wait()
+                rc[:, masked * V:(masked + 1) * V] = rc[:, masked * V:(masked + 1) * V] * live_b
+                masked += 1
             left = own[...].reshape(n * 2 * V, V)
             r = jnp.dot(left, rc[:, t * 256:(t + 1) * 256], preferred_element_type=jnp.float32).astype(jnp.bfloat16)
             for lo_col, hi_col, pair, at in columns(t):

time: 71.8 us -> 73.3 us (1.021)
  Pallas kernels: 70.7 us -> 72.2 us
    pallas_call x1, Pallas kernels: 9.46 us -> 11 us  [shards(): pl.pallas_call(rest_kernel, out_shape=jax.ShapeDtypeStruct((NI * V, V), j...]
where the time goes in v6:
time: 73.3 us; the launch traced here: 72.4 us
  Pallas kernels  72.2 us (98%)
    pallas_call x1, Pallas kernels, shards(): pl.pallas_call(kernel, out_shape=[jax.ShapeDtypeStruct((NI * V, V), jnp.f...  61.2 us
    pallas_call x1, Pallas kernels, shards(): pl.pallas_call(rest_kernel, out_shape=jax.ShapeDtypeStruct((NI * V, V), j...  11 us

profile of v6, /device:TPU:3, one launch (start us, length us, event | category | flops | bytes accessed | tf_op | source)
XLA Modules:
  0.0 72.4 jit_solution(14564408116818428993)
XLA Ops:
  0.0 61.2 %ladder.1 = (f32[3072,384]{1,0:T(8,128)}, bf16[1,4,192,384]{3,2,1,0:T(8,128)(2,1)}, bf16[1,4,192,384]{3,2,1,0:T(8,128)(2,1)}) custom-call(s32[8]{0:T(128)} %dims.3, bf16[384,384]{1,0:T(8,128)(2,1)} %bitcast.5, bf16[8,384,384]{2,1,0:T(8,128)(2,1)} %bitcast.3), custom_call_target="tpu_custom_call" | custom-call | flops 25200001024 | bytes 12000000 | tf_op jit(solution)/shard_map/ladder/pallas_call | solution.py:764
  61.2 11.0 %rest.1 = f32[3072,384]{1,0:T(8,128)} custom-call(s32[8]{0:T(128)} %dims.3, bf16[1,4,192,384]{3,2,1,0:T(8,128)(2,1)} %get-tuple-element.8.own_hbm, bf16[1,4,192,384]{3,2,1,0:T(8,128)(2,1)} %get-tuple-element.9.par_hbm, bf16[8,384,384]{2,1,0:T(8,128)(2,1)} %bitcast.4, f32[3072,384]{1,0:T(8,128)} %get-tuple-element.10.raw), custom_call_target="tpu_custom_call" | custom-call | flops 3600000000 | bytes 16000000 | tf_op jit(solution)/shard_map/rest/pallas_call | solution.py:789
